TPU v7x, 128 devices: a whole 4x4x4 slice. The times are simulated.
128 devices in a mesh: row: 8 (over x_hi, z), col: 16 (over y, x_lo, core).
Axes of the slice: x: 4 (x_hi: 2, x_lo: 2; x = x_hi * 2 + x_lo), y: 4, z: 4, core: 2. Of those that a mesh axis runs over, the one named last changes fastest.
Arguments:
- features: bfloat16 [65536, 512], P(('row', 'col')), may hold values from -6 to 6
- weight: bfloat16 [512, 512], replicated, may hold values from -0.25 to 0.25
- bias: float32 [512], replicated, may hold values from -3 to 3
- cotangent: bfloat16 [65536, 512], P(('row', 'col')), may hold values from -6 to 6
- tile_values: bfloat16 [49152, 128, 128], P(('row', 'col')), may hold values from -0.09375 to 0.09375
- tile_row: int32 [128, 384], P(('row', 'col')), may hold values from 0 to 63
- tile_col: int32 [128, 384], P(('row', 'col')), may hold values from 0 to 31
- tile_count: int32 [128], P(('row', 'col')), may hold values from 48 to 384, as said below
Outputs:
- output: bfloat16 [65536, 512], P(('row', 'col'))
- grad_features: bfloat16 [65536, 512], P(('row', 'col'))
- grad_weight: float32 [512, 512], replicated
- grad_bias: float32 [512], replicated
Inputs may be any that keep to these rules, and one draw needn't show every extreme that they name: Each device uses slots 0 to tile_count - 1 of its lists; some device uses all 384 slots. `tile_row`: A tile position may be listed more than once; such tiles add.
All inputs are finite; a program needn't handle non-finite values.
Results may differ from a plain program's by a relative error of at most 0.024.
Values may be sent and summed in bfloat16 or wider, within the bound.
No kernel may reach another device: no remote copies, remote signals or barrier semaphores. Data moves between devices by JAX's collectives and lax.ppermute only.
A program may use at most 192 MiB of HBM per device.

v0:
```python
import math

import jax
import jax.numpy as jnp
from jax import lax
from jax.sharding import PartitionSpec as P


def tile_product(values, block_rows, block_columns, in_use, source, out_rows, transpose):
    width = source.shape[1]
    tile = values.shape[1]
    blocks = source.reshape(-1, tile, width)
    group_size = math.gcd(values.shape[0], 32)

    def advance(totals, position):
        start = position * group_size
        tile_group = lax.dynamic_slice_in_dim(values, start, group_size, 0)
        row_group = lax.dynamic_slice_in_dim(block_rows, start, group_size, 0)
        column_group = lax.dynamic_slice_in_dim(block_columns, start, group_size, 0)
        used_group = lax.dynamic_slice_in_dim(in_use, start, group_size, 0)
        if transpose:
            picked = blocks[row_group]
            target = column_group
            form = "tji,tjf->tif"
        else:
            picked = blocks[column_group]
            target = row_group
            form = "tij,tjf->tif"
        product = jnp.einsum(form, tile_group, picked, preferred_element_type=jnp.float32)
        product = product * used_group[:, None, None]
        return (totals.at[target].add(product), None)

    initial = jnp.zeros((out_rows // tile, tile, width), jnp.float32)
    totals, unused = lax.scan(
        advance, initial, jnp.arange(values.shape[0] // group_size, dtype=jnp.int32)
    )
    return totals.reshape(out_rows, width)


def body(features, weight, bias, cotangent, tile_values, tile_row, tile_col, tile_count):
    node_rows = features.shape[0]
    block_rows = tile_row[0]
    block_columns = tile_col[0]
    in_use = (jnp.arange(block_rows.shape[0], dtype=jnp.int32) < tile_count[0]).astype(jnp.float32)
    hidden_own = jnp.dot(features, weight, preferred_element_type=jnp.float32).astype(jnp.bfloat16)
    hidden = lax.all_gather(hidden_own, "row", axis=0, tiled=True)
    group_rows = node_rows * lax.axis_size("col")
    partial_value = tile_product(
        tile_values, block_rows, block_columns, in_use, hidden, group_rows, False
    )
    own_sum = lax.psum_scatter(
        partial_value.astype(jnp.bfloat16), "col", scatter_dimension=0, tiled=True
    ).astype(jnp.float32)
    summed_input = own_sum + bias[None, :]
    sigma = jax.nn.sigmoid(summed_input)
    output = (summed_input * sigma).astype(jnp.bfloat16)
    grad_own = (
        cotangent.astype(jnp.float32) * sigma * (1.0 + summed_input * (1.0 - sigma))
    ).astype(jnp.bfloat16)
    grad_rows = lax.all_gather(grad_own, "col", axis=0, tiled=True)
    bias_term = jnp.sum(grad_own.astype(jnp.float32), axis=0)
    back_part = tile_product(
        tile_values, block_rows, block_columns, in_use, grad_rows, hidden.shape[0], True
    )
    back_own = lax.psum_scatter(
        back_part.astype(jnp.bfloat16), "row", scatter_dimension=0, tiled=True
    ).astype(jnp.float32)
    grad_features = lax.dot_general(
        back_own.astype(jnp.bfloat16),
        weight,
        (((1,), (1,)), ((), ())),
        preferred_element_type=jnp.float32,
    ).astype(jnp.bfloat16)
    weight_term = lax.dot_general(
        features.astype(jnp.float32),
        back_own,
        (((0,), (0,)), ((), ())),
        precision=lax.Precision.HIGHEST,
    )
    grad_weight, grad_bias = lax.psum((weight_term, bias_term), ("row", "col"))
    return (output, grad_features, grad_weight, grad_bias)


def solution(mesh):
    in_specs = (
        P(("row", "col"), None),
        P(),
        P(),
        P(("row", "col"), None),
        P(("row", "col"), None, None),
        P(("row", "col"), None),
        P(("row", "col"), None),
        P(("row", "col")),
    )
    out_specs = (P(("row", "col"), None), P(("row", "col"), None), P(), P())
    return jax.shard_map(body, mesh=mesh, in_specs=in_specs, out_specs=out_specs, check_vma=False)
```

profile of v0, /device:TPU:1, one launch (start us, length us, event | category | flops | bytes accessed | tf_op | source)
XLA Modules:
  0.0 1295.9 jit_solution(2365478727928136077)
XLA Ops:
  12.6 72.7 %all-gather.3.cloned.1.call-done = bf16[4096,512]{1,0:T(8,128)(2,1)} async-done(((bf16[512,512]{1,0:T(8,128)(2,1)}), bf16[4096,512]{1,0:T(8,128)(2,1)}) %all-gather.3.cloned.1.call-update) | async-done | bytes 4194320 | tf_op jit(solution)/shard_map/all_gather | solution.py:46
  85.4 7.9 broadcast_in_dim.21
  93.2 384.8 %while.20 = (s32[]{:T(128)}, f32[64,128,512]{2,1,0:T(8,128)}, s32[12]{0:T(128)S(1)}, s32[384]{0:T(512)S(1)}, bf16[384,128,128]{2,1,0:T(8,128)(2,1)}, /*index=5*/...) while((s32[]{:T(128)}, f32[64,128,512]{2,1,0:T(8,128)}, ...), condition=%wide.region_2.3_spmd, body=%wide.region_0.2_spmd.sunk | while | flops 541066432 | bytes 47191480 | solution.py:34
  106.5 18.8 %scatter_fusion = f32[64,128,512]{2,1,0:T(8,128)} fusion(f32[64,128,512]{2,1,0:T(8,128)} %get-tuple-element.260, s32[32]{0:T(128)S(1)} %get-tuple-element.235, f32[32,128,512]{2,1,0:T(8,128)} %broadcast_multiply_fusion.4), kind=kCustom, calls=%fused_computation.2.clone.1 | custom fusion | flops 2097152 | bytes 25165952 | tf_op jit(solution)/shard_map/while/body/eval_jaxpr/scatter-add | solution.py:31
  131.7 7.0 broadcast_multiply_fusion.4
  138.7 19.0 %scatter_fusion = f32[64,128,512]{2,1,0:T(8,128)} fusion(f32[64,128,512]{2,1,0:T(8,128)} %get-tuple-element.260, s32[32]{0:T(128)S(1)} %get-tuple-element.235, f32[32,128,512]{2,1,0:T(8,128)} %broadcast_multiply_fusion.4), kind=kCustom, calls=%fused_computation.2.clone.1 | custom fusion | flops 2097152 | bytes 25165952 | tf_op jit(solution)/shard_map/while/body/eval_jaxpr/scatter-add | solution.py:31
  164.0 7.0 broadcast_multiply_fusion.4
  171.0 18.9 %scatter_fusion = f32[64,128,512]{2,1,0:T(8,128)} fusion(f32[64,128,512]{2,1,0:T(8,128)} %get-tuple-element.260, s32[32]{0:T(128)S(1)} %get-tuple-element.235, f32[32,128,512]{2,1,0:T(8,128)} %broadcast_multiply_fusion.4), kind=kCustom, calls=%fused_computation.2.clone.1 | custom fusion | flops 2097152 | bytes 25165952 | tf_op jit(solution)/shard_map/while/body/eval_jaxpr/scatter-add | solution.py:31
  203.2 18.7 %scatter_fusion = f32[64,128,512]{2,1,0:T(8,128)} fusion(f32[64,128,512]{2,1,0:T(8,128)} %get-tuple-element.260, s32[32]{0:T(128)S(1)} %get-tuple-element.235, f32[32,128,512]{2,1,0:T(8,128)} %broadcast_multiply_fusion.4), kind=kCustom, calls=%fused_computation.2.clone.1 | custom fusion | flops 2097152 | bytes 25165952 | tf_op jit(solution)/shard_map/while/body/eval_jaxpr/scatter-add | solution.py:31
  235.2 18.7 %scatter_fusion = f32[64,128,512]{2,1,0:T(8,128)} fusion(f32[64,128,512]{2,1,0:T(8,128)} %get-tuple-element.260, s32[32]{0:T(128)S(1)} %get-tuple-element.235, f32[32,128,512]{2,1,0:T(8,128)} %broadcast_multiply_fusion.4), kind=kCustom, calls=%fused_computation.2.clone.1 | custom fusion | flops 2097152 | bytes 25165952 | tf_op jit(solution)/shard_map/while/body/eval_jaxpr/scatter-add | solution.py:31
  267.2 18.5 %scatter_fusion = f32[64,128,512]{2,1,0:T(8,128)} fusion(f32[64,128,512]{2,1,0:T(8,128)} %get-tuple-element.260, s32[32]{0:T(128)S(1)} %get-tuple-element.235, f32[32,128,512]{2,1,0:T(8,128)} %broadcast_multiply_fusion.4), kind=kCustom, calls=%fused_computation.2.clone.1 | custom fusion | flops 2097152 | bytes 25165952 | tf_op jit(solution)/shard_map/while/body/eval_jaxpr/scatter-add | solution.py:31
  299.1 18.6 %scatter_fusion = f32[64,128,512]{2,1,0:T(8,128)} fusion(f32[64,128,512]{2,1,0:T(8,128)} %get-tuple-element.260, s32[32]{0:T(128)S(1)} %get-tuple-element.235, f32[32,128,512]{2,1,0:T(8,128)} %broadcast_multiply_fusion.4), kind=kCustom, calls=%fused_computation.2.clone.1 | custom fusion | flops 2097152 | bytes 25165952 | tf_op jit(solution)/shard_map/while/body/eval_jaxpr/scatter-add | solution.py:31
  331.0 18.9 %scatter_fusion = f32[64,128,512]{2,1,0:T(8,128)} fusion(f32[64,128,512]{2,1,0:T(8,128)} %get-tuple-element.260, s32[32]{0:T(128)S(1)} %get-tuple-element.235, f32[32,128,512]{2,1,0:T(8,128)} %broadcast_multiply_fusion.4), kind=kCustom, calls=%fused_computation.2.clone.1 | custom fusion | flops 2097152 | bytes 25165952 | tf_op jit(solution)/shard_map/while/body/eval_jaxpr/scatter-add | solution.py:31
  363.2 18.8 %scatter_fusion = f32[64,128,512]{2,1,0:T(8,128)} fusion(f32[64,128,512]{2,1,0:T(8,128)} %get-tuple-element.260, s32[32]{0:T(128)S(1)} %get-tuple-element.235, f32[32,128,512]{2,1,0:T(8,128)} %broadcast_multiply_fusion.4), kind=kCustom, calls=%fused_computation.2.clone.1 | custom fusion | flops 2097152 | bytes 25165952 | tf_op jit(solution)/shard_map/while/body/eval_jaxpr/scatter-add | solution.py:31
  395.3 18.6 %scatter_fusion = f32[64,128,512]{2,1,0:T(8,128)} fusion(f32[64,128,512]{2,1,0:T(8,128)} %get-tuple-element.260, s32[32]{0:T(128)S(1)} %get-tuple-element.235, f32[32,128,512]{2,1,0:T(8,128)} %broadcast_multiply_fusion.4), kind=kCustom, calls=%fused_computation.2.clone.1 | custom fusion | flops 2097152 | bytes 25165952 | tf_op jit(solution)/shard_map/while/body/eval_jaxpr/scatter-add | solution.py:31
  427.3 18.7 %scatter_fusion = f32[64,128,512]{2,1,0:T(8,128)} fusion(f32[64,128,512]{2,1,0:T(8,128)} %get-tuple-element.260, s32[32]{0:T(128)S(1)} %get-tuple-element.235, f32[32,128,512]{2,1,0:T(8,128)} %broadcast_multiply_fusion.4), kind=kCustom, calls=%fused_computation.2.clone.1 | custom fusion | flops 2097152 | bytes 25165952 | tf_op jit(solution)/shard_map/while/body/eval_jaxpr/scatter-add | solution.py:31
  459.3 18.8 %scatter_fusion = f32[64,128,512]{2,1,0:T(8,128)} fusion(f32[64,128,512]{2,1,0:T(8,128)} %get-tuple-element.260, s32[32]{0:T(128)S(1)} %get-tuple-element.235, f32[32,128,512]{2,1,0:T(8,128)} %broadcast_multiply_fusion.4), kind=kCustom, calls=%fused_computation.2.clone.1 | custom fusion | flops 2097152 | bytes 25165952 | tf_op jit(solution)/shard_map/while/body/eval_jaxpr/scatter-add | solution.py:31
  478.0 9.0 convert_element_type.41
  487.1 94.4 %reduce-scatter.3.cloned.1.call-done = bf16[512,512]{1,0:T(8,128)(2,1)} async-done(((bf16[8192,512]{1,0:T(8,128)(2,1)}), bf16[512,512]{1,0:T(8,128)(2,1)}) %reduce-scatter.3.cloned.1.call-update) | async-done | bytes 524304 | tf_op jit(solution)/shard_map/reduce_scatter | solution.py:51
  584.1 53.1 %all-gather.5.cloned.1.call-done = bf16[8192,512]{1,0:T(8,128)(2,1)} async-done(((bf16[512,512]{1,0:T(8,128)(2,1)}), bf16[8192,512]{1,0:T(8,128)(2,1)}) %all-gather.5.cloned.1.call-update) | async-done | bytes 8388624 | tf_op jit(solution)/shard_map/all_gather | solution.py:60
  641.5 401.7 %while.21 = (s32[]{:T(128)}, f32[32,128,512]{2,1,0:T(8,128)}, s32[12]{0:T(128)S(1)}, s32[384]{0:T(512)S(1)}, bf16[384,128,128]{2,1,0:T(8,128)(2,1)}, /*index=5*/...) while((s32[]{:T(128)}, f32[32,128,512]{2,1,0:T(8,128)}, ...), condition=%wide.region_6.0_spmd, body=%wide.region_4.0_spmd.sunk | while | flops 541066432 | bytes 47191480 | solution.py:34
  649.1 7.3 broadcast_multiply_fusion.5
  656.3 18.5 %scatter_fusion.1 = f32[32,128,512]{2,1,0:T(8,128)} fusion(f32[32,128,512]{2,1,0:T(8,128)} %get-tuple-element.296, s32[32]{0:T(128)S(1)} %get-tuple-element.245, f32[32,128,512]{2,1,0:T(8,128)} %broadcast_multiply_fusion.5), kind=kCustom, calls=%fused_computation.3.clone.1 | custom fusion | flops 2097152 | bytes 25165952 | tf_op jit(solution)/shard_map/while/body/eval_jaxpr/scatter-add | solution.py:31
  682.4 7.3 broadcast_multiply_fusion.5
  689.7 18.7 %scatter_fusion.1 = f32[32,128,512]{2,1,0:T(8,128)} fusion(f32[32,128,512]{2,1,0:T(8,128)} %get-tuple-element.296, s32[32]{0:T(128)S(1)} %get-tuple-element.245, f32[32,128,512]{2,1,0:T(8,128)} %broadcast_multiply_fusion.5), kind=kCustom, calls=%fused_computation.3.clone.1 | custom fusion | flops 2097152 | bytes 25165952 | tf_op jit(solution)/shard_map/while/body/eval_jaxpr/scatter-add | solution.py:31
  716.0 7.3 broadcast_multiply_fusion.5
  723.2 18.6 %scatter_fusion.1 = f32[32,128,512]{2,1,0:T(8,128)} fusion(f32[32,128,512]{2,1,0:T(8,128)} %get-tuple-element.296, s32[32]{0:T(128)S(1)} %get-tuple-element.245, f32[32,128,512]{2,1,0:T(8,128)} %broadcast_multiply_fusion.5), kind=kCustom, calls=%fused_computation.3.clone.1 | custom fusion | flops 2097152 | bytes 25165952 | tf_op jit(solution)/shard_map/while/body/eval_jaxpr/scatter-add | solution.py:31
  749.4 7.3 broadcast_multiply_fusion.5
  756.6 18.9 %scatter_fusion.1 = f32[32,128,512]{2,1,0:T(8,128)} fusion(f32[32,128,512]{2,1,0:T(8,128)} %get-tuple-element.296, s32[32]{0:T(128)S(1)} %get-tuple-element.245, f32[32,128,512]{2,1,0:T(8,128)} %broadcast_multiply_fusion.5), kind=kCustom, calls=%fused_computation.3.clone.1 | custom fusion | flops 2097152 | bytes 25165952 | tf_op jit(solution)/shard_map/while/body/eval_jaxpr/scatter-add | solution.py:31
  783.1 7.3 broadcast_multiply_fusion.5
  790.3 18.5 %scatter_fusion.1 = f32[32,128,512]{2,1,0:T(8,128)} fusion(f32[32,128,512]{2,1,0:T(8,128)} %get-tuple-element.296, s32[32]{0:T(128)S(1)} %get-tuple-element.245, f32[32,128,512]{2,1,0:T(8,128)} %broadcast_multiply_fusion.5), kind=kCustom, calls=%fused_computation.3.clone.1 | custom fusion | flops 2097152 | bytes 25165952 | tf_op jit(solution)/shard_map/while/body/eval_jaxpr/scatter-add | solution.py:31
  816.4 7.3 broadcast_multiply_fusion.5
  823.7 18.8 %scatter_fusion.1 = f32[32,128,512]{2,1,0:T(8,128)} fusion(f32[32,128,512]{2,1,0:T(8,128)} %get-tuple-element.296, s32[32]{0:T(128)S(1)} %get-tuple-element.245, f32[32,128,512]{2,1,0:T(8,128)} %broadcast_multiply_fusion.5), kind=kCustom, calls=%fused_computation.3.clone.1 | custom fusion | flops 2097152 | bytes 25165952 | tf_op jit(solution)/shard_map/while/body/eval_jaxpr/scatter-add | solution.py:31
  850.0 7.3 broadcast_multiply_fusion.5
  857.3 18.6 %scatter_fusion.1 = f32[32,128,512]{2,1,0:T(8,128)} fusion(f32[32,128,512]{2,1,0:T(8,128)} %get-tuple-element.296, s32[32]{0:T(128)S(1)} %get-tuple-element.245, f32[32,128,512]{2,1,0:T(8,128)} %broadcast_multiply_fusion.5), kind=kCustom, calls=%fused_computation.3.clone.1 | custom fusion | flops 2097152 | bytes 25165952 | tf_op jit(solution)/shard_map/while/body/eval_jaxpr/scatter-add | solution.py:31
  883.4 7.3 broadcast_multiply_fusion.5
  890.7 18.7 %scatter_fusion.1 = f32[32,128,512]{2,1,0:T(8,128)} fusion(f32[32,128,512]{2,1,0:T(8,128)} %get-tuple-element.296, s32[32]{0:T(128)S(1)} %get-tuple-element.245, f32[32,128,512]{2,1,0:T(8,128)} %broadcast_multiply_fusion.5), kind=kCustom, calls=%fused_computation.3.clone.1 | custom fusion | flops 2097152 | bytes 25165952 | tf_op jit(solution)/shard_map/while/body/eval_jaxpr/scatter-add | solution.py:31
  917.0 7.3 broadcast_multiply_fusion.5
  924.2 18.5 %scatter_fusion.1 = f32[32,128,512]{2,1,0:T(8,128)} fusion(f32[32,128,512]{2,1,0:T(8,128)} %get-tuple-element.296, s32[32]{0:T(128)S(1)} %get-tuple-element.245, f32[32,128,512]{2,1,0:T(8,128)} %broadcast_multiply_fusion.5), kind=kCustom, calls=%fused_computation.3.clone.1 | custom fusion | flops 2097152 | bytes 25165952 | tf_op jit(solution)/shard_map/while/body/eval_jaxpr/scatter-add | solution.py:31
  950.3 7.3 broadcast_multiply_fusion.5
  957.6 18.7 %scatter_fusion.1 = f32[32,128,512]{2,1,0:T(8,128)} fusion(f32[32,128,512]{2,1,0:T(8,128)} %get-tuple-element.296, s32[32]{0:T(128)S(1)} %get-tuple-element.245, f32[32,128,512]{2,1,0:T(8,128)} %broadcast_multiply_fusion.5), kind=kCustom, calls=%fused_computation.3.clone.1 | custom fusion | flops 2097152 | bytes 25165952 | tf_op jit(solution)/shard_map/while/body/eval_jaxpr/scatter-add | solution.py:31
  983.9 7.3 broadcast_multiply_fusion.5
  991.1 18.6 %scatter_fusion.1 = f32[32,128,512]{2,1,0:T(8,128)} fusion(f32[32,128,512]{2,1,0:T(8,128)} %get-tuple-element.296, s32[32]{0:T(128)S(1)} %get-tuple-element.245, f32[32,128,512]{2,1,0:T(8,128)} %broadcast_multiply_fusion.5), kind=kCustom, calls=%fused_computation.3.clone.1 | custom fusion | flops 2097152 | bytes 25165952 | tf_op jit(solution)/shard_map/while/body/eval_jaxpr/scatter-add | solution.py:31
  1017.3 7.3 broadcast_multiply_fusion.5
  1024.6 18.6 %scatter_fusion.1 = f32[32,128,512]{2,1,0:T(8,128)} fusion(f32[32,128,512]{2,1,0:T(8,128)} %get-tuple-element.296, s32[32]{0:T(128)S(1)} %get-tuple-element.245, f32[32,128,512]{2,1,0:T(8,128)} %broadcast_multiply_fusion.5), kind=kCustom, calls=%fused_computation.3.clone.1 | custom fusion | flops 2097152 | bytes 25165952 | tf_op jit(solution)/shard_map/while/body/eval_jaxpr/scatter-add | solution.py:31
  1049.3 84.4 %reduce-scatter.5.cloned.1.call-done = bf16[512,512]{1,0:T(8,128)(2,1)} async-done(((bf16[4096,512]{1,0:T(8,128)(2,1)}), bf16[512,512]{1,0:T(8,128)(2,1)}) %reduce-scatter.5.cloned.1.call-update) | async-done | bytes 524304 | tf_op jit(solution)/shard_map/reduce_scatter | solution.py:65
  1136.1 65.4 %psum.15 = f32[512]{0:T(512)} all-reduce(f32[512]{0:T(512)S(1)} %get-tuple-element.134), channel_id=1, replica_groups=mesh['row'=8,'col'=16] {'row','col'}, use_global_device_ids=true, to_apply=%region_10.11 | all-reduce | flops 512 | bytes 4096 | tf_op jit(solution)/shard_map/psum | solution.py:80
  1203.9 83.0 %all-reduce.2.cloned.1.call-done = f32[512,512]{0,1:T(8,128)} async-done(((f32[512,512]{0,1:T(8,128)}), f32[512,512]{0,1:T(8,128)}) %all-reduce.2.cloned.1.call-update) | async-done | bytes 1048592 | tf_op jit(solution)/shard_map/psum | solution.py:80
  (160 shorter events, 246.0 us)
Async XLA Ops:
  7.2 1.0 copy-start
  7.2 78.2 %all-gather.3.cloned.1.call-start = ((), (), s32[]{:S(2)}) async-start(), calls=%async_computation.2 | async-start | bytes 4718592 | tf_op jit(solution)/shard_map/all_gather | solution.py:46
  10.5 571.0 %reduce-scatter.3.cloned.1.call-start = ((), (), s32[]{:S(2)}) async-start(), calls=%async_computation.3 | async-start | bytes 8912896 | tf_op jit(solution)/shard_map/reduce_scatter | solution.py:51
  487.1 94.5 %copy-start.2 = (bf16[512,512]{1,0:T(8,128)(2,1)S(1)}, bf16[512,512]{1,0:T(8,128)(2,1)}, u32[]{:S(2)}) copy-start(bf16[512,512]{1,0:T(8,128)(2,1)} %param.15) | copy-start | bytes 1572868
  487.1 94.5 %copy-start.3 = (f32[512]{0:T(512)S(1)}, f32[512]{0:T(512)}, u32[]{:S(2)}) copy-start(f32[512]{0:T(512)} %param.14) | copy-start | bytes 6148
  487.1 150.1 %all-gather.5.cloned.1.call-start = ((), (), s32[]{:S(2)}) async-start(), calls=%async_computation.4 | async-start | bytes 8912896 | tf_op jit(solution)/shard_map/all_gather | solution.py:60
  584.1 549.6 %reduce-scatter.5.cloned.1.call-start = ((), (), s32[]{:S(2)}) async-start(), calls=%async_computation.5 | async-start | bytes 4718592 | tf_op jit(solution)/shard_map/reduce_scatter | solution.py:65
  1043.2 158.3 %copy-start.1 = (bf16[512,512]{1,0:T(8,128)(2,1)S(1)}, bf16[512,512]{1,0:T(8,128)(2,1)}, u32[]{:S(2)}) copy-start(bf16[512,512]{1,0:T(8,128)(2,1)} %param.13) | copy-start | bytes 1572868
  1049.2 237.6 %all-reduce.2.cloned.1.call-start = ((), (), s32[]{:S(2)}) async-start(), calls=%async_computation.6 | async-start | bytes 2097152 | tf_op jit(solution)/shard_map/psum | solution.py:80
Sparse Core Ops, SparseCore 0:
  10.9 74.3 all-gather.2
  487.2 94.2 reduce-scatter.2
  584.2 52.9 all-gather.4
  1049.3 84.2 reduce-scatter.4
  1139.6 147.2 all-reduce.1
where the time goes:
time: 1300 us
  other arithmetic  470 us (36%)
  waiting for transfers between devices  388 us (30%)
  matrix products  178 us (14%)
  local copies, waits for them, and re-layouts  165 us (13%)
  blocking collectives  65.4 us (5%)
  loops' own time  15.8 us (1%)
  between operations  14.4 us (1%)
    scatter-add x24, other arithmetic, advance(): return (totals.at[target].add(product), None)  449 us
    dot_general x24, matrix products, advance(): jnp.einsum(form, tile_group, picked, preferred_element_type=jnp.float32)  171 us
    reduce_scatter x1, waiting for transfers between devices, body(): lax.psum_scatter(partial_value.astype(jnp.bfloat16), 'col', scatter_dimen...  94.4 us
    reduce_scatter x1, waiting for transfers between devices, body(): lax.psum_scatter(back_part.astype(jnp.bfloat16), 'row', scatter_dimension...  84.4 us
    psum x1, waiting for transfers between devices, body(): grad_weight, grad_bias = lax.psum((weight_term, bias_term), ('row', 'col'))  83 us
    gather x12, local copies, waits for them, and re-layouts, advance(): picked = blocks[row_group]  74.1 us
    all_gather x1, waiting for transfers between devices, body(): hidden = lax.all_gather(hidden_own, 'row', axis=0, tiled=True)  72.7 us
    psum x1, blocking collectives, body(): grad_weight, grad_bias = lax.psum((weight_term, bias_term), ('row', 'col'))  65.4 us
  transfers between devices with their start and end apart: 5, of which 5 were waited for; matrix products, arithmetic and copies ran while one was open for 0% of the time, Pallas kernels for 0%

commit v1 on v0

v1 whole, which is shorter than its diff:
```python
import functools

import jax
import jax.numpy as jnp
from jax import lax
from jax.experimental import pallas as pl
from jax.experimental.pallas import tpu as pltpu
from jax.sharding import PartitionSpec as P

CHUNKS = 1
GROUP = 16
TILE = 128
SPAN = 512
BF = jnp.bfloat16
F32 = jnp.float32


def product_kernel(n_src, n_out, transpose, count_ref, src_idx, dst_idx, values, *refs):
    sources, outs = refs[:n_src], refs[n_src : n_src + n_out]
    source, total = refs[n_src + n_out :]
    step = pl.program_id(0)

    @pl.when(step == 0)
    def _():
        at = 0
        for ref in sources:
            source[at : at + ref.shape[0], :] = ref[...]
            at += ref.shape[0]
        total[...] = jnp.zeros_like(total)

    def one(t):
        slot = step * GROUP + t
        start = pl.multiple_of(src_idx[slot] * TILE, TILE)
        end = pl.multiple_of(dst_idx[slot] * TILE, TILE)
        block = source[pl.ds(start, TILE), :]
        dims = (((0,), (0,)), ((), ())) if transpose else (((1,), (0,)), ((), ()))
        total[pl.ds(end, TILE), :] += lax.dot_general(
            values[t], block, dims, preferred_element_type=F32
        )

    left = count_ref[0] - step * GROUP

    @pl.when(left >= GROUP)
    def _():
        for t in range(GROUP):
            one(t)

    @pl.when((left > 0) & (left < GROUP))
    def _():
        @pl.loop(0, left)
        def _(t):
            one(t)

    @pl.when(step == pl.num_programs(0) - 1)
    def _():
        at = 0
        for ref in outs:
            ref[...] = total[at : at + ref.shape[0], :].astype(BF)
            at += ref.shape[0]


def product(values, count, src_idx, dst_idx, sources, chunk, width, out_rows, transpose):
    rows = sum(s.shape[0] for s in sources)

    def tile_at(i, count_ref, *_):
        return (jnp.minimum(i, (count_ref[0] - 1) // GROUP), 0, 0)

    return pl.pallas_call(
        functools.partial(product_kernel, len(sources), len(out_rows), transpose),
        grid_spec=pltpu.PrefetchScalarGridSpec(
            num_scalar_prefetch=3,
            grid=(values.shape[0] // GROUP,),
            in_specs=[pl.BlockSpec((GROUP, TILE, TILE), tile_at)]
            + [pl.BlockSpec((s.shape[0], width), lambda i, *_: (0, chunk)) for s in sources],
            out_specs=[pl.BlockSpec((r, width), lambda i, *_: (0, 0)) for r in out_rows],
            scratch_shapes=[pltpu.VMEM((rows, width), BF), pltpu.VMEM((sum(out_rows), width), F32)],
        ),
        out_shape=[jax.ShapeDtypeStruct((r, width), BF) for r in out_rows],
        compiler_params=pltpu.CompilerParams(vmem_limit_bytes=58 * 2**20),
        cost_estimate=pl.CostEstimate(
            flops=2 * values.shape[0] * TILE * TILE * width,
            bytes_accessed=2 * values.size + 2 * (rows + sum(out_rows)) * width,
            transcendentals=0,
        ),
    )(count, src_idx, dst_idx, values, *sources)


def from_z(x, s):
    return lax.ppermute(x, "row", [(i, (i & 4) | ((i - s) & 3)) for i in range(8)])


def from_y(x, s):
    return lax.ppermute(x, "col", [(i, (i - 4 * s) & 15) for i in range(16)])


def swap(x, axis, bit):
    return lax.ppermute(x, axis, [(i, i ^ bit) for i in range(lax.axis_size(axis))])


def gather(x, far, axis, bit):
    other = swap(x, axis, bit)
    pieces = [x, other]
    for s in (1, 2, 3):
        pieces += [far(x, s), far(other, s)]
    return pieces


def send_pieces(parts, far):
    return {s: far(parts[s].astype(BF), -s) for s in (1, 3, 2)}


def add_pieces(own, got, axis, bit):
    total = own.astype(F32) + sum(g.astype(F32) for g in got.values())
    rows = total.shape[0] // 2
    across = swap(total[rows:].astype(BF), axis, bit)
    return total[:rows] + across.astype(F32)


def all_sum(x, extra, got):
    col, row = lax.axis_index("col"), lax.axis_index("row")
    path = []
    for bit, axis, at in ((1, "col", col), (2, "col", col)):
        half = x.shape[0] // 2
        side = (at // bit) & 1
        mine = lax.dynamic_slice_in_dim(x, side * half, half, 0)
        theirs = lax.dynamic_slice_in_dim(x, (1 - side) * half, half, 0)
        x = mine + swap(theirs.astype(BF), axis, bit).astype(F32)
        path.append((side, axis, bit))
    x, got[1], got[3] = lax.optimization_barrier((x, got[1], got[3]))
    quarter = x.shape[0] // 4
    y = col // 4
    own = lax.dynamic_slice_in_dim(x, y * quarter, quarter, 0)
    for s in (1, 2, 3):
        part = lax.dynamic_slice_in_dim(x, ((y + s) & 3) * quarter, quarter, 0)
        own = own + from_y(part.astype(BF), -s).astype(F32)
    own = jnp.concatenate([own, jnp.broadcast_to(extra[None], (8, extra.shape[0]))], 0)
    own = own + swap(own, "row", 4)
    far = [from_z(own, s) for s in (1, 2, 3)]
    own = own + far[0] + far[1] + far[2]
    extra = own[-1]
    x = own[:-8].astype(BF)
    pieces = jnp.stack([x] + [from_y(x, s) for s in (1, 2, 3)])
    x = jnp.concatenate([lax.dynamic_index_in_dim(pieces, (k - y) & 3, 0, False) for k in range(4)], 0)
    for side, axis, bit in reversed(path):
        other = swap(x, axis, bit)
        low = jnp.where(side == 0, x, other)
        high = jnp.where(side == 0, other, x)
        x = jnp.concatenate([low, high], 0)
    return x.astype(F32), extra


def body(features, weight, bias, cotangent, tile_values, tile_row, tile_col, tile_count):
    width = weight.shape[1] // CHUNKS
    row, col = lax.axis_index("row"), lax.axis_index("col")
    dest = tile_row[0] >> 2
    order = ((dest ^ col) & 1) * 8 + (((dest >> 2) - (col >> 2)) & 3) * 2 + (((dest ^ col) >> 1) & 1)
    row_idx = order * 4 + (tile_row[0] & 3)
    owner = tile_col[0] >> 2
    order = ((owner - row) & 3) * 2 + (((owner ^ row) >> 2) & 1)
    col_idx = order * 4 + (tile_col[0] & 3)

    feats = gather(features, from_z, "row", 4)
    hidden = [jnp.dot(f, weight, preferred_element_type=F32).astype(BF) for f in feats]

    outputs, features_sum, weight_terms, bias_sums = [], None, [], []
    for chunk in range(CHUNKS):
        cols = slice(chunk * width, (chunk + 1) * width)
        mine, theirs = product(
            tile_values, tile_count, col_idx, row_idx, hidden, chunk, width, [8 * SPAN] * 2, False
        )
        theirs = swap(theirs, "col", 1)
        both = mine.astype(F32) + theirs.astype(F32)
        parts = [both[s * 2 * SPAN : (s + 1) * 2 * SPAN] for s in range(4)]
        got = send_pieces(parts, from_y)
        summed_input = add_pieces(parts[0], got, "col", 2) + bias[None, cols]
        sigma = jax.nn.sigmoid(summed_input)
        outputs.append((summed_input * sigma).astype(BF))
        grad_own = (
            cotangent[:, cols].astype(F32) * sigma * (1.0 + summed_input * (1.0 - sigma))
        ).astype(BF)
        grads = gather(grad_own, from_y, "col", 2)
        grads = grads + [swap(g, "col", 1) for g in grads]
        bias_sum = sum(jnp.sum(g.astype(F32), axis=0) for g in grads)
        backs = product(
            tile_values, tile_count, row_idx, col_idx, grads, 0, width, [2 * SPAN] * 4, True
        )
        got = send_pieces(backs, from_z)
        term = sum(
            lax.dot_general(
                feats[2 * s + t],
                backs[s][t * SPAN : (t + 1) * SPAN],
                (((0,), (0,)), ((), ())),
                preferred_element_type=F32,
            )
            for s in range(4)
            for t in range(2)
        )
        term, bias_sum = all_sum(term, bias_sum, got)
        weight_terms.append(term)
        bias_sums.append(bias_sum)
        back_own = add_pieces(backs[0], got, "row", 4)
        term = lax.dot_general(
            back_own.astype(BF), weight[:, cols], (((1,), (1,)), ((), ())), preferred_element_type=F32
        )
        features_sum = term if features_sum is None else features_sum + term
    return (
        jnp.concatenate(outputs, 1),
        features_sum.astype(BF),
        jnp.concatenate(weight_terms, 1),
        jnp.concatenate(bias_sums),
    )


def solution(mesh):
    in_specs = (
        P(("row", "col"), None),
        P(),
        P(),
        P(("row", "col"), None),
        P(("row", "col"), None, None),
        P(("row", "col"), None),
        P(("row", "col"), None),
        P(("row", "col")),
    )
    out_specs = (P(("row", "col"), None), P(("row", "col"), None), P(), P())
    return jax.shard_map(body, mesh=mesh, in_specs=in_specs, out_specs=out_specs, check_vma=False)
```

time: 1300 us -> 336 us (0.26)
  other arithmetic: 470 us -> 18.3 us
  waiting for transfers between devices: 388 us -> 173 us
  matrix products: 178 us -> 17.2 us
  local copies, waits for them, and re-layouts: 165 us -> 7.21 us
  starting transfers between devices: 0.21 us -> 80.3 us
  blocking collectives: 65.4 us -> 0 us
  Pallas kernels: 0 us -> 38.3 us
  loops' own time: 15.8 us -> 0 us
    scatter-add x24 -> x0, other arithmetic: 449 us -> none  [advance(): return (totals.at[target].add(product), None)]
    reduce_scatter x2 -> x0, waiting for transfers between devices: 179 us -> none  [the longest x1 94.4 us: body(): lax.psum_scatter(partial_value.astype(jnp.bfloat16), 'col', scatter_dimen...]
    ppermute x0 -> x45, waiting for transfers between devices: none -> 173 us  [the longest x15 78 us: from_y(): return lax.ppermute(x, 'col', [(i, i - 4 * s & 15) for i in range(16)])]
    dot_general x27 -> x17, matrix products: 178 us -> 17.2 us  [the longest x8 11 us: body(): jnp.dot(f, weight, preferred_element_type=F32).astype(BF)]
    gather x24 -> x0, local copies, waits for them, and re-layouts: 133 us -> none  [the longest x12 74.1 us: advance(): picked = blocks[row_group]]
    all_gather x2 -> x0, waiting for transfers between devices: 126 us -> none  [the longest x1 72.7 us: body(): hidden = lax.all_gather(hidden_own, 'row', axis=0, tiled=True)]
    psum x1 -> x0, waiting for transfers between devices: 83 us -> none  [body(): grad_weight, grad_bias = lax.psum((weight_term, bias_term), ('row', 'col'))]
    ppermute x0 -> x45, starting transfers between devices: none -> 80.3 us  [the longest x18 35.4 us: swap(): lax.ppermute(x, axis, [(i, i ^ bit) for i in range(lax.axis_size(axis))])]
  transfers between devices with their start and end apart: 5 -> 45, of which waited for: 5 -> 27; matrix products, arithmetic and copies ran while one was open for 0% -> 8% of each run, Pallas kernels for 0% -> 0%
where the time goes in v1:
time: 336 us
  waiting for transfers between devices  173 us (51%)
  starting transfers between devices  80.3 us (24%)
  Pallas kernels  38.3 us (11%)
  other arithmetic  18.3 us (5%)
  matrix products  17.2 us (5%)
  local copies, waits for them, and re-layouts  7.21 us (2%)
    ppermute x15, waiting for transfers between devices, from_y(): return lax.ppermute(x, 'col', [(i, i - 4 * s & 15) for i in range(16)])  78 us
    ppermute x12, waiting for transfers between devices, from_z(): return lax.ppermute(x, 'row', [(i, i & 4 | i - s & 3) for i in range(8)])  53.8 us
    ppermute x18, waiting for transfers between devices, swap(): lax.ppermute(x, axis, [(i, i ^ bit) for i in range(lax.axis_size(axis))])  41 us
    pallas_call x2, Pallas kernels, product(): pl.pallas_call(functools.partial(product_kernel, len(sources), len(out_ro...  38.3 us
    ppermute x18, starting transfers between devices, swap(): lax.ppermute(x, axis, [(i, i ^ bit) for i in range(lax.axis_size(axis))])  35.4 us
    ppermute x12, starting transfers between devices, from_z(): return lax.ppermute(x, 'row', [(i, i & 4 | i - s & 3) for i in range(8)])  23.7 us
    ppermute x15, starting transfers between devices, from_y(): return lax.ppermute(x, 'col', [(i, i - 4 * s & 15) for i in range(16)])  21.2 us
    dot_general x8, matrix products, body(): jnp.dot(f, weight, preferred_element_type=F32).astype(BF)  11 us
  transfers between devices with their start and end apart: 45, of which 27 were waited for; matrix products, arithmetic and copies ran while one was open for 8% of the time, Pallas kernels for 0%

profile of v1, /device:TPU:1, one launch (start us, length us, event | category | flops | bytes accessed | tf_op | source)
XLA Modules:
  0.0 335.8 jit_solution(8742798363935700465)
XLA Ops:
  0.6 3.7 %collective-permute-start = (bf16[512,512]{1,0:T(8,128)(2,1)}, bf16[512,512]{1,0:T(8,128)(2,1)S(1)}, u32[]{:S(2)}, u32[]{:S(2)}) collective-permute-start(bf16[512,512]{1,0:T(8,128)(2,1)} %param.8), channel_id=1, source_target_pairs={{0,64},{16,80},{32,96},{48,112},{64,0},{80,16},{96,32},{112,48},{1... | collective-permute-start | bytes 1572872 | tf_op jit(solution)/shard_map/ppermute | solution.py:97
  4.3 1.6 collective-permute-start.5
  5.9 3.3 collective-permute-start.3
  10.6 1.3 add_reduce_fusion
  11.9 2.3 convolution_convert_fusion.8.refs_0_
  14.2 1.5 collective-permute-done
  15.7 2.0 collective-permute-start.6
  17.7 3.3 collective-permute-start.4
  24.2 7.5 %collective-permute-done.3 = bf16[512,512]{1,0:T(8,128)(2,1)S(1)} collective-permute-done((bf16[512,512]{1,0:T(8,128)(2,1)}, bf16[512,512]{1,0:T(8,128)(2,1)S(1)}, u32[]{:S(2)}, u32[]{:S(2)}) %collective-permute-start.3) | collective-permute-done | bytes 524320 | tf_op jit(solution)/shard_map/ppermute | solution.py:89
  34.2 8.1 %collective-permute-done.6 = bf16[512,512]{1,0:T(8,128)(2,1)S(1)} collective-permute-done((bf16[512,512]{1,0:T(8,128)(2,1)S(1)}, bf16[512,512]{1,0:T(8,128)(2,1)S(1)}, u32[]{:S(2)}, u32[]{:S(2)}) %collective-permute-start.6) | collective-permute-done | bytes 524320 | tf_op jit(solution)/shard_map/ppermute | solution.py:89
  43.6 10.6 %collective-permute-done.4 = bf16[512,512]{1,0:T(8,128)(2,1)S(1)} collective-permute-done((bf16[512,512]{1,0:T(8,128)(2,1)S(1)}, bf16[512,512]{1,0:T(8,128)(2,1)S(1)}, u32[]{:S(2)}, u32[]{:S(2)}) %collective-permute-start.4) | collective-permute-done | bytes 524320 | tf_op jit(solution)/shard_map/ppermute | solution.py:89
  56.7 19.0 %shard_map.111 = (bf16[4096,512]{1,0:T(8,128)(2,1)}, bf16[4096,512]{1,0:T(8,128)(2,1)}) custom-call(s32[1]{0:T(128)S(6)} %copy.33.count_ref, s32[384]{0:T(512)} %get-tuple-element.42.src_idx.dst_idx, s32[384]{0:T(512)} %get-tuple-element.41.dst_idx.src_idx, bf16[384,128,128]{2,1,0:T(8,128)(2,1)} %values.3, ...), custom_call_target="tpu_custom_call" | custom-call | flops 6442450944 | bytes 25165824 | tf_op jit(solution)/shard_map/pallas_call | solution.py:68
  76.3 7.0 %collective-permute-done.7 = bf16[4096,512]{1,0:T(8,128)(2,1)S(1)} collective-permute-done((bf16[4096,512]{1,0:T(8,128)(2,1)}, bf16[4096,512]{1,0:T(8,128)(2,1)S(1)}, u32[]{:S(2)}, u32[]{:S(2)}) %collective-permute-start.7) | collective-permute-done | bytes 4194336 | tf_op jit(solution)/shard_map/ppermute | solution.py:97
  83.3 2.0 copy-done.1
  85.3 5.2 %fusion.20 = (bf16[4096,512]{1,0:T(8,128)(2,1)S(1)}, f32[4096,512]{1,0:T(8,128)S(1)}) fusion(bf16[4096,512]{1,0:T(8,128)(2,1)} %copy-done.1, bf16[4096,512]{1,0:T(8,128)(2,1)} %get-tuple-element.13), kind=kLoop, calls=%fused_computation.84 | loop fusion | flops 8388608 | bytes 20971520 | tf_op jit(solution)/shard_map/convert.5
  90.8 9.5 %collective-permute-start.8 = (bf16[1024,512]{1,0:T(8,128)(2,1)S(1)}, bf16[1024,512]{1,0:T(8,128)(2,1)S(1)}, u32[]{:S(2)}, u32[]{:S(2)}) collective-permute-start(bf16[1024,512]{1,0:T(8,128)(2,1)S(1)} %get-tuple-element.26), channel_id=1, source_target_pairs={{0,4},{1,5},{2,6},{3,7},{4,8},{5,9},{6,10},{7,11},{8,12},{9,13},{1... | collective-permute-start | bytes 3145736 | tf_op jit(solution)/shard_map/ppermute | solution.py:93
  100.4 16.4 %collective-permute-done.10 = bf16[1024,512]{1,0:T(8,128)(2,1)S(1)} collective-permute-done((bf16[1024,512]{1,0:T(8,128)(2,1)S(1)}, bf16[1024,512]{1,0:T(8,128)(2,1)S(1)}, u32[]{:S(2)}, u32[]{:S(2)}) %collective-permute-start.10) | collective-permute-done | bytes 1048608 | tf_op jit(solution)/shard_map/ppermute | solution.py:93
  116.7 23.2 %collective-permute-done.8 = bf16[1024,512]{1,0:T(8,128)(2,1)S(1)} collective-permute-done((bf16[1024,512]{1,0:T(8,128)(2,1)S(1)}, bf16[1024,512]{1,0:T(8,128)(2,1)S(1)}, u32[]{:S(2)}, u32[]{:S(2)}) %collective-permute-start.8) | collective-permute-done | bytes 1048608 | tf_op jit(solution)/shard_map/ppermute | solution.py:93
  139.9 6.1 %collective-permute-done.9 = bf16[1024,512]{1,0:T(8,128)(2,1)S(1)} collective-permute-done((bf16[1024,512]{1,0:T(8,128)(2,1)S(1)}, bf16[1024,512]{1,0:T(8,128)(2,1)S(1)}, u32[]{:S(2)}, u32[]{:S(2)}) %collective-permute-start.9) | collective-permute-done | bytes 1048608 | tf_op jit(solution)/shard_map/ppermute | solution.py:93
  146.7 2.7 collective-permute-start.11
  149.3 11.9 %collective-permute-done.11 = bf16[512,512]{1,0:T(8,128)(2,1)S(1)} collective-permute-done((bf16[512,512]{1,0:T(8,128)(2,1)S(1)}, bf16[512,512]{1,0:T(8,128)(2,1)S(1)}, u32[]{:S(2)}, u32[]{:S(2)}) %collective-permute-start.11) | collective-permute-done | bytes 524320 | tf_op jit(solution)/shard_map/ppermute | solution.py:97
  161.2 1.5 convert_reduce_fusion.15
  164.4 2.4 collective-permute-start.13
  166.8 2.7 collective-permute-start.19
  169.5 5.9 %collective-permute-done.12.refs_1_ = bf16[512,512]{1,0:T(8,128)(2,1)S(1)} collective-permute-done((bf16[512,512]{1,0:T(8,128)(2,1)}, bf16[512,512]{1,0:T(8,128)(2,1)S(1)}, u32[]{:S(2)}, u32[]{:S(2)}) %collective-permute-start.12) | collective-permute-done | bytes 524320 | tf_op jit(solution)/shard_map/ppermute | solution.py:97
  177.6 10.4 %collective-permute-done.13.refs_2_ = bf16[512,512]{1,0:T(8,128)(2,1)} collective-permute-done((bf16[512,512]{1,0:T(8,128)(2,1)}, bf16[512,512]{1,0:T(8,128)(2,1)}, u32[]{:S(2)}, u32[]{:S(2)}) %collective-permute-start.13) | collective-permute-done | bytes 524320 | tf_op jit(solution)/shard_map/ppermute | solution.py:93
  187.9 1.7 collective-permute-start.18
  190.8 2.0 collective-permute-done.17.refs_6_
  194.9 5.1 %collective-permute-done.16.refs_5_ = bf16[512,512]{1,0:T(8,128)(2,1)S(1)} collective-permute-done((bf16[512,512]{1,0:T(8,128)(2,1)S(1)}, bf16[512,512]{1,0:T(8,128)(2,1)S(1)}, u32[]{:S(2)}, u32[]{:S(2)}) %collective-permute-start.16) | collective-permute-done | bytes 524320 | tf_op jit(solution)/shard_map/ppermute | solution.py:93
  200.0 4.7 %collective-permute-start.20 = (bf16[512,512]{1,0:T(8,128)(2,1)S(1)}, bf16[512,512]{1,0:T(8,128)(2,1)S(1)}, u32[]{:S(2)}, u32[]{:S(2)}) collective-permute-start(bf16[512,512]{1,0:T(8,128)(2,1)S(1)} %collective-permute-done.12.refs_1_), channel_id=1, source_target_pairs={{0,1},{1,0},{2,3},{3,2},{4,5},{5,4},{6,7},{7,6},{8,9},{9,8},{10,11... | collective-permute-start | bytes 1572872 | tf_op jit(solution)/shard_map/ppermute | solution.py:97
  205.0 8.1 %collective-permute-done.18.refs_7_ = bf16[512,512]{1,0:T(8,128)(2,1)S(1)} collective-permute-done((bf16[512,512]{1,0:T(8,128)(2,1)S(1)}, bf16[512,512]{1,0:T(8,128)(2,1)S(1)}, u32[]{:S(2)}, u32[]{:S(2)}) %collective-permute-start.18) | collective-permute-done | bytes 524320 | tf_op jit(solution)/shard_map/ppermute | solution.py:93
  215.2 1.5 collective-permute-done.24.refs_13_
  217.6 19.3 %shard_map.112 = (bf16[1024,512]{1,0:T(8,128)(2,1)}, bf16[1024,512]{1,0:T(8,128)(2,1)}, bf16[1024,512]{1,0:T(8,128)(2,1)}, bf16[1024,512]{1,0:T(8,128)(2,1)}) custom-call(s32[1]{0:T(128)S(6)} %copy.33.count_ref, s32[384]{0:T(512)} %get-tuple-element.41.dst_idx.src_idx, s32[384]{0:T(512)} %get-tuple-element.42.src_idx.dst_idx, bf16[384,128,128]{2,1,0:T(8,128)(2,1)} %values.3, ...), custom_call_target="tpu_custom_call" | custom-call | flops 6442450944 | bytes 25165824 | tf_op jit(solution)/shard_map/pallas_call | solution.py:68
  238.1 1.6 collective-permute-start.30
  239.9 1.5 fusion.13
  247.5 1.7 collective-permute-start.27
  250.6 3.4 %collective-permute-start.28 = (bf16[128,512]{1,0:T(8,128)(2,1)S(1)}, bf16[128,512]{1,0:T(8,128)(2,1)S(1)}, u32[]{:S(2)}, u32[]{:S(2)}) collective-permute-start(bf16[128,512]{1,0:T(8,128)(2,1)S(1)} %dynamic-slice_convert_fusion.1), channel_id=1, source_target_pairs={{0,2},{1,3},{2,0},{3,1},{4,6},{5,7},{6,4},{7,5},{8,10},{9,11},{10,... | collective-permute-start | bytes 393224 | tf_op jit(solution)/shard_map/ppermute | solution.py:97
  254.1 3.7 %collective-permute-done.28 = bf16[128,512]{1,0:T(8,128)(2,1)S(1)} collective-permute-done((bf16[128,512]{1,0:T(8,128)(2,1)S(1)}, bf16[128,512]{1,0:T(8,128)(2,1)S(1)}, u32[]{:S(2)}, u32[]{:S(2)}) %collective-permute-start.28) | collective-permute-done | bytes 131104 | tf_op jit(solution)/shard_map/ppermute | solution.py:97
  257.9 27.4 %collective-permute-done.29 = bf16[1024,512]{1,0:T(8,128)(2,1)} collective-permute-done((bf16[1024,512]{1,0:T(8,128)(2,1)}, bf16[1024,512]{1,0:T(8,128)(2,1)}, u32[]{:S(2)}, u32[]{:S(2)}) %collective-permute-start.29) | collective-permute-done | bytes 1048608 | tf_op jit(solution)/shard_map/ppermute | solution.py:89
  285.4 2.6 collective-permute-start.35
  291.3 4.1 %collective-permute-done.36 = f32[40,512]{1,0:T(8,128)S(1)} collective-permute-done((f32[40,512]{1,0:T(8,128)S(1)}, f32[40,512]{1,0:T(8,128)S(1)}, u32[]{:S(2)}, u32[]{:S(2)}) %collective-permute-start.36) | collective-permute-done | bytes 81952 | tf_op jit(solution)/shard_map/ppermute | solution.py:97
  295.5 2.8 collective-permute-start.37
  298.2 5.4 %collective-permute-start.38 = (f32[40,512]{1,0:T(8,128)S(1)}, f32[40,512]{1,0:T(8,128)S(1)}, u32[]{:S(2)}, u32[]{:S(2)}) collective-permute-start(f32[40,512]{1,0:T(8,128)S(1)} %fusion.19), channel_id=1, source_target_pairs={{0,32},{16,48},{32,0},{48,16},{64,96},{80,112},{96,64},{112,80},{1... | collective-permute-start | bytes 245768 | tf_op jit(solution)/shard_map/ppermute | solution.py:89
  304.4 2.7 add_add_fusion
  308.2 2.3 collective-permute-start.40
  311.5 3.3 collective-permute-done.41
  316.1 5.2 %collective-permute-done.43 = bf16[128,512]{1,0:T(8,128)(2,1)S(1)} collective-permute-done((bf16[128,512]{1,0:T(8,128)(2,1)}, bf16[128,512]{1,0:T(8,128)(2,1)S(1)}, u32[]{:S(2)}, u32[]{:S(2)}) %collective-permute-start.43) | collective-permute-done | bytes 131104 | tf_op jit(solution)/shard_map/ppermute | solution.py:97
  321.4 11.9 %collective-permute-start.44 = (bf16[256,512]{1,0:T(8,128)(2,1)S(1)}, bf16[256,512]{1,0:T(8,128)(2,1)S(1)}, u32[]{:S(2)}, u32[]{:S(2)}) collective-permute-start(bf16[256,512]{1,0:T(8,128)(2,1)S(1)} %pad_maximum_fusion), channel_id=1, source_target_pairs={{0,1},{1,0},{2,3},{3,2},{4,5},{5,4},{6,7},{7,6},{8,9},{9,8},{10,11... | collective-permute-start | bytes 786440 | tf_op jit(solution)/shard_map/ppermute | solution.py:97
  (171 shorter events, 41.2 us)
Async XLA Ops:
  0.6 15.0 %collective-permute-start = (bf16[512,512]{1,0:T(8,128)(2,1)}, bf16[512,512]{1,0:T(8,128)(2,1)S(1)}, u32[]{:S(2)}, u32[]{:S(2)}) collective-permute-start(bf16[512,512]{1,0:T(8,128)(2,1)} %param.8), channel_id=1, source_target_pairs={{0,64},{16,80},{32,96},{48,112},{64,0},{80,16},{96,32},{112,48},{1... | collective-permute-start | bytes 1572872 | tf_op jit(solution)/shard_map/ppermute | solution.py:97
  4.3 17.9 %collective-permute-start.5 = (bf16[512,512]{1,0:T(8,128)(2,1)}, bf16[512,512]{1,0:T(8,128)(2,1)S(1)}, u32[]{:S(2)}, u32[]{:S(2)}) collective-permute-start(bf16[512,512]{1,0:T(8,128)(2,1)} %param.8), channel_id=1, source_target_pairs={{0,16},{16,32},{32,48},{48,0},{64,80},{80,96},{96,112},{112,64},{1... | collective-permute-start | bytes 1572872 | tf_op jit(solution)/shard_map/ppermute | solution.py:89
  5.9 25.8 %collective-permute-start.3 = (bf16[512,512]{1,0:T(8,128)(2,1)}, bf16[512,512]{1,0:T(8,128)(2,1)S(1)}, u32[]{:S(2)}, u32[]{:S(2)}) collective-permute-start(bf16[512,512]{1,0:T(8,128)(2,1)} %param.8), channel_id=1, source_target_pairs={{0,32},{16,48},{32,0},{48,16},{64,96},{80,112},{96,64},{112,80},{1... | collective-permute-start | bytes 1572872 | tf_op jit(solution)/shard_map/ppermute | solution.py:89
  9.2 23.7 %collective-permute-start.1 = (bf16[512,512]{1,0:T(8,128)(2,1)}, bf16[512,512]{1,0:T(8,128)(2,1)S(1)}, u32[]{:S(2)}, u32[]{:S(2)}) collective-permute-start(bf16[512,512]{1,0:T(8,128)(2,1)} %param.8), channel_id=1, source_target_pairs={{0,48},{16,0},{32,16},{48,32},{64,112},{80,64},{96,80},{112,96},{1... | collective-permute-start | bytes 1572872 | tf_op jit(solution)/shard_map/ppermute | solution.py:89
  15.7 26.6 %collective-permute-start.6 = (bf16[512,512]{1,0:T(8,128)(2,1)S(1)}, bf16[512,512]{1,0:T(8,128)(2,1)S(1)}, u32[]{:S(2)}, u32[]{:S(2)}) collective-permute-start(bf16[512,512]{1,0:T(8,128)(2,1)S(1)} %collective-permute-done), channel_id=1, source_target_pairs={{0,16},{16,32},{32,48},{48,0},{64,80},{80,96},{96,112},{112,64},{1... | collective-permute-start | bytes 1572872 | tf_op jit(solution)/shard_map/ppermute | solution.py:89
  17.7 36.5 %collective-permute-start.4 = (bf16[512,512]{1,0:T(8,128)(2,1)S(1)}, bf16[512,512]{1,0:T(8,128)(2,1)S(1)}, u32[]{:S(2)}, u32[]{:S(2)}) collective-permute-start(bf16[512,512]{1,0:T(8,128)(2,1)S(1)} %collective-permute-done), channel_id=1, source_target_pairs={{0,32},{16,48},{32,0},{48,16},{64,96},{80,112},{96,64},{112,80},{1... | collective-permute-start | bytes 1572872 | tf_op jit(solution)/shard_map/ppermute | solution.py:89
  22.2 33.3 %collective-permute-start.2 = (bf16[512,512]{1,0:T(8,128)(2,1)S(1)}, bf16[512,512]{1,0:T(8,128)(2,1)S(1)}, u32[]{:S(2)}, u32[]{:S(2)}) collective-permute-start(bf16[512,512]{1,0:T(8,128)(2,1)S(1)} %collective-permute-done), channel_id=1, source_target_pairs={{0,48},{16,0},{32,16},{48,32},{64,112},{80,64},{96,80},{112,96},{1... | collective-permute-start | bytes 1572872 | tf_op jit(solution)/shard_map/ppermute | solution.py:89
  75.7 7.6 %collective-permute-start.7 = (bf16[4096,512]{1,0:T(8,128)(2,1)}, bf16[4096,512]{1,0:T(8,128)(2,1)S(1)}, u32[]{:S(2)}, u32[]{:S(2)}) collective-permute-start(bf16[4096,512]{1,0:T(8,128)(2,1)} %get-tuple-element.14), channel_id=1, source_target_pairs={{0,1},{1,0},{2,3},{3,2},{4,5},{5,4},{6,7},{7,6},{8,9},{9,8},{10,11... | collective-permute-start | bytes 12582920 | tf_op jit(solution)/shard_map/ppermute | solution.py:97
  90.7 26.0 %collective-permute-start.10 = (bf16[1024,512]{1,0:T(8,128)(2,1)S(1)}, bf16[1024,512]{1,0:T(8,128)(2,1)S(1)}, u32[]{:S(2)}, u32[]{:S(2)}) collective-permute-start(bf16[1024,512]{1,0:T(8,128)(2,1)S(1)} %get-tuple-element.27), channel_id=1, source_target_pairs={{0,8},{1,9},{2,10},{3,11},{4,12},{5,13},{6,14},{7,15},{8,0},{9,1},... | collective-permute-start | bytes 3145736 | tf_op jit(solution)/shard_map/ppermute | solution.py:93
  90.8 49.1 %collective-permute-start.8 = (bf16[1024,512]{1,0:T(8,128)(2,1)S(1)}, bf16[1024,512]{1,0:T(8,128)(2,1)S(1)}, u32[]{:S(2)}, u32[]{:S(2)}) collective-permute-start(bf16[1024,512]{1,0:T(8,128)(2,1)S(1)} %get-tuple-element.26), channel_id=1, source_target_pairs={{0,4},{1,5},{2,6},{3,7},{4,8},{5,9},{6,10},{7,11},{8,12},{9,13},{1... | collective-permute-start | bytes 3145736 | tf_op jit(solution)/shard_map/ppermute | solution.py:93
  100.4 45.7 %collective-permute-start.9 = (bf16[1024,512]{1,0:T(8,128)(2,1)S(1)}, bf16[1024,512]{1,0:T(8,128)(2,1)S(1)}, u32[]{:S(2)}, u32[]{:S(2)}) collective-permute-start(bf16[1024,512]{1,0:T(8,128)(2,1)S(1)} %get-tuple-element.28), channel_id=1, source_target_pairs={{0,12},{1,13},{2,14},{3,15},{4,0},{5,1},{6,2},{7,3},{8,4},{9,5},{1... | collective-permute-start | bytes 3145736 | tf_op jit(solution)/shard_map/ppermute | solution.py:93
  146.7 14.5 %collective-permute-start.11 = (bf16[512,512]{1,0:T(8,128)(2,1)S(1)}, bf16[512,512]{1,0:T(8,128)(2,1)S(1)}, u32[]{:S(2)}, u32[]{:S(2)}) collective-permute-start(bf16[512,512]{1,0:T(8,128)(2,1)S(1)} %slice.120), channel_id=1, source_target_pairs={{0,2},{1,3},{2,0},{3,1},{4,6},{5,7},{6,4},{7,5},{8,10},{9,11},{10,... | collective-permute-start | bytes 1572872 | tf_op jit(solution)/shard_map/ppermute | solution.py:97
  162.8 12.6 %collective-permute-start.12 = (bf16[512,512]{1,0:T(8,128)(2,1)}, bf16[512,512]{1,0:T(8,128)(2,1)S(1)}, u32[]{:S(2)}, u32[]{:S(2)}) collective-permute-start(bf16[512,512]{1,0:T(8,128)(2,1)} %get-tuple-element.23.refs_0_), channel_id=1, source_target_pairs={{0,2},{1,3},{2,0},{3,1},{4,6},{5,7},{6,4},{7,5},{8,10},{9,11},{10,... | collective-permute-start | bytes 1572872 | tf_op jit(solution)/shard_map/ppermute | solution.py:97
  163.9 13.6 %collective-permute-start.15 = (bf16[512,512]{1,0:T(8,128)(2,1)}, bf16[512,512]{1,0:T(8,128)(2,1)S(1)}, u32[]{:S(2)}, u32[]{:S(2)}) collective-permute-start(bf16[512,512]{1,0:T(8,128)(2,1)} %get-tuple-element.23.refs_0_), channel_id=1, source_target_pairs={{0,8},{1,9},{2,10},{3,11},{4,12},{5,13},{6,14},{7,15},{8,0},{9,1},... | collective-permute-start | bytes 1572872 | tf_op jit(solution)/shard_map/ppermute | solution.py:93
  164.4 23.5 %collective-permute-start.13 = (bf16[512,512]{1,0:T(8,128)(2,1)}, bf16[512,512]{1,0:T(8,128)(2,1)}, u32[]{:S(2)}, u32[]{:S(2)}) collective-permute-start(bf16[512,512]{1,0:T(8,128)(2,1)} %get-tuple-element.23.refs_0_), channel_id=1, source_target_pairs={{0,12},{1,13},{2,14},{3,15},{4,0},{5,1},{6,2},{7,3},{8,4},{9,5},{1... | collective-permute-start | bytes 1572872 | tf_op jit(solution)/shard_map/ppermute | solution.py:93
  166.8 26.0 %collective-permute-start.17 = (bf16[512,512]{1,0:T(8,128)(2,1)}, bf16[512,512]{1,0:T(8,128)(2,1)}, u32[]{:S(2)}, u32[]{:S(2)}) collective-permute-start(bf16[512,512]{1,0:T(8,128)(2,1)} %get-tuple-element.23.refs_0_), channel_id=1, source_target_pairs={{0,4},{1,5},{2,6},{3,7},{4,8},{5,9},{6,10},{7,11},{8,12},{9,13},{1... | collective-permute-start | bytes 1572872 | tf_op jit(solution)/shard_map/ppermute | solution.py:93
  166.8 27.9 %collective-permute-start.19 = (bf16[512,512]{1,0:T(8,128)(2,1)}, bf16[512,512]{1,0:T(8,128)(2,1)S(1)}, u32[]{:S(2)}, u32[]{:S(2)}) collective-permute-start(bf16[512,512]{1,0:T(8,128)(2,1)} %get-tuple-element.23.refs_0_), channel_id=1, source_target_pairs={{0,1},{1,0},{2,3},{3,2},{4,5},{5,4},{6,7},{7,6},{8,9},{9,8},{10,11... | collective-permute-start | bytes 1572872 | tf_op jit(solution)/shard_map/ppermute | solution.py:97
  175.4 38.4 %copy-start.17 = (bf16[512,512]{1,0:T(8,128)(2,1)}, bf16[512,512]{1,0:T(8,128)(2,1)S(1)}, u32[]{:S(2)}) copy-start(bf16[512,512]{1,0:T(8,128)(2,1)S(1)} %collective-permute-done.12.refs_1_) | copy-start | bytes 1572868
  175.4 29.4 %collective-permute-start.14 = (bf16[512,512]{1,0:T(8,128)(2,1)S(1)}, bf16[512,512]{1,0:T(8,128)(2,1)S(1)}, u32[]{:S(2)}, u32[]{:S(2)}) collective-permute-start(bf16[512,512]{1,0:T(8,128)(2,1)S(1)} %collective-permute-done.12.refs_1_), channel_id=1, source_target_pairs={{0,12},{1,13},{2,14},{3,15},{4,0},{5,1},{6,2},{7,3},{8,4},{9,5},{1... | collective-permute-start | bytes 1572872 | tf_op jit(solution)/shard_map/ppermute | solution.py:93
  177.5 37.0 %copy-start.18 = (bf16[512,512]{1,0:T(8,128)(2,1)}, bf16[512,512]{1,0:T(8,128)(2,1)S(1)}, u32[]{:S(2)}) copy-start(bf16[512,512]{1,0:T(8,128)(2,1)S(1)} %collective-permute-done.15.refs_4_) | copy-start | bytes 1572868
  177.5 22.5 %collective-permute-start.16 = (bf16[512,512]{1,0:T(8,128)(2,1)S(1)}, bf16[512,512]{1,0:T(8,128)(2,1)S(1)}, u32[]{:S(2)}, u32[]{:S(2)}) collective-permute-start(bf16[512,512]{1,0:T(8,128)(2,1)S(1)} %collective-permute-done.12.refs_1_), channel_id=1, source_target_pairs={{0,8},{1,9},{2,10},{3,11},{4,12},{5,13},{6,14},{7,15},{8,0},{9,1},... | collective-permute-start | bytes 1572872 | tf_op jit(solution)/shard_map/ppermute | solution.py:93
  187.9 25.1 %collective-permute-start.18 = (bf16[512,512]{1,0:T(8,128)(2,1)S(1)}, bf16[512,512]{1,0:T(8,128)(2,1)S(1)}, u32[]{:S(2)}, u32[]{:S(2)}) collective-permute-start(bf16[512,512]{1,0:T(8,128)(2,1)S(1)} %collective-permute-done.12.refs_1_), channel_id=1, source_target_pairs={{0,4},{1,5},{2,6},{3,7},{4,8},{5,9},{6,10},{7,11},{8,12},{9,13},{1... | collective-permute-start | bytes 1572872 | tf_op jit(solution)/shard_map/ppermute | solution.py:93
  192.8 21.0 %collective-permute-start.23 = (bf16[512,512]{1,0:T(8,128)(2,1)S(1)}, bf16[512,512]{1,0:T(8,128)(2,1)S(1)}, u32[]{:S(2)}, u32[]{:S(2)}) collective-permute-start(bf16[512,512]{1,0:T(8,128)(2,1)S(1)} %collective-permute-done.15.refs_4_), channel_id=1, source_target_pairs={{0,1},{1,0},{2,3},{3,2},{4,5},{5,4},{6,7},{7,6},{8,9},{9,8},{10,11... | collective-permute-start | bytes 1572872 | tf_op jit(solution)/shard_map/ppermute | solution.py:97
  194.7 19.2 %collective-permute-start.25 = (bf16[512,512]{1,0:T(8,128)(2,1)}, bf16[512,512]{1,0:T(8,128)(2,1)S(1)}, u32[]{:S(2)}, u32[]{:S(2)}) collective-permute-start(bf16[512,512]{1,0:T(8,128)(2,1)} %collective-permute-done.17.refs_6_), channel_id=1, source_target_pairs={{0,1},{1,0},{2,3},{3,2},{4,5},{5,4},{6,7},{7,6},{8,9},{9,8},{10,11... | collective-permute-start | bytes 1572872 | tf_op jit(solution)/shard_map/ppermute | solution.py:97
  200.0 14.8 %collective-permute-start.20 = (bf16[512,512]{1,0:T(8,128)(2,1)S(1)}, bf16[512,512]{1,0:T(8,128)(2,1)S(1)}, u32[]{:S(2)}, u32[]{:S(2)}) collective-permute-start(bf16[512,512]{1,0:T(8,128)(2,1)S(1)} %collective-permute-done.12.refs_1_), channel_id=1, source_target_pairs={{0,1},{1,0},{2,3},{3,2},{4,5},{5,4},{6,7},{7,6},{8,9},{9,8},{10,11... | collective-permute-start | bytes 1572872 | tf_op jit(solution)/shard_map/ppermute | solution.py:97
  204.8 9.9 %collective-permute-start.21 = (bf16[512,512]{1,0:T(8,128)(2,1)}, bf16[512,512]{1,0:T(8,128)(2,1)S(1)}, u32[]{:S(2)}, u32[]{:S(2)}) collective-permute-start(bf16[512,512]{1,0:T(8,128)(2,1)} %collective-permute-done.13.refs_2_), channel_id=1, source_target_pairs={{0,1},{1,0},{2,3},{3,2},{4,5},{5,4},{6,7},{7,6},{8,9},{9,8},{10,11... | collective-permute-start | bytes 1572872 | tf_op jit(solution)/shard_map/ppermute | solution.py:97
  213.1 2.1 collective-permute-start.22
  213.8 2.9 collective-permute-start.24
  213.9 3.6 %collective-permute-start.26 = (bf16[512,512]{1,0:T(8,128)(2,1)S(1)}, bf16[512,512]{1,0:T(8,128)(2,1)}, u32[]{:S(2)}, u32[]{:S(2)}) collective-permute-start(bf16[512,512]{1,0:T(8,128)(2,1)S(1)} %collective-permute-done.18.refs_7_), channel_id=1, source_target_pairs={{0,1},{1,0},{2,3},{3,2},{4,5},{5,4},{6,7},{7,6},{8,9},{9,8},{10,11... | collective-permute-start | bytes 1572872 | tf_op jit(solution)/shard_map/ppermute | solution.py:97
  214.9 25.1 %copy-start.6 = (bf16[512,512]{1,0:T(8,128)(2,1)S(1)}, bf16[512,512]{1,0:T(8,128)(2,1)}, u32[]{:S(2)}) copy-start(bf16[512,512]{1,0:T(8,128)(2,1)} %copy-done.5) | copy-start | bytes 1572868
  236.9 48.3 %collective-permute-start.29 = (bf16[1024,512]{1,0:T(8,128)(2,1)}, bf16[1024,512]{1,0:T(8,128)(2,1)}, u32[]{:S(2)}, u32[]{:S(2)}) collective-permute-start(bf16[1024,512]{1,0:T(8,128)(2,1)} %get-tuple-element.16), channel_id=1, source_target_pairs={{0,16},{16,32},{32,48},{48,0},{64,80},{80,96},{96,112},{112,64},{1... | collective-permute-start | bytes 3145736 | tf_op jit(solution)/shard_map/ppermute | solution.py:89
  238.1 47.2 %collective-permute-start.30 = (bf16[1024,512]{1,0:T(8,128)(2,1)}, bf16[1024,512]{1,0:T(8,128)(2,1)}, u32[]{:S(2)}, u32[]{:S(2)}) collective-permute-start(bf16[1024,512]{1,0:T(8,128)(2,1)} %get-tuple-element.18), channel_id=1, source_target_pairs={{0,48},{16,0},{32,16},{48,32},{64,112},{80,64},{96,80},{112,96},{1... | collective-permute-start | bytes 3145736 | tf_op jit(solution)/shard_map/ppermute | solution.py:89
  239.7 64.8 %collective-permute-start.31 = (bf16[1024,512]{1,0:T(8,128)(2,1)}, bf16[1024,512]{1,0:T(8,128)(2,1)}, u32[]{:S(2)}, u32[]{:S(2)}) collective-permute-start(bf16[1024,512]{1,0:T(8,128)(2,1)} %get-tuple-element.17), channel_id=1, source_target_pairs={{0,32},{16,48},{32,0},{48,16},{64,96},{80,112},{96,64},{112,80},{1... | collective-permute-start | bytes 3145736 | tf_op jit(solution)/shard_map/ppermute | solution.py:89
  247.5 3.0 collective-permute-start.27
  250.6 7.2 %collective-permute-start.28 = (bf16[128,512]{1,0:T(8,128)(2,1)S(1)}, bf16[128,512]{1,0:T(8,128)(2,1)S(1)}, u32[]{:S(2)}, u32[]{:S(2)}) collective-permute-start(bf16[128,512]{1,0:T(8,128)(2,1)S(1)} %dynamic-slice_convert_fusion.1), channel_id=1, source_target_pairs={{0,2},{1,3},{2,0},{3,1},{4,6},{5,7},{6,4},{7,5},{8,10},{9,11},{10,... | collective-permute-start | bytes 393224 | tf_op jit(solution)/shard_map/ppermute | solution.py:97
  285.2 4.1 %collective-permute-start.33 = (bf16[32,512]{1,0:T(8,128)(2,1)S(1)}, bf16[32,512]{1,0:T(8,128)(2,1)S(1)}, u32[]{:S(2)}, u32[]{:S(2)}) collective-permute-start(bf16[32,512]{1,0:T(8,128)(2,1)S(1)} %get-tuple-element.34), channel_id=1, source_target_pairs={{0,4},{1,5},{2,6},{3,7},{4,8},{5,9},{6,10},{7,11},{8,12},{9,13},{1... | collective-permute-start | bytes 98312 | tf_op jit(solution)/shard_map/ppermute | solution.py:93
  285.3 4.4 %collective-permute-start.34 = (bf16[32,512]{1,0:T(8,128)(2,1)S(1)}, bf16[32,512]{1,0:T(8,128)(2,1)S(1)}, u32[]{:S(2)}, u32[]{:S(2)}) collective-permute-start(bf16[32,512]{1,0:T(8,128)(2,1)S(1)} %get-tuple-element.36), channel_id=1, source_target_pairs={{0,8},{1,9},{2,10},{3,11},{4,12},{5,13},{6,14},{7,15},{8,0},{9,1},... | collective-permute-start | bytes 98312 | tf_op jit(solution)/shard_map/ppermute | solution.py:93
  285.4 5.1 %collective-permute-start.35 = (bf16[32,512]{1,0:T(8,128)(2,1)S(1)}, bf16[32,512]{1,0:T(8,128)(2,1)S(1)}, u32[]{:S(2)}, u32[]{:S(2)}) collective-permute-start(bf16[32,512]{1,0:T(8,128)(2,1)S(1)} %get-tuple-element.35), channel_id=1, source_target_pairs={{0,12},{1,13},{2,14},{3,15},{4,0},{5,1},{6,2},{7,3},{8,4},{9,5},{1... | collective-permute-start | bytes 98312 | tf_op jit(solution)/shard_map/ppermute | solution.py:93
  290.6 4.9 %collective-permute-start.36 = (f32[40,512]{1,0:T(8,128)S(1)}, f32[40,512]{1,0:T(8,128)S(1)}, u32[]{:S(2)}, u32[]{:S(2)}) collective-permute-start(f32[40,512]{1,0:T(8,128)S(1)} %pad_maximum_fusion.3), channel_id=1, source_target_pairs={{0,64},{16,80},{32,96},{48,112},{64,0},{80,16},{96,32},{112,48},{1... | collective-permute-start | bytes 245768 | tf_op jit(solution)/shard_map/ppermute | solution.py:97
  295.5 12.5 %collective-permute-start.37 = (f32[40,512]{1,0:T(8,128)S(1)}, f32[40,512]{1,0:T(8,128)S(1)}, u32[]{:S(2)}, u32[]{:S(2)}) collective-permute-start(f32[40,512]{1,0:T(8,128)S(1)} %fusion.19), channel_id=1, source_target_pairs={{0,48},{16,0},{32,16},{48,32},{64,112},{80,64},{96,80},{112,96},{1... | collective-permute-start | bytes 245768 | tf_op jit(solution)/shard_map/ppermute | solution.py:89
  298.2 9.8 %collective-permute-start.38 = (f32[40,512]{1,0:T(8,128)S(1)}, f32[40,512]{1,0:T(8,128)S(1)}, u32[]{:S(2)}, u32[]{:S(2)}) collective-permute-start(f32[40,512]{1,0:T(8,128)S(1)} %fusion.19), channel_id=1, source_target_pairs={{0,32},{16,48},{32,0},{48,16},{64,96},{80,112},{96,64},{112,80},{1... | collective-permute-start | bytes 245768 | tf_op jit(solution)/shard_map/ppermute | solution.py:89
  303.6 4.5 %collective-permute-start.39 = (f32[40,512]{1,0:T(8,128)S(1)}, f32[40,512]{1,0:T(8,128)S(1)}, u32[]{:S(2)}, u32[]{:S(2)}) collective-permute-start(f32[40,512]{1,0:T(8,128)S(1)} %fusion.19), channel_id=1, source_target_pairs={{0,16},{16,32},{32,48},{48,0},{64,80},{80,96},{96,112},{112,64},{1... | collective-permute-start | bytes 245768 | tf_op jit(solution)/shard_map/ppermute | solution.py:89
  308.0 25.3 %collective-permute-start.32 = (bf16[512,512]{1,0:T(8,128)(2,1)}, bf16[512,512]{1,0:T(8,128)(2,1)S(1)}, u32[]{:S(2)}, u32[]{:S(2)}) collective-permute-start(bf16[512,512]{1,0:T(8,128)(2,1)} %slice.119), channel_id=1, source_target_pairs={{0,64},{16,80},{32,96},{48,112},{64,0},{80,16},{96,32},{112,48},{1... | collective-permute-start | bytes 1572872 | tf_op jit(solution)/shard_map/ppermute | solution.py:97
  308.2 3.3 collective-permute-start.40
  310.4 4.3 %collective-permute-start.41 = (bf16[32,512]{1,0:T(8,128)(2,1)S(1)}, bf16[32,512]{1,0:T(8,128)(2,1)S(1)}, u32[]{:S(2)}, u32[]{:S(2)}) collective-permute-start(bf16[32,512]{1,0:T(8,128)(2,1)S(1)} %slice.121), channel_id=1, source_target_pairs={{0,8},{1,9},{2,10},{3,11},{4,12},{5,13},{6,14},{7,15},{8,0},{9,1},... | collective-permute-start | bytes 98312 | tf_op jit(solution)/shard_map/ppermute | solution.py:93
  310.4 4.3 %collective-permute-start.42 = (bf16[32,512]{1,0:T(8,128)(2,1)S(1)}, bf16[32,512]{1,0:T(8,128)(2,1)S(1)}, u32[]{:S(2)}, u32[]{:S(2)}) collective-permute-start(bf16[32,512]{1,0:T(8,128)(2,1)S(1)} %slice.121), channel_id=1, source_target_pairs={{0,4},{1,5},{2,6},{3,7},{4,8},{5,9},{6,10},{7,11},{8,12},{9,13},{1... | collective-permute-start | bytes 98312 | tf_op jit(solution)/shard_map/ppermute | solution.py:93
  315.5 5.8 %collective-permute-start.43 = (bf16[128,512]{1,0:T(8,128)(2,1)}, bf16[128,512]{1,0:T(8,128)(2,1)S(1)}, u32[]{:S(2)}, u32[]{:S(2)}) collective-permute-start(bf16[128,512]{1,0:T(8,128)(2,1)} %pad_maximum_fusion.2), channel_id=1, source_target_pairs={{0,2},{1,3},{2,0},{3,1},{4,6},{5,7},{6,4},{7,5},{8,10},{9,11},{10,... | collective-permute-start | bytes 393224 | tf_op jit(solution)/shard_map/ppermute | solution.py:97
  321.4 13.2 %collective-permute-start.44 = (bf16[256,512]{1,0:T(8,128)(2,1)S(1)}, bf16[256,512]{1,0:T(8,128)(2,1)S(1)}, u32[]{:S(2)}, u32[]{:S(2)}) collective-permute-start(bf16[256,512]{1,0:T(8,128)(2,1)S(1)} %pad_maximum_fusion), channel_id=1, source_target_pairs={{0,1},{1,0},{2,3},{3,2},{4,5},{5,4},{6,7},{7,6},{8,9},{9,8},{10,11... | collective-permute-start | bytes 786440 | tf_op jit(solution)/shard_map/ppermute | solution.py:97
  (30 other events, 189.3 us)

commit v2 on v1

v2 whole, which is shorter than its diff:
```python
import functools

import jax
import jax.numpy as jnp
from jax import lax
from jax.experimental import pallas as pl
from jax.experimental.pallas import tpu as pltpu
from jax.sharding import PartitionSpec as P

GROUP = 16
TILE = 128
BF = jnp.bfloat16
F32 = jnp.float32


def product_kernel(n_src, n_out, transpose, count_ref, src_idx, dst_idx, values, *refs):
    sources, outs = refs[:n_src], refs[n_src : n_src + n_out]
    source, total = refs[n_src + n_out :]
    step = pl.program_id(0)

    @pl.when(step == 0)
    def _():
        at = 0
        for ref in sources:
            source[at : at + ref.shape[0], :] = ref[...]
            at += ref.shape[0]
        source[at:, :] = jnp.zeros((TILE, source.shape[1]), BF)
        total[...] = jnp.zeros_like(total)

    def one(t):
        slot = step * GROUP + t
        start = pl.multiple_of(src_idx[slot] * TILE, TILE)
        end = pl.multiple_of(dst_idx[slot] * TILE, TILE)
        block = source[pl.ds(start, TILE), :]
        dims = (((0,), (0,)), ((), ())) if transpose else (((1,), (0,)), ((), ()))
        total[pl.ds(end, TILE), :] += lax.dot_general(
            values[t], block, dims, preferred_element_type=F32
        )

    @pl.when(step * GROUP < count_ref[0])
    def _():
        for t in range(GROUP):
            one(t)

    @pl.when(step == pl.num_programs(0) - 1)
    def _():
        at = 0
        for ref in outs:
            ref[...] = total[at : at + ref.shape[0], :].astype(BF)
            at += ref.shape[0]


def product(values, count, src_idx, dst_idx, sources, chunk, width, out_rows, transpose):
    rows = sum(s.shape[0] for s in sources)
    used = jnp.arange(values.shape[0], dtype=jnp.int32) < count
    src_idx = jnp.where(used, src_idx, rows // TILE)

    def tile_at(i, count_ref, *_):
        return (jnp.minimum(i, (count_ref[0] - 1) // GROUP), 0, 0)

    return pl.pallas_call(
        functools.partial(product_kernel, len(sources), len(out_rows), transpose),
        grid_spec=pltpu.PrefetchScalarGridSpec(
            num_scalar_prefetch=3,
            grid=(values.shape[0] // GROUP,),
            in_specs=[pl.BlockSpec((GROUP, TILE, TILE), tile_at)]
            + [pl.BlockSpec((s.shape[0], width), lambda i, *_: (0, chunk)) for s in sources],
            out_specs=[pl.BlockSpec((r, width), lambda i, *_: (0, 0)) for r in out_rows],
            scratch_shapes=[pltpu.VMEM((rows + TILE, width), BF), pltpu.VMEM((sum(out_rows), width), F32)],
        ),
        out_shape=[jax.ShapeDtypeStruct((r, width), BF) for r in out_rows],
        compiler_params=pltpu.CompilerParams(vmem_limit_bytes=58 * 2**20),
        cost_estimate=pl.CostEstimate(
            flops=2 * values.shape[0] * TILE * TILE * width,
            bytes_accessed=2 * values.size + 2 * (rows + sum(out_rows)) * width,
            transcendentals=0,
        ),
    )(count, src_idx, dst_idx, values, *sources)


def from_z(x, s):
    return lax.ppermute(x, "row", [(i, (i & 4) | ((i - s) & 3)) for i in range(8)])


def from_y(x, s):
    return lax.ppermute(x, "col", [(i, (i - 4 * s) & 15) for i in range(16)])


def swap(x, axis, bit):
    return lax.ppermute(x, axis, [(i, i ^ bit) for i in range(lax.axis_size(axis))])


def gather_across_first(x, far, axis, bit):
    other = swap(x, axis, bit)
    pieces = [x, other]
    for s in (1, 2, 3):
        pieces += [far(x, s), far(other, s)]
    return pieces


def gather_along_first(x, far, axis, bit, pieces):
    near = jnp.concatenate([x] + [far(x, s) for s in (1, 2, 3)], 0)
    near, pieces[1] = lax.optimization_barrier((near, pieces[1]))
    return [near, swap(near, axis, bit)]


def send_along(parts, far):
    return {s: far(parts[s].astype(BF), -s) for s in (1, 3, 2)}


def end_across(own, got, axis, bit):
    total = own.astype(F32) + sum(g.astype(F32) for g in got.values())
    rows = total.shape[0] // 2
    across = swap(total[rows:].astype(BF), axis, bit)
    return total[:rows] + across.astype(F32)


def end_along(own, across, far):
    total = own.astype(F32) + across.astype(F32)
    rows = total.shape[0] // 4
    parts = [total[s * rows : (s + 1) * rows] for s in range(4)]
    return parts[0] + sum(g.astype(F32) for g in send_along(parts, far).values())


def with_rows(x, extra):
    return jnp.concatenate([x, jnp.broadcast_to(extra[None], (16, extra.shape[0]))], 0).astype(BF)


def halve(x, extra, axis, bit):
    half = x.shape[0] // 2
    side = (lax.axis_index(axis) // bit) & 1
    mine = lax.dynamic_slice_in_dim(x, side * half, half, 0)
    theirs = lax.dynamic_slice_in_dim(x, (1 - side) * half, half, 0)
    got = swap(with_rows(theirs, extra), axis, bit).astype(F32)
    return mine + got[:half], extra + got[half]


def join(x, axis, bit):
    side = (lax.axis_index(axis) // bit) & 1
    x = x.astype(BF)
    other = swap(x, axis, bit)
    return jnp.concatenate([jnp.where(side == 0, x, other), jnp.where(side == 0, other, x)], 0)


def add_all(x, extra, far):
    rows = x.shape[0]
    sent = with_rows(x, extra)
    got = sum(far(sent, s).astype(F32) for s in (1, 2, 3)) + sent.astype(F32)
    return got[:rows], got[rows]


def place(block, side, along, across, sides):
    half, part = (block >> 1) & 1, block & 1
    order = jnp.where(half == 0, along * 2 + across, across * 4 + along)
    return ((half * sides + side) * 8 + order) * 2 + part


def body(features, weight, bias, cotangent, tile_values, tile_row, tile_col, tile_count):
    width = weight.shape[1]
    half = features.shape[0] // 2
    row, col = lax.axis_index("row"), lax.axis_index("col")
    dest = tile_row[0] >> 2
    row_idx = place(
        tile_row[0], (dest ^ col) & 1, ((dest >> 2) - (col >> 2)) & 3, ((dest ^ col) >> 1) & 1, 2
    )
    owner = tile_col[0] >> 2
    col_idx = place(tile_col[0], 0, (owner - row) & 3, ((owner ^ row) >> 2) & 1, 1)

    feats = gather_across_first(features[:half], from_z, "row", 4)
    feats += gather_along_first(features[half:], from_z, "row", 4, feats)

    mine_0, theirs_0, mine_1, theirs_1 = product(
        tile_values, tile_count, col_idx, row_idx, feats, 0, width, [8 * half] * 4, False
    )
    theirs_1 = swap(theirs_1, "col", 1)
    theirs_0 = swap(theirs_0, "col", 1)
    far_1 = mine_1[4 * half :].astype(F32) + theirs_1[4 * half :].astype(F32)
    far_1 = swap(far_1.astype(BF), "col", 2)
    both = mine_0.astype(F32) + theirs_0.astype(F32)
    parts = [both[s * 2 * half : (s + 1) * 2 * half] for s in range(4)]
    got = send_along(parts, from_y)
    sum_1 = end_along(
        mine_1[: 4 * half].astype(F32) + theirs_1[: 4 * half].astype(F32), far_1, from_y
    )
    sum_0 = end_across(parts[0], got, "col", 2)

    def activation(total, rows):
        summed = total.astype(BF)
        summed_input = jnp.dot(summed, weight, preferred_element_type=F32) + bias[None, :]
        sigma = jax.nn.sigmoid(summed_input)
        output = (summed_input * sigma).astype(BF)
        grad = cotangent[rows].astype(F32) * sigma * (1.0 + summed_input * (1.0 - sigma))
        return summed, output, grad.astype(BF)

    summed_0, output_0, grad_0 = activation(sum_0, slice(0, half))
    pieces = gather_across_first(grad_0, from_y, "col", 2)
    summed_1, output_1, grad_1 = activation(sum_1, slice(half, 2 * half))
    other = gather_along_first(grad_1, from_y, "col", 2, pieces)
    grads = [jnp.concatenate(pieces[:4], 0), jnp.concatenate(pieces[4:], 0)]
    grads += [swap(p, "col", 1) for p in grads]
    grads += other + [swap(p, "col", 1) for p in other]

    grad_weight = sum(
        lax.dot_general(s, g, (((0,), (0,)), ((), ())), preferred_element_type=F32)
        for s, g in ((summed_0, grad_0), (summed_1, grad_1))
    )
    grad_bias = jnp.sum(grad_0.astype(F32), axis=0) + jnp.sum(grad_1.astype(F32), axis=0)
    grad_weight, grad_bias = halve(grad_weight, grad_bias, "row", 4)
    grad_weight, grad_bias = add_all(grad_weight, grad_bias, from_z)
    grads[0], grad_weight = lax.optimization_barrier((grads[0], grad_weight))
    grad_weight = join(grad_weight, "row", 4)

    *backs, near_1, far_1 = product(
        tile_values, tile_count, row_idx, col_idx, grads, 0, width, [2 * half] * 4 + [4 * half] * 2, True
    )
    got = send_along(backs, from_z)
    far_1 = swap(far_1, "row", 4)
    for bit in (1, 2):
        grad_weight, grad_bias = halve(grad_weight, grad_bias, "col", bit)
    grad_weight, got[1], got[3] = lax.optimization_barrier((grad_weight, got[1], got[3]))
    grad_weight, grad_bias = add_all(grad_weight, grad_bias, from_y)
    for bit in (2, 1):
        grad_weight = join(grad_weight, "col", bit)
    back_1 = end_along(near_1, far_1, from_z)
    back_0 = end_across(backs[0], got, "row", 4)
    grad_features = [
        lax.dot_general(
            b.astype(BF), weight, (((1,), (1,)), ((), ())), preferred_element_type=F32
        ).astype(BF)
        for b in (back_0, back_1)
    ]
    return (
        jnp.concatenate([output_0, output_1], 0),
        jnp.concatenate(grad_features, 0),
        grad_weight.astype(F32),
        grad_bias,
    )


def solution(mesh):
    in_specs = (
        P(("row", "col"), None),
        P(),
        P(),
        P(("row", "col"), None),
        P(("row", "col"), None, None),
        P(("row", "col"), None),
        P(("row", "col"), None),
        P(("row", "col")),
    )
    out_specs = (P(("row", "col"), None), P(("row", "col"), None), P(), P())
    return jax.shard_map(body, mesh=mesh, in_specs=in_specs, out_specs=out_specs, check_vma=False)
```

time: 336 us -> 288 us (0.86); the launches traced: 336 us -> 283 us
  waiting for transfers between devices: 173 us -> 116 us
  starting transfers between devices: 80.3 us -> 108 us
  matrix products: 17.2 us -> 3.11 us
  Pallas kernels: 38.3 us -> 27.7 us
    ppermute x18 -> x20, waiting for transfers between devices: 41 us -> 16.1 us  [swap(): lax.ppermute(x, axis, [(i, i ^ bit) for i in range(lax.axis_size(axis))])]
    ppermute x15 -> x18, waiting for transfers between devices: 78 us -> 53.5 us  [from_y(): return lax.ppermute(x, 'col', [(i, i - 4 * s & 15) for i in range(16)])]
    dot_general x17 -> x6, matrix products: 17.2 us -> 3.11 us  [the longest x2 1.76 us: activation(): jnp.dot(summed, weight, preferred_element_type=F32) + bias[None, :]]
    ppermute x12 -> x18, starting transfers between devices: 23.7 us -> 37.6 us  [from_z(): return lax.ppermute(x, 'row', [(i, i & 4 | i - s & 3) for i in range(8)])]
    ppermute x18 -> x20, starting transfers between devices: 35.4 us -> 46.6 us  [swap(): lax.ppermute(x, axis, [(i, i ^ bit) for i in range(lax.axis_size(axis))])]
    pallas_call x2, Pallas kernels: 38.3 us -> 27.7 us  [product(): pl.pallas_call(functools.partial(product_kernel, len(sources), len(out_ro...]
    ppermute x12 -> x18, waiting for transfers between devices: 53.8 us -> 46.1 us  [from_z(): return lax.ppermute(x, 'row', [(i, i & 4 | i - s & 3) for i in range(8)])]
    reduce_sum x16 -> x0, other arithmetic: 6.39 us -> none  [body(): bias_sum = sum((jnp.sum(g.astype(F32), axis=0) for g in grads))]
  transfers between devices with their start and end apart: 45 -> 56, of which waited for: 27 -> 24; matrix products, arithmetic and copies ran while one was open for 8% -> 9% of each run, Pallas kernels for 0% -> 0%
where the time goes in v2:
time: 288 us; the launch traced here: 283 us
  waiting for transfers between devices  116 us (40%)
  starting transfers between devices  108 us (38%)
  Pallas kernels  27.7 us (10%)
  other arithmetic  19.1 us (7%)
  local copies, waits for them, and re-layouts  7.96 us (3%)
  matrix products  3.11 us (1%)
    ppermute x18, waiting for transfers between devices, from_y(): return lax.ppermute(x, 'col', [(i, i - 4 * s & 15) for i in range(16)])  53.5 us
    ppermute x20, starting transfers between devices, swap(): lax.ppermute(x, axis, [(i, i ^ bit) for i in range(lax.axis_size(axis))])  46.6 us
    ppermute x18, waiting for transfers between devices, from_z(): return lax.ppermute(x, 'row', [(i, i & 4 | i - s & 3) for i in range(8)])  46.1 us
    ppermute x18, starting transfers between devices, from_z(): return lax.ppermute(x, 'row', [(i, i & 4 | i - s & 3) for i in range(8)])  37.6 us
    pallas_call x2, Pallas kernels, product(): pl.pallas_call(functools.partial(product_kernel, len(sources), len(out_ro...  27.7 us
    ppermute x18, starting transfers between devices, from_y(): return lax.ppermute(x, 'col', [(i, i - 4 * s & 15) for i in range(16)])  23.7 us
    ppermute x20, waiting for transfers between devices, swap(): lax.ppermute(x, axis, [(i, i ^ bit) for i in range(lax.axis_size(axis))])  16.1 us
  transfers between devices with their start and end apart: 56, of which 24 were waited for; matrix products, arithmetic and copies ran while one was open for 9% of the time, Pallas kernels for 0%

profile of v2, /device:TPU:1, one launch (start us, length us, event | category | flops | bytes accessed | tf_op | source)
XLA Modules:
  0.0 283.4 jit_solution(11099153480683045974)
XLA Ops:
  1.8 4.7 %collective-permute-start = (bf16[256,512]{1,0:T(8,128)(2,1)S(1)}, bf16[256,512]{1,0:T(8,128)(2,1)S(1)}, u32[]{:S(2)}, u32[]{:S(2)}) collective-permute-start(bf16[256,512]{1,0:T(8,128)(2,1)S(1)} %get-tuple-element.85), channel_id=1, source_target_pairs={{0,48},{16,0},{32,16},{48,32},{64,112},{80,64},{96,80},{112,96},{1... | collective-permute-start | bytes 786440 | tf_op jit(solution)/shard_map/ppermute | solution.py:82
  7.2 2.7 collective-permute-start.3
  9.9 7.0 %collective-permute-done = bf16[256,512]{1,0:T(8,128)(2,1)S(1)} collective-permute-done((bf16[256,512]{1,0:T(8,128)(2,1)S(1)}, bf16[256,512]{1,0:T(8,128)(2,1)S(1)}, u32[]{:S(2)}, u32[]{:S(2)}) %collective-permute-start) | collective-permute-done | bytes 262176 | tf_op jit(solution)/shard_map/ppermute | solution.py:82
  16.9 4.3 %collective-permute-done.2 = bf16[256,512]{1,0:T(8,128)(2,1)S(1)} collective-permute-done((bf16[256,512]{1,0:T(8,128)(2,1)S(1)}, bf16[256,512]{1,0:T(8,128)(2,1)S(1)}, u32[]{:S(2)}, u32[]{:S(2)}) %collective-permute-start.2) | collective-permute-done | bytes 262176 | tf_op jit(solution)/shard_map/ppermute | solution.py:82
  21.3 2.8 collective-permute-start.10
  25.7 2.4 collective-permute-start.5
  28.1 2.6 collective-permute-done.4.refs_2_
  31.9 5.0 %collective-permute-start.9 = (bf16[256,512]{1,0:T(8,128)(2,1)S(1)}, bf16[256,512]{1,0:T(8,128)(2,1)S(1)}, u32[]{:S(2)}, u32[]{:S(2)}) collective-permute-start(bf16[256,512]{1,0:T(8,128)(2,1)S(1)} %collective-permute-done.3.refs_1_), channel_id=1, source_target_pairs={{0,16},{16,32},{32,48},{48,0},{64,80},{80,96},{96,112},{112,64},{1... | collective-permute-start | bytes 786440 | tf_op jit(solution)/shard_map/ppermute | solution.py:82
  38.2 3.7 %collective-permute-done.8.refs_6_ = bf16[256,512]{1,0:T(8,128)(2,1)} collective-permute-done((bf16[256,512]{1,0:T(8,128)(2,1)S(1)}, bf16[256,512]{1,0:T(8,128)(2,1)}, u32[]{:S(2)}, u32[]{:S(2)}) %collective-permute-start.8) | collective-permute-done | bytes 262176 | tf_op jit(solution)/shard_map/ppermute | solution.py:82
  42.7 7.3 %collective-permute-done.9.refs_7_ = bf16[256,512]{1,0:T(8,128)(2,1)S(1)} collective-permute-done((bf16[256,512]{1,0:T(8,128)(2,1)S(1)}, bf16[256,512]{1,0:T(8,128)(2,1)S(1)}, u32[]{:S(2)}, u32[]{:S(2)}) %collective-permute-start.9) | collective-permute-done | bytes 262176 | tf_op jit(solution)/shard_map/ppermute | solution.py:82
  51.1 14.1 %shard_map.111 = (bf16[2048,512]{1,0:T(8,128)(2,1)}, bf16[2048,512]{1,0:T(8,128)(2,1)}, bf16[2048,512]{1,0:T(8,128)(2,1)}, bf16[2048,512]{1,0:T(8,128)(2,1)}) custom-call(s32[1]{0:T(128)} %copy.15.count_ref, s32[384]{0:T(512)} %get-tuple-element.89.src_idx, s32[384]{0:T(512)} %get-tuple-element.59.dst_idx, bf16[384,128,128]{2,1,0:T(8,128)(2,1)} %values.3, ...), custom_call_target="tpu_custom_call" | custom-call | flops 6442450944 | bytes 25165824 | tf_op jit(solution)/shard_map/pallas_call | solution.py:61
  65.2 6.9 %collective-permute-start.16 = (bf16[2048,512]{1,0:T(8,128)(2,1)}, bf16[2048,512]{1,0:T(8,128)(2,1)S(1)}, u32[]{:S(2)}, u32[]{:S(2)}) collective-permute-start(bf16[2048,512]{1,0:T(8,128)(2,1)} %get-tuple-element.28), channel_id=1, source_target_pairs={{0,1},{1,0},{2,3},{3,2},{4,5},{5,4},{6,7},{7,6},{8,9},{9,8},{10,11... | collective-permute-start | bytes 6291464 | tf_op jit(solution)/shard_map/ppermute | solution.py:90
  72.2 3.9 %collective-permute-done.16 = bf16[2048,512]{1,0:T(8,128)(2,1)S(1)} collective-permute-done((bf16[2048,512]{1,0:T(8,128)(2,1)}, bf16[2048,512]{1,0:T(8,128)(2,1)S(1)}, u32[]{:S(2)}, u32[]{:S(2)}) %collective-permute-start.16) | collective-permute-done | bytes 2097184 | tf_op jit(solution)/shard_map/ppermute | solution.py:90
  76.2 2.5 add_convert_fusion
  78.6 5.3 %collective-permute-start.17 = (bf16[1024,512]{1,0:T(8,128)(2,1)}, bf16[1024,512]{1,0:T(8,128)(2,1)}, u32[]{:S(2)}, u32[]{:S(2)}) collective-permute-start(bf16[1024,512]{1,0:T(8,128)(2,1)} %add_convert_fusion), channel_id=1, source_target_pairs={{0,2},{1,3},{2,0},{3,1},{4,6},{5,7},{6,4},{7,5},{8,10},{9,11},{10,... | collective-permute-start | bytes 3145736 | tf_op jit(solution)/shard_map/ppermute | solution.py:90
  84.0 2.8 fusion.18
  88.0 3.2 %collective-permute-start.12 = (bf16[512,512]{1,0:T(8,128)(2,1)}, bf16[512,512]{1,0:T(8,128)(2,1)S(1)}, u32[]{:S(2)}, u32[]{:S(2)}) collective-permute-start(bf16[512,512]{1,0:T(8,128)(2,1)} %get-tuple-element.68), channel_id=1, source_target_pairs={{0,4},{1,5},{2,6},{3,7},{4,8},{5,9},{6,10},{7,11},{8,12},{9,13},{1... | collective-permute-start | bytes 1572872 | tf_op jit(solution)/shard_map/ppermute | solution.py:86
  93.6 10.9 %collective-permute-done.12 = bf16[512,512]{1,0:T(8,128)(2,1)S(1)} collective-permute-done((bf16[512,512]{1,0:T(8,128)(2,1)}, bf16[512,512]{1,0:T(8,128)(2,1)S(1)}, u32[]{:S(2)}, u32[]{:S(2)}) %collective-permute-start.12) | collective-permute-done | bytes 524320 | tf_op jit(solution)/shard_map/ppermute | solution.py:86
  104.6 12.2 %collective-permute-done.14 = bf16[512,512]{1,0:T(8,128)(2,1)} collective-permute-done((bf16[512,512]{1,0:T(8,128)(2,1)}, bf16[512,512]{1,0:T(8,128)(2,1)}, u32[]{:S(2)}, u32[]{:S(2)}) %collective-permute-start.14) | collective-permute-done | bytes 524320 | tf_op jit(solution)/shard_map/ppermute | solution.py:86
  116.8 1.9 slice_add_fusion
  122.1 2.1 collective-permute-start.19
  125.7 4.5 %collective-permute-done.18 = bf16[256,512]{1,0:T(8,128)(2,1)S(1)} collective-permute-done((bf16[256,512]{1,0:T(8,128)(2,1)S(1)}, bf16[256,512]{1,0:T(8,128)(2,1)S(1)}, u32[]{:S(2)}, u32[]{:S(2)}) %collective-permute-start.18) | collective-permute-done | bytes 262176 | tf_op jit(solution)/shard_map/ppermute | solution.py:86
  130.2 3.9 %collective-permute-done.20 = bf16[256,512]{1,0:T(8,128)(2,1)S(1)} collective-permute-done((bf16[256,512]{1,0:T(8,128)(2,1)S(1)}, bf16[256,512]{1,0:T(8,128)(2,1)S(1)}, u32[]{:S(2)}, u32[]{:S(2)}) %collective-permute-start.20) | collective-permute-done | bytes 262176 | tf_op jit(solution)/shard_map/ppermute | solution.py:86
  136.0 2.1 collective-permute-start.21
  140.1 2.7 collective-permute-done.21
  142.8 3.6 %collective-permute-start.25 = (bf16[256,512]{1,0:T(8,128)(2,1)S(1)}, bf16[256,512]{1,0:T(8,128)(2,1)S(1)}, u32[]{:S(2)}, u32[]{:S(2)}) collective-permute-start(bf16[256,512]{1,0:T(8,128)(2,1)S(1)} %get-tuple-element.82), channel_id=1, source_target_pairs={{0,12},{1,13},{2,14},{3,15},{4,0},{5,1},{6,2},{7,3},{8,4},{9,5},{1... | collective-permute-start | bytes 786440 | tf_op jit(solution)/shard_map/ppermute | solution.py:86
  146.5 2.8 collective-permute-start.26
  149.3 4.2 %collective-permute-done.23 = bf16[256,512]{1,0:T(8,128)(2,1)S(1)} collective-permute-done((bf16[256,512]{1,0:T(8,128)(2,1)S(1)}, bf16[256,512]{1,0:T(8,128)(2,1)S(1)}, u32[]{:S(2)}, u32[]{:S(2)}) %collective-permute-start.23) | collective-permute-done | bytes 262176 | tf_op jit(solution)/shard_map/ppermute | solution.py:86
  156.7 2.8 collective-permute-start.28
  161.4 5.8 %collective-permute-done.26 = bf16[256,512]{1,0:T(8,128)(2,1)S(1)} collective-permute-done((bf16[256,512]{1,0:T(8,128)(2,1)}, bf16[256,512]{1,0:T(8,128)(2,1)S(1)}, u32[]{:S(2)}, u32[]{:S(2)}) %collective-permute-start.26) | collective-permute-done | bytes 262176 | tf_op jit(solution)/shard_map/ppermute | solution.py:86
  167.3 2.0 pad_maximum_fusion.2.refs_0_
  171.3 6.5 %collective-permute-start.38 = (bf16[1024,512]{1,0:T(8,128)(2,1)S(1)}, bf16[1024,512]{1,0:T(8,128)(2,1)}, u32[]{:S(2)}, u32[]{:S(2)}) collective-permute-start(bf16[1024,512]{1,0:T(8,128)(2,1)S(1)} %pad_maximum_fusion.1.refs_4_), channel_id=1, source_target_pairs={{0,1},{1,0},{2,3},{3,2},{4,5},{5,4},{6,7},{7,6},{8,9},{9,8},{10,11... | collective-permute-start | bytes 3145736 | tf_op jit(solution)/shard_map/ppermute | solution.py:90
  179.0 8.6 %collective-permute-done.34 = bf16[256,512]{1,0:T(8,128)(2,1)S(1)} collective-permute-done((bf16[256,512]{1,0:T(8,128)(2,1)}, bf16[256,512]{1,0:T(8,128)(2,1)S(1)}, u32[]{:S(2)}, u32[]{:S(2)}) %collective-permute-start.34) | collective-permute-done | bytes 262176 | tf_op jit(solution)/shard_map/ppermute | solution.py:86
  188.4 2.0 collective-permute-start.36
  190.4 6.0 %collective-permute-start.39 = (bf16[1024,512]{1,0:T(8,128)(2,1)}, bf16[1024,512]{1,0:T(8,128)(2,1)}, u32[]{:S(2)}, u32[]{:S(2)}) collective-permute-start(bf16[1024,512]{1,0:T(8,128)(2,1)} %collective-permute-done.37.refs_5_), channel_id=1, source_target_pairs={{0,1},{1,0},{2,3},{3,2},{4,5},{5,4},{6,7},{7,6},{8,9},{9,8},{10,11... | collective-permute-start | bytes 3145736 | tf_op jit(solution)/shard_map/ppermute | solution.py:90
  197.1 2.0 collective-permute-done.41
  199.6 13.6 %shard_map.112 = (bf16[512,512]{1,0:T(8,128)(2,1)}, bf16[512,512]{1,0:T(8,128)(2,1)}, bf16[512,512]{1,0:T(8,128)(2,1)}, bf16[512,512]{1,0:T(8,128)(2,1)}, bf16[1...) custom-call(s32[1]{0:T(128)} %copy.15.count_ref, s32[384]{0:T(512)} %get-tuple-element.58.src_idx, ...), custom_call_target="tpu_custom_call" | custom-call | flops 6442450944 | bytes 25165824 | tf_op jit(solution)/shard_map/pallas_call | solution.py:61
  213.1 13.3 %collective-permute-start.44 = (bf16[512,512]{1,0:T(8,128)(2,1)}, bf16[512,512]{1,0:T(8,128)(2,1)S(1)}, u32[]{:S(2)}, u32[]{:S(2)}) collective-permute-start(bf16[512,512]{1,0:T(8,128)(2,1)} %get-tuple-element.35), channel_id=1, source_target_pairs={{0,48},{16,0},{32,16},{48,32},{64,112},{80,64},{96,80},{112,96},{1... | collective-permute-start | bytes 1572872 | tf_op jit(solution)/shard_map/ppermute | solution.py:82
  226.6 2.2 collective-permute-start.45
  228.7 2.1 collective-permute-done.42
  231.0 5.5 %collective-permute-start.47 = (bf16[1024,512]{1,0:T(8,128)(2,1)}, bf16[1024,512]{1,0:T(8,128)(2,1)S(1)}, u32[]{:S(2)}, u32[]{:S(2)}) collective-permute-start(bf16[1024,512]{1,0:T(8,128)(2,1)} %get-tuple-element.40), channel_id=1, source_target_pairs={{0,64},{16,80},{32,96},{48,112},{64,0},{80,16},{96,32},{112,48},{1... | collective-permute-start | bytes 3145736 | tf_op jit(solution)/shard_map/ppermute | solution.py:90
  236.4 10.1 %collective-permute-done.43 = bf16[512,512]{1,0:T(8,128)(2,1)S(1)} collective-permute-done((bf16[512,512]{1,0:T(8,128)(2,1)}, bf16[512,512]{1,0:T(8,128)(2,1)S(1)}, u32[]{:S(2)}, u32[]{:S(2)}) %collective-permute-start.43) | collective-permute-done | bytes 524320 | tf_op jit(solution)/shard_map/ppermute | solution.py:82
  246.6 4.8 %collective-permute-start.52 = (bf16[144,512]{1,0:T(8,128)(2,1)S(1)}, bf16[144,512]{1,0:T(8,128)(2,1)S(1)}, u32[]{:S(2)}, u32[]{:S(2)}) collective-permute-start(bf16[144,512]{1,0:T(8,128)(2,1)S(1)} %pad_maximum_fusion.10), channel_id=1, source_target_pairs={{0,8},{1,9},{2,10},{3,11},{4,12},{5,13},{6,14},{7,15},{8,0},{9,1},... | collective-permute-start | bytes 442376 | tf_op jit(solution)/shard_map/ppermute | solution.py:86
  251.7 3.7 %collective-permute-start.46 = (bf16[256,512]{1,0:T(8,128)(2,1)S(1)}, bf16[256,512]{1,0:T(8,128)(2,1)S(1)}, u32[]{:S(2)}, u32[]{:S(2)}) collective-permute-start(bf16[256,512]{1,0:T(8,128)(2,1)S(1)} %slice.220), channel_id=1, source_target_pairs={{0,64},{16,80},{32,96},{48,112},{64,0},{80,16},{96,32},{112,48},{1... | collective-permute-start | bytes 786440 | tf_op jit(solution)/shard_map/ppermute | solution.py:90
  257.6 2.4 collective-permute-start.54
  260.0 6.0 %collective-permute-done.46 = bf16[256,512]{1,0:T(8,128)(2,1)S(1)} collective-permute-done((bf16[256,512]{1,0:T(8,128)(2,1)S(1)}, bf16[256,512]{1,0:T(8,128)(2,1)S(1)}, u32[]{:S(2)}, u32[]{:S(2)}) %collective-permute-start.46) | collective-permute-done | bytes 262176 | tf_op jit(solution)/shard_map/ppermute | solution.py:90
  268.0 2.7 collective-permute-start.49
  271.9 10.3 %collective-permute-done.48 = bf16[256,512]{1,0:T(8,128)(2,1)S(1)} collective-permute-done((bf16[256,512]{1,0:T(8,128)(2,1)S(1)}, bf16[256,512]{1,0:T(8,128)(2,1)S(1)}, u32[]{:S(2)}, u32[]{:S(2)}) %collective-permute-start.48) | collective-permute-done | bytes 262176 | tf_op jit(solution)/shard_map/ppermute | solution.py:82
  (179 shorter events, 36.9 us)
Async XLA Ops:
  1.8 15.1 %collective-permute-start = (bf16[256,512]{1,0:T(8,128)(2,1)S(1)}, bf16[256,512]{1,0:T(8,128)(2,1)S(1)}, u32[]{:S(2)}, u32[]{:S(2)}) collective-permute-start(bf16[256,512]{1,0:T(8,128)(2,1)S(1)} %get-tuple-element.85), channel_id=1, source_target_pairs={{0,48},{16,0},{32,16},{48,32},{64,112},{80,64},{96,80},{112,96},{1... | collective-permute-start | bytes 786440 | tf_op jit(solution)/shard_map/ppermute | solution.py:82
  6.5 10.5 %collective-permute-start.1 = (bf16[256,512]{1,0:T(8,128)(2,1)S(1)}, bf16[256,512]{1,0:T(8,128)(2,1)S(1)}, u32[]{:S(2)}, u32[]{:S(2)}) collective-permute-start(bf16[256,512]{1,0:T(8,128)(2,1)S(1)} %get-tuple-element.85), channel_id=1, source_target_pairs={{0,32},{16,48},{32,0},{48,16},{64,96},{80,112},{96,64},{112,80},{1... | collective-permute-start | bytes 786440 | tf_op jit(solution)/shard_map/ppermute | solution.py:82
  6.5 14.7 %collective-permute-start.2 = (bf16[256,512]{1,0:T(8,128)(2,1)S(1)}, bf16[256,512]{1,0:T(8,128)(2,1)S(1)}, u32[]{:S(2)}, u32[]{:S(2)}) collective-permute-start(bf16[256,512]{1,0:T(8,128)(2,1)S(1)} %get-tuple-element.85), channel_id=1, source_target_pairs={{0,16},{16,32},{32,48},{48,0},{64,80},{80,96},{96,112},{112,64},{1... | collective-permute-start | bytes 786440 | tf_op jit(solution)/shard_map/ppermute | solution.py:82
  7.2 14.1 %collective-permute-start.3 = (bf16[256,512]{1,0:T(8,128)(2,1)S(1)}, bf16[256,512]{1,0:T(8,128)(2,1)S(1)}, u32[]{:S(2)}, u32[]{:S(2)}) collective-permute-start(bf16[256,512]{1,0:T(8,128)(2,1)S(1)} %get-tuple-element.86.refs_0_), channel_id=1, source_target_pairs={{0,64},{16,80},{32,96},{48,112},{64,0},{80,16},{96,32},{112,48},{1... | collective-permute-start | bytes 786440 | tf_op jit(solution)/shard_map/ppermute | solution.py:90
  21.3 28.7 %collective-permute-start.10 = (bf16[1024,512]{1,0:T(8,128)(2,1)S(1)}, bf16[1024,512]{1,0:T(8,128)(2,1)S(1)}, u32[]{:S(2)}, u32[]{:S(2)}) collective-permute-start(bf16[1024,512]{1,0:T(8,128)(2,1)S(1)} %pad_maximum_fusion.refs_8_), channel_id=1, source_target_pairs={{0,64},{16,80},{32,96},{48,112},{64,0},{80,16},{96,32},{112,48},{1... | collective-permute-start | bytes 3145736 | tf_op jit(solution)/shard_map/ppermute | solution.py:90
  24.1 7.8 %collective-permute-start.6 = (bf16[256,512]{1,0:T(8,128)(2,1)S(1)}, bf16[256,512]{1,0:T(8,128)(2,1)}, u32[]{:S(2)}, u32[]{:S(2)}) collective-permute-start(bf16[256,512]{1,0:T(8,128)(2,1)S(1)} %get-tuple-element.86.refs_0_), channel_id=1, source_target_pairs={{0,32},{16,48},{32,0},{48,16},{64,96},{80,112},{96,64},{112,80},{1... | collective-permute-start | bytes 786440 | tf_op jit(solution)/shard_map/ppermute | solution.py:82
  24.7 17.2 %collective-permute-start.8 = (bf16[256,512]{1,0:T(8,128)(2,1)S(1)}, bf16[256,512]{1,0:T(8,128)(2,1)}, u32[]{:S(2)}, u32[]{:S(2)}) collective-permute-start(bf16[256,512]{1,0:T(8,128)(2,1)S(1)} %get-tuple-element.86.refs_0_), channel_id=1, source_target_pairs={{0,16},{16,32},{32,48},{48,0},{64,80},{80,96},{96,112},{112,64},{1... | collective-permute-start | bytes 786440 | tf_op jit(solution)/shard_map/ppermute | solution.py:82
  25.7 16.4 %collective-permute-start.5 = (bf16[256,512]{1,0:T(8,128)(2,1)S(1)}, bf16[256,512]{1,0:T(8,128)(2,1)S(1)}, u32[]{:S(2)}, u32[]{:S(2)}) collective-permute-start(bf16[256,512]{1,0:T(8,128)(2,1)S(1)} %collective-permute-done.3.refs_1_), channel_id=1, source_target_pairs={{0,48},{16,0},{32,16},{48,32},{64,112},{80,64},{96,80},{112,96},{1... | collective-permute-start | bytes 786440 | tf_op jit(solution)/shard_map/ppermute | solution.py:82
  30.8 11.9 %collective-permute-start.7 = (bf16[256,512]{1,0:T(8,128)(2,1)S(1)}, bf16[256,512]{1,0:T(8,128)(2,1)S(1)}, u32[]{:S(2)}, u32[]{:S(2)}) collective-permute-start(bf16[256,512]{1,0:T(8,128)(2,1)S(1)} %collective-permute-done.3.refs_1_), channel_id=1, source_target_pairs={{0,32},{16,48},{32,0},{48,16},{64,96},{80,112},{96,64},{112,80},{1... | collective-permute-start | bytes 786440 | tf_op jit(solution)/shard_map/ppermute | solution.py:82
  31.9 18.1 %collective-permute-start.9 = (bf16[256,512]{1,0:T(8,128)(2,1)S(1)}, bf16[256,512]{1,0:T(8,128)(2,1)S(1)}, u32[]{:S(2)}, u32[]{:S(2)}) collective-permute-start(bf16[256,512]{1,0:T(8,128)(2,1)S(1)} %collective-permute-done.3.refs_1_), channel_id=1, source_target_pairs={{0,16},{16,32},{32,48},{48,0},{64,80},{80,96},{96,112},{112,64},{1... | collective-permute-start | bytes 786440 | tf_op jit(solution)/shard_map/ppermute | solution.py:82
  65.2 10.9 %collective-permute-start.16 = (bf16[2048,512]{1,0:T(8,128)(2,1)}, bf16[2048,512]{1,0:T(8,128)(2,1)S(1)}, u32[]{:S(2)}, u32[]{:S(2)}) collective-permute-start(bf16[2048,512]{1,0:T(8,128)(2,1)} %get-tuple-element.28), channel_id=1, source_target_pairs={{0,1},{1,0},{2,3},{3,2},{4,5},{5,4},{6,7},{7,6},{8,9},{9,8},{10,11... | collective-permute-start | bytes 6291464 | tf_op jit(solution)/shard_map/ppermute | solution.py:90
  72.2 11.8 %collective-permute-start.11 = (bf16[2048,512]{1,0:T(8,128)(2,1)}, bf16[2048,512]{1,0:T(8,128)(2,1)S(1)}, u32[]{:S(2)}, u32[]{:S(2)}) collective-permute-start(bf16[2048,512]{1,0:T(8,128)(2,1)} %get-tuple-element.26), channel_id=1, source_target_pairs={{0,1},{1,0},{2,3},{3,2},{4,5},{5,4},{6,7},{7,6},{8,9},{9,8},{10,11... | collective-permute-start | bytes 6291464 | tf_op jit(solution)/shard_map/ppermute | solution.py:90
  78.6 41.0 %collective-permute-start.17 = (bf16[1024,512]{1,0:T(8,128)(2,1)}, bf16[1024,512]{1,0:T(8,128)(2,1)}, u32[]{:S(2)}, u32[]{:S(2)}) collective-permute-start(bf16[1024,512]{1,0:T(8,128)(2,1)} %add_convert_fusion), channel_id=1, source_target_pairs={{0,2},{1,3},{2,0},{3,1},{4,6},{5,7},{6,4},{7,5},{8,10},{9,11},{10,... | collective-permute-start | bytes 3145736 | tf_op jit(solution)/shard_map/ppermute | solution.py:90
  88.0 16.6 %collective-permute-start.12 = (bf16[512,512]{1,0:T(8,128)(2,1)}, bf16[512,512]{1,0:T(8,128)(2,1)S(1)}, u32[]{:S(2)}, u32[]{:S(2)}) collective-permute-start(bf16[512,512]{1,0:T(8,128)(2,1)} %get-tuple-element.68), channel_id=1, source_target_pairs={{0,4},{1,5},{2,6},{3,7},{4,8},{5,9},{6,10},{7,11},{8,12},{9,13},{1... | collective-permute-start | bytes 1572872 | tf_op jit(solution)/shard_map/ppermute | solution.py:86
  91.2 13.4 %collective-permute-start.13 = (bf16[512,512]{1,0:T(8,128)(2,1)}, bf16[512,512]{1,0:T(8,128)(2,1)}, u32[]{:S(2)}, u32[]{:S(2)}) collective-permute-start(bf16[512,512]{1,0:T(8,128)(2,1)} %get-tuple-element.70), channel_id=1, source_target_pairs={{0,12},{1,13},{2,14},{3,15},{4,0},{5,1},{6,2},{7,3},{8,4},{9,5},{1... | collective-permute-start | bytes 1572872 | tf_op jit(solution)/shard_map/ppermute | solution.py:86
  92.4 24.3 %collective-permute-start.14 = (bf16[512,512]{1,0:T(8,128)(2,1)}, bf16[512,512]{1,0:T(8,128)(2,1)}, u32[]{:S(2)}, u32[]{:S(2)}) collective-permute-start(bf16[512,512]{1,0:T(8,128)(2,1)} %get-tuple-element.69), channel_id=1, source_target_pairs={{0,8},{1,9},{2,10},{3,11},{4,12},{5,13},{6,14},{7,15},{8,0},{9,1},... | collective-permute-start | bytes 1572872 | tf_op jit(solution)/shard_map/ppermute | solution.py:86
  121.5 8.7 %collective-permute-start.18 = (bf16[256,512]{1,0:T(8,128)(2,1)S(1)}, bf16[256,512]{1,0:T(8,128)(2,1)S(1)}, u32[]{:S(2)}, u32[]{:S(2)}) collective-permute-start(bf16[256,512]{1,0:T(8,128)(2,1)S(1)} %get-tuple-element.74), channel_id=1, source_target_pairs={{0,4},{1,5},{2,6},{3,7},{4,8},{5,9},{6,10},{7,11},{8,12},{9,13},{1... | collective-permute-start | bytes 786440 | tf_op jit(solution)/shard_map/ppermute | solution.py:86
  122.1 8.1 %collective-permute-start.19 = (bf16[256,512]{1,0:T(8,128)(2,1)S(1)}, bf16[256,512]{1,0:T(8,128)(2,1)S(1)}, u32[]{:S(2)}, u32[]{:S(2)}) collective-permute-start(bf16[256,512]{1,0:T(8,128)(2,1)S(1)} %get-tuple-element.76), channel_id=1, source_target_pairs={{0,12},{1,13},{2,14},{3,15},{4,0},{5,1},{6,2},{7,3},{8,4},{9,5},{1... | collective-permute-start | bytes 786440 | tf_op jit(solution)/shard_map/ppermute | solution.py:86
  124.2 9.8 %collective-permute-start.20 = (bf16[256,512]{1,0:T(8,128)(2,1)S(1)}, bf16[256,512]{1,0:T(8,128)(2,1)S(1)}, u32[]{:S(2)}, u32[]{:S(2)}) collective-permute-start(bf16[256,512]{1,0:T(8,128)(2,1)S(1)} %get-tuple-element.75), channel_id=1, source_target_pairs={{0,8},{1,9},{2,10},{3,11},{4,12},{5,13},{6,14},{7,15},{8,0},{9,1},... | collective-permute-start | bytes 786440 | tf_op jit(solution)/shard_map/ppermute | solution.py:86
  138.1 8.4 %collective-permute-start.22 = (bf16[256,512]{1,0:T(8,128)(2,1)S(1)}, bf16[256,512]{1,0:T(8,128)(2,1)S(1)}, u32[]{:S(2)}, u32[]{:S(2)}) collective-permute-start(bf16[256,512]{1,0:T(8,128)(2,1)S(1)} %get-tuple-element.55), channel_id=1, source_target_pairs={{0,8},{1,9},{2,10},{3,11},{4,12},{5,13},{6,14},{7,15},{8,0},{9,1},... | collective-permute-start | bytes 786440 | tf_op jit(solution)/shard_map/ppermute | solution.py:86
  138.4 15.0 %collective-permute-start.23 = (bf16[256,512]{1,0:T(8,128)(2,1)S(1)}, bf16[256,512]{1,0:T(8,128)(2,1)S(1)}, u32[]{:S(2)}, u32[]{:S(2)}) collective-permute-start(bf16[256,512]{1,0:T(8,128)(2,1)S(1)} %get-tuple-element.55), channel_id=1, source_target_pairs={{0,4},{1,5},{2,6},{3,7},{4,8},{5,9},{6,10},{7,11},{8,12},{9,13},{1... | collective-permute-start | bytes 786440 | tf_op jit(solution)/shard_map/ppermute | solution.py:86
  140.0 15.4 %collective-permute-start.27 = (bf16[272,512]{1,0:T(8,128)(2,1)S(1)}, bf16[272,512]{1,0:T(8,128)(2,1)}, u32[]{:S(2)}, u32[]{:S(2)}) collective-permute-start(bf16[272,512]{1,0:T(8,128)(2,1)S(1)} %pad_maximum_fusion.5), channel_id=1, source_target_pairs={{0,64},{16,80},{32,96},{48,112},{64,0},{80,16},{96,32},{112,48},{1... | collective-permute-start | bytes 835592 | tf_op jit(solution)/shard_map/ppermute | solution.py:90
  142.8 16.7 %collective-permute-start.25 = (bf16[256,512]{1,0:T(8,128)(2,1)S(1)}, bf16[256,512]{1,0:T(8,128)(2,1)S(1)}, u32[]{:S(2)}, u32[]{:S(2)}) collective-permute-start(bf16[256,512]{1,0:T(8,128)(2,1)S(1)} %get-tuple-element.82), channel_id=1, source_target_pairs={{0,12},{1,13},{2,14},{3,15},{4,0},{5,1},{6,2},{7,3},{8,4},{9,5},{1... | collective-permute-start | bytes 786440 | tf_op jit(solution)/shard_map/ppermute | solution.py:86
  146.5 13.5 %collective-permute-start.31 = (bf16[256,512]{1,0:T(8,128)(2,1)S(1)}, bf16[256,512]{1,0:T(8,128)(2,1)S(1)}, u32[]{:S(2)}, u32[]{:S(2)}) collective-permute-start(bf16[256,512]{1,0:T(8,128)(2,1)S(1)} %get-tuple-element.82), channel_id=1, source_target_pairs={{0,8},{1,9},{2,10},{3,11},{4,12},{5,13},{6,14},{7,15},{8,0},{9,1},... | collective-permute-start | bytes 786440 | tf_op jit(solution)/shard_map/ppermute | solution.py:86
  146.5 20.8 %collective-permute-start.26 = (bf16[256,512]{1,0:T(8,128)(2,1)}, bf16[256,512]{1,0:T(8,128)(2,1)S(1)}, u32[]{:S(2)}, u32[]{:S(2)}) collective-permute-start(bf16[256,512]{1,0:T(8,128)(2,1)} %collective-permute-done.24), channel_id=1, source_target_pairs={{0,12},{1,13},{2,14},{3,15},{4,0},{5,1},{6,2},{7,3},{8,4},{9,5},{1... | collective-permute-start | bytes 786440 | tf_op jit(solution)/shard_map/ppermute | solution.py:86
  154.1 15.1 %collective-permute-start.32 = (bf16[256,512]{1,0:T(8,128)(2,1)}, bf16[256,512]{1,0:T(8,128)(2,1)S(1)}, u32[]{:S(2)}, u32[]{:S(2)}) collective-permute-start(bf16[256,512]{1,0:T(8,128)(2,1)} %collective-permute-done.24), channel_id=1, source_target_pairs={{0,8},{1,9},{2,10},{3,11},{4,12},{5,13},{6,14},{7,15},{8,0},{9,1},... | collective-permute-start | bytes 786440 | tf_op jit(solution)/shard_map/ppermute | solution.py:86
  156.7 14.6 %collective-permute-start.28 = (bf16[272,512]{1,0:T(8,128)(2,1)S(1)}, bf16[272,512]{1,0:T(8,128)(2,1)S(1)}, u32[]{:S(2)}, u32[]{:S(2)}) collective-permute-start(bf16[272,512]{1,0:T(8,128)(2,1)S(1)} %pad_maximum_fusion.6), channel_id=1, source_target_pairs={{0,48},{16,0},{32,16},{48,32},{64,112},{80,64},{96,80},{112,96},{1... | collective-permute-start | bytes 835592 | tf_op jit(solution)/shard_map/ppermute | solution.py:82
  159.5 18.3 %collective-permute-start.29 = (bf16[272,512]{1,0:T(8,128)(2,1)S(1)}, bf16[272,512]{1,0:T(8,128)(2,1)S(1)}, u32[]{:S(2)}, u32[]{:S(2)}) collective-permute-start(bf16[272,512]{1,0:T(8,128)(2,1)S(1)} %pad_maximum_fusion.6), channel_id=1, source_target_pairs={{0,32},{16,48},{32,0},{48,16},{64,96},{80,112},{96,64},{112,80},{1... | collective-permute-start | bytes 835592 | tf_op jit(solution)/shard_map/ppermute | solution.py:82
  159.9 17.9 %collective-permute-start.30 = (bf16[272,512]{1,0:T(8,128)(2,1)S(1)}, bf16[272,512]{1,0:T(8,128)(2,1)S(1)}, u32[]{:S(2)}, u32[]{:S(2)}) collective-permute-start(bf16[272,512]{1,0:T(8,128)(2,1)S(1)} %pad_maximum_fusion.6), channel_id=1, source_target_pairs={{0,16},{16,32},{32,48},{48,0},{64,80},{80,96},{96,112},{112,64},{1... | collective-permute-start | bytes 835592 | tf_op jit(solution)/shard_map/ppermute | solution.py:82
  167.3 23.1 %collective-permute-start.37 = (bf16[1024,512]{1,0:T(8,128)(2,1)S(1)}, bf16[1024,512]{1,0:T(8,128)(2,1)}, u32[]{:S(2)}, u32[]{:S(2)}) collective-permute-start(bf16[1024,512]{1,0:T(8,128)(2,1)S(1)} %pad_maximum_fusion.1.refs_4_), channel_id=1, source_target_pairs={{0,2},{1,3},{2,0},{3,1},{4,6},{5,7},{6,4},{7,5},{8,10},{9,11},{10,... | collective-permute-start | bytes 3145736 | tf_op jit(solution)/shard_map/ppermute | solution.py:90
  169.3 8.9 %collective-permute-start.33 = (bf16[256,512]{1,0:T(8,128)(2,1)S(1)}, bf16[256,512]{1,0:T(8,128)(2,1)S(1)}, u32[]{:S(2)}, u32[]{:S(2)}) collective-permute-start(bf16[256,512]{1,0:T(8,128)(2,1)S(1)} %get-tuple-element.82), channel_id=1, source_target_pairs={{0,4},{1,5},{2,6},{3,7},{4,8},{5,9},{6,10},{7,11},{8,12},{9,13},{1... | collective-permute-start | bytes 786440 | tf_op jit(solution)/shard_map/ppermute | solution.py:86
  171.3 28.2 %collective-permute-start.38 = (bf16[1024,512]{1,0:T(8,128)(2,1)S(1)}, bf16[1024,512]{1,0:T(8,128)(2,1)}, u32[]{:S(2)}, u32[]{:S(2)}) collective-permute-start(bf16[1024,512]{1,0:T(8,128)(2,1)S(1)} %pad_maximum_fusion.1.refs_4_), channel_id=1, source_target_pairs={{0,1},{1,0},{2,3},{3,2},{4,5},{5,4},{6,7},{7,6},{8,9},{9,8},{10,11... | collective-permute-start | bytes 3145736 | tf_op jit(solution)/shard_map/ppermute | solution.py:90
  177.8 9.8 %collective-permute-start.34 = (bf16[256,512]{1,0:T(8,128)(2,1)}, bf16[256,512]{1,0:T(8,128)(2,1)S(1)}, u32[]{:S(2)}, u32[]{:S(2)}) collective-permute-start(bf16[256,512]{1,0:T(8,128)(2,1)} %collective-permute-done.24), channel_id=1, source_target_pairs={{0,4},{1,5},{2,6},{3,7},{4,8},{5,9},{6,10},{7,11},{8,12},{9,13},{1... | collective-permute-start | bytes 786440 | tf_op jit(solution)/shard_map/ppermute | solution.py:86
  177.8 21.7 %collective-permute-start.35 = (bf16[1024,512]{1,0:T(8,128)(2,1)}, bf16[1024,512]{1,0:T(8,128)(2,1)}, u32[]{:S(2)}, u32[]{:S(2)}) collective-permute-start(bf16[1024,512]{1,0:T(8,128)(2,1)} %pad_maximum_fusion.2.refs_0_), channel_id=1, source_target_pairs={{0,1},{1,0},{2,3},{3,2},{4,5},{5,4},{6,7},{7,6},{8,9},{9,8},{10,11... | collective-permute-start | bytes 3145736 | tf_op jit(solution)/shard_map/ppermute | solution.py:90
  178.2 12.2 %collective-permute-start.40 = (bf16[256,512]{1,0:T(8,128)(2,1)S(1)}, bf16[256,512]{1,0:T(8,128)(2,1)S(1)}, u32[]{:S(2)}, u32[]{:S(2)}) collective-permute-start(bf16[256,512]{1,0:T(8,128)(2,1)S(1)} %slice.162), channel_id=1, source_target_pairs={{0,64},{16,80},{32,96},{48,112},{64,0},{80,16},{96,32},{112,48},{1... | collective-permute-start | bytes 786440 | tf_op jit(solution)/shard_map/ppermute | solution.py:90
  188.4 11.2 %collective-permute-start.36 = (bf16[1024,512]{1,0:T(8,128)(2,1)}, bf16[1024,512]{1,0:T(8,128)(2,1)}, u32[]{:S(2)}, u32[]{:S(2)}) collective-permute-start(bf16[1024,512]{1,0:T(8,128)(2,1)} %constant_dynamic-update-slice_fusion.refs_1_), channel_id=1, source_target_pairs={{0,1},{1,0},{2,3},{3,2},{4,5},{5,4},{6,7},{7,6},{8,9},{9,8},{10,11... | collective-permute-start | bytes 3145736 | tf_op jit(solution)/shard_map/ppermute | solution.py:90
  190.4 9.1 %collective-permute-start.39 = (bf16[1024,512]{1,0:T(8,128)(2,1)}, bf16[1024,512]{1,0:T(8,128)(2,1)}, u32[]{:S(2)}, u32[]{:S(2)}) collective-permute-start(bf16[1024,512]{1,0:T(8,128)(2,1)} %collective-permute-done.37.refs_5_), channel_id=1, source_target_pairs={{0,1},{1,0},{2,3},{3,2},{4,5},{5,4},{6,7},{7,6},{8,9},{9,8},{10,11... | collective-permute-start | bytes 3145736 | tf_op jit(solution)/shard_map/ppermute | solution.py:90
  213.1 33.4 %collective-permute-start.43 = (bf16[512,512]{1,0:T(8,128)(2,1)}, bf16[512,512]{1,0:T(8,128)(2,1)S(1)}, u32[]{:S(2)}, u32[]{:S(2)}) collective-permute-start(bf16[512,512]{1,0:T(8,128)(2,1)} %get-tuple-element.34), channel_id=1, source_target_pairs={{0,16},{16,32},{32,48},{48,0},{64,80},{80,96},{96,112},{112,64},{1... | collective-permute-start | bytes 1572872 | tf_op jit(solution)/shard_map/ppermute | solution.py:82
  213.1 33.4 %collective-permute-start.44 = (bf16[512,512]{1,0:T(8,128)(2,1)}, bf16[512,512]{1,0:T(8,128)(2,1)S(1)}, u32[]{:S(2)}, u32[]{:S(2)}) collective-permute-start(bf16[512,512]{1,0:T(8,128)(2,1)} %get-tuple-element.35), channel_id=1, source_target_pairs={{0,48},{16,0},{32,16},{48,32},{64,112},{80,64},{96,80},{112,96},{1... | collective-permute-start | bytes 1572872 | tf_op jit(solution)/shard_map/ppermute | solution.py:82
  226.6 24.8 %collective-permute-start.45 = (bf16[512,512]{1,0:T(8,128)(2,1)}, bf16[512,512]{1,0:T(8,128)(2,1)S(1)}, u32[]{:S(2)}, u32[]{:S(2)}) collective-permute-start(bf16[512,512]{1,0:T(8,128)(2,1)} %get-tuple-element.38), channel_id=1, source_target_pairs={{0,32},{16,48},{32,0},{48,16},{64,96},{80,112},{96,64},{112,80},{1... | collective-permute-start | bytes 1572872 | tf_op jit(solution)/shard_map/ppermute | solution.py:82
  231.0 36.5 %collective-permute-start.47 = (bf16[1024,512]{1,0:T(8,128)(2,1)}, bf16[1024,512]{1,0:T(8,128)(2,1)S(1)}, u32[]{:S(2)}, u32[]{:S(2)}) collective-permute-start(bf16[1024,512]{1,0:T(8,128)(2,1)} %get-tuple-element.40), channel_id=1, source_target_pairs={{0,64},{16,80},{32,96},{48,112},{64,0},{80,16},{96,32},{112,48},{1... | collective-permute-start | bytes 3145736 | tf_op jit(solution)/shard_map/ppermute | solution.py:90
  246.5 9.7 %collective-permute-start.51 = (bf16[144,512]{1,0:T(8,128)(2,1)S(1)}, bf16[144,512]{1,0:T(8,128)(2,1)S(1)}, u32[]{:S(2)}, u32[]{:S(2)}) collective-permute-start(bf16[144,512]{1,0:T(8,128)(2,1)S(1)} %pad_maximum_fusion.10), channel_id=1, source_target_pairs={{0,12},{1,13},{2,14},{3,15},{4,0},{5,1},{6,2},{7,3},{8,4},{9,5},{1... | collective-permute-start | bytes 442376 | tf_op jit(solution)/shard_map/ppermute | solution.py:86
  246.6 9.7 %collective-permute-start.52 = (bf16[144,512]{1,0:T(8,128)(2,1)S(1)}, bf16[144,512]{1,0:T(8,128)(2,1)S(1)}, u32[]{:S(2)}, u32[]{:S(2)}) collective-permute-start(bf16[144,512]{1,0:T(8,128)(2,1)S(1)} %pad_maximum_fusion.10), channel_id=1, source_target_pairs={{0,8},{1,9},{2,10},{3,11},{4,12},{5,13},{6,14},{7,15},{8,0},{9,1},... | collective-permute-start | bytes 442376 | tf_op jit(solution)/shard_map/ppermute | solution.py:86
  251.7 14.2 %collective-permute-start.46 = (bf16[256,512]{1,0:T(8,128)(2,1)S(1)}, bf16[256,512]{1,0:T(8,128)(2,1)S(1)}, u32[]{:S(2)}, u32[]{:S(2)}) collective-permute-start(bf16[256,512]{1,0:T(8,128)(2,1)S(1)} %slice.220), channel_id=1, source_target_pairs={{0,64},{16,80},{32,96},{48,112},{64,0},{80,16},{96,32},{112,48},{1... | collective-permute-start | bytes 786440 | tf_op jit(solution)/shard_map/ppermute | solution.py:90
  257.6 9.7 %collective-permute-start.54 = (bf16[128,512]{1,0:T(8,128)(2,1)S(1)}, bf16[128,512]{1,0:T(8,128)(2,1)S(1)}, u32[]{:S(2)}, u32[]{:S(2)}) collective-permute-start(bf16[128,512]{1,0:T(8,128)(2,1)S(1)} %slice.222), channel_id=1, source_target_pairs={{0,2},{1,3},{2,0},{3,1},{4,6},{5,7},{6,4},{7,5},{8,10},{9,11},{10,... | collective-permute-start | bytes 393224 | tf_op jit(solution)/shard_map/ppermute | solution.py:90
  268.0 14.3 %collective-permute-start.48 = (bf16[256,512]{1,0:T(8,128)(2,1)S(1)}, bf16[256,512]{1,0:T(8,128)(2,1)S(1)}, u32[]{:S(2)}, u32[]{:S(2)}) collective-permute-start(bf16[256,512]{1,0:T(8,128)(2,1)S(1)} %get-tuple-element.71), channel_id=1, source_target_pairs={{0,16},{16,32},{32,48},{48,0},{64,80},{80,96},{96,112},{112,64},{1... | collective-permute-start | bytes 786440 | tf_op jit(solution)/shard_map/ppermute | solution.py:82
  268.0 14.2 %collective-permute-start.49 = (bf16[256,512]{1,0:T(8,128)(2,1)S(1)}, bf16[256,512]{1,0:T(8,128)(2,1)S(1)}, u32[]{:S(2)}, u32[]{:S(2)}) collective-permute-start(bf16[256,512]{1,0:T(8,128)(2,1)S(1)} %get-tuple-element.73), channel_id=1, source_target_pairs={{0,48},{16,0},{32,16},{48,32},{64,112},{80,64},{96,80},{112,96},{1... | collective-permute-start | bytes 786440 | tf_op jit(solution)/shard_map/ppermute | solution.py:82
  270.7 11.6 %collective-permute-start.50 = (bf16[256,512]{1,0:T(8,128)(2,1)S(1)}, bf16[256,512]{1,0:T(8,128)(2,1)S(1)}, u32[]{:S(2)}, u32[]{:S(2)}) collective-permute-start(bf16[256,512]{1,0:T(8,128)(2,1)S(1)} %get-tuple-element.72), channel_id=1, source_target_pairs={{0,32},{16,48},{32,0},{48,16},{64,96},{80,112},{96,64},{112,80},{1... | collective-permute-start | bytes 786440 | tf_op jit(solution)/shard_map/ppermute | solution.py:82
  (31 other events, 533.8 us)

commit v3 on v2

v3 whole, which is shorter than its diff:
```python
import functools

import jax
import jax.numpy as jnp
from jax import lax
from jax.experimental import pallas as pl
from jax.experimental.pallas import tpu as pltpu
from jax.sharding import PartitionSpec as P

GROUP = 32
TILE = 128
BF = jnp.bfloat16
F32 = jnp.float32


def product_kernel(n_src, n_out, transpose, count_ref, src_idx, dst_idx, values, *refs):
    sources, outs = refs[:n_src], refs[n_src : n_src + n_out]
    tiles, source, total, staged, sem_source, sem_tile, sem_out = refs[n_src + n_out :]
    groups = (count_ref[0] + GROUP - 1) // GROUP
    arriving = []
    at = 0
    for k, ref in enumerate(sources):
        here = source.at[pl.ds(at, ref.shape[0]), :]
        arriving.append(pltpu.make_async_copy(ref, here, sem_source.at[k]))
        at += ref.shape[0]
    for copy in arriving:
        copy.start()

    def tile_copy(g):
        part = pl.ds(g * GROUP, GROUP)
        return pltpu.make_async_copy(values.at[part], tiles.at[part], sem_tile.at[g])

    @pl.loop(0, groups)
    def _(g):
        tile_copy(g).start()

    source[at:, :] = jnp.zeros((TILE, source.shape[1]), BF)
    total[...] = jnp.zeros_like(total)
    for copy in arriving:
        copy.wait()

    def one(slot):
        start = pl.multiple_of(src_idx[slot] * TILE, TILE)
        end = pl.multiple_of(dst_idx[slot] * TILE, TILE)
        block = source[pl.ds(start, TILE), :]
        dims = (((0,), (0,)), ((), ())) if transpose else (((1,), (0,)), ((), ()))
        total[pl.ds(end, TILE), :] += lax.dot_general(
            tiles[slot], block, dims, preferred_element_type=F32
        )

    @pl.loop(0, groups)
    def _(g):
        tile_copy(g).wait()
        for t in range(GROUP):
            one(g * GROUP + t)

    leaving = []
    at = 0
    for k, ref in enumerate(outs):
        part = pl.ds(at, ref.shape[0])
        staged[part, :] = total[part, :].astype(BF)
        leaving.append(pltpu.make_async_copy(staged.at[part, :], ref, sem_out.at[k]))
        leaving[-1].start()
        at += ref.shape[0]
    for copy in leaving:
        copy.wait()


def product(values, count, src_idx, dst_idx, sources, out_rows, transpose):
    rows, width = sum(s.shape[0] for s in sources), sources[0].shape[1]
    slots = values.shape[0]
    used = jnp.arange(slots, dtype=jnp.int32) < count
    src_idx = jnp.where(used, src_idx, rows // TILE)
    anywhere = pl.BlockSpec(memory_space=pl.ANY)
    return pl.pallas_call(
        functools.partial(product_kernel, len(sources), len(out_rows), transpose),
        in_specs=[pl.BlockSpec(memory_space=pltpu.SMEM)] * 3 + [anywhere] * (1 + len(sources)),
        out_specs=[anywhere] * len(out_rows),
        scratch_shapes=[
            pltpu.VMEM(values.shape, BF),
            pltpu.VMEM((rows + TILE, width), BF),
            pltpu.VMEM((sum(out_rows), width), F32),
            pltpu.VMEM((sum(out_rows), width), BF),
            pltpu.SemaphoreType.DMA((len(sources),)),
            pltpu.SemaphoreType.DMA((slots // GROUP,)),
            pltpu.SemaphoreType.DMA((len(out_rows),)),
        ],
        out_shape=[jax.ShapeDtypeStruct((r, width), BF) for r in out_rows],
        compiler_params=pltpu.CompilerParams(vmem_limit_bytes=60 * 2**20),
        cost_estimate=pl.CostEstimate(
            flops=2 * slots * TILE * TILE * width,
            bytes_accessed=2 * values.size + 2 * (rows + sum(out_rows)) * width,
            transcendentals=0,
        ),
    )(count, src_idx, dst_idx, values, *sources)


def from_z(x, s):
    return lax.ppermute(x, "row", [(i, (i & 4) | ((i - s) & 3)) for i in range(8)])


def from_y(x, s):
    return lax.ppermute(x, "col", [(i, (i - 4 * s) & 15) for i in range(16)])


def swap(x, axis, bit):
    return lax.ppermute(x, axis, [(i, i ^ bit) for i in range(lax.axis_size(axis))])


def gather_across_first(x, far, axis, bit):
    near = jnp.concatenate([x, swap(x, axis, bit)], 0)
    return [near] + [far(near, s) for s in (1, 2, 3)]


def gather_along(x, far):
    return jnp.concatenate([x] + [far(x, s) for s in (1, 2, 3)], 0)


def send_along(parts, far):
    return {s: far(parts[s].astype(BF), -s) for s in (1, 3, 2)}


def end_across(own, got, axis, bit):
    total = own.astype(F32) + sum(g.astype(F32) for g in got.values())
    rows = total.shape[0] // 2
    across = swap(total[rows:].astype(BF), axis, bit)
    return total[:rows] + across.astype(F32)


def meet_across(own, across):
    total = own.astype(F32) + across.astype(F32)
    rows = total.shape[0] // 4
    return [total[s * rows : (s + 1) * rows] for s in range(4)]


def end_along(own, got):
    return own + sum(g.astype(F32) for g in got.values())


def with_rows(x, extra):
    return jnp.concatenate([x, jnp.broadcast_to(extra[None], (16, extra.shape[0]))], 0).astype(BF)


def halve(x, extra, axis, bit):
    half = x.shape[0] // 2
    side = (lax.axis_index(axis) // bit) & 1
    mine = lax.dynamic_slice_in_dim(x, side * half, half, 0)
    theirs = lax.dynamic_slice_in_dim(x, (1 - side) * half, half, 0)
    got = swap(with_rows(theirs, extra), axis, bit).astype(F32)
    return mine + got[:half], extra.astype(BF).astype(F32) + got[half]


def join(x, axis, bit):
    side = (lax.axis_index(axis) // bit) & 1
    x = x.astype(BF)
    other = swap(x, axis, bit)
    return jnp.concatenate([jnp.where(side == 0, x, other), jnp.where(side == 0, other, x)], 0)


def add_all(x, extra, far):
    rows = x.shape[0]
    sent = with_rows(x, extra)
    got = {s: far(sent, s).astype(F32) for s in (1, 2, 3)}
    total = (sent.astype(F32) + got[2]) + (got[1] + got[3])
    return total[:rows], total[rows]


def add_pair(x, extra, axis, bit):
    rows = x.shape[0]
    sent = with_rows(x, extra)
    total = sent.astype(F32) + swap(sent, axis, bit).astype(F32)
    return total[:rows], total[rows]


def place(block, side, along, across, sides):
    half, part = (block >> 1) & 1, block & 1
    order = jnp.where(half == 0, along * 2 + across, across * 4 + along)
    return ((half * sides + side) * 8 + order) * 2 + part


def body(features, weight, bias, cotangent, tile_values, tile_row, tile_col, tile_count):
    half = features.shape[0] // 2
    row, col = lax.axis_index("row"), lax.axis_index("col")
    dest = tile_row[0] >> 2
    row_idx = place(
        tile_row[0], (dest ^ col) & 1, ((dest >> 2) - (col >> 2)) & 3, ((dest ^ col) >> 1) & 1, 2
    )
    owner = tile_col[0] >> 2
    col_idx = place(tile_col[0], 0, (owner - row) & 3, ((owner ^ row) >> 2) & 1, 1)

    feats = gather_across_first(features[:half], from_z, "row", 4)
    near = gather_along(features[half:], from_z)
    near, feats[0] = lax.optimization_barrier((near, feats[0]))
    feats += [near, swap(near, "row", 4)]

    mine_0, theirs_0, mine_1, theirs_1 = product(
        tile_values, tile_count, col_idx, row_idx, feats, [8 * half] * 4, False
    )
    theirs_1 = swap(theirs_1, "col", 1)
    theirs_0 = swap(theirs_0, "col", 1)
    far_1 = mine_1[4 * half :].astype(F32) + theirs_1[4 * half :].astype(F32)
    far_1 = swap(far_1.astype(BF), "col", 2)
    both = mine_0.astype(F32) + theirs_0.astype(F32)
    parts = [both[s * 2 * half : (s + 1) * 2 * half] for s in range(4)]
    got = send_along(parts, from_y)
    parts_1 = meet_across(mine_1[: 4 * half].astype(F32) + theirs_1[: 4 * half].astype(F32), far_1)
    got_1 = send_along(parts_1, from_y)
    got[2], got_1[1] = lax.optimization_barrier((got[2], got_1[1]))
    sum_1 = end_along(parts_1[0], got_1)
    sum_0 = end_across(parts[0], got, "col", 2)

    def activation(total, rows):
        summed = total.astype(BF)
        summed_input = jnp.dot(summed, weight, preferred_element_type=F32) + bias[None, :]
        sigma = jax.nn.sigmoid(summed_input)
        output = (summed_input * sigma).astype(BF)
        grad = cotangent[rows].astype(F32) * sigma * (1.0 + summed_input * (1.0 - sigma))
        return summed, output, grad.astype(BF)

    summed_0, output_0, grad_0 = activation(sum_0, slice(0, half))
    pieces = gather_across_first(grad_0, from_y, "col", 2)
    summed_1, output_1, grad_1 = activation(sum_1, slice(half, 2 * half))
    near = gather_along(grad_1, from_y)

    grad_0, grad_1 = lax.optimization_barrier((grad_0, grad_1))
    grad_weight = sum(
        lax.dot_general(s, g, (((0,), (0,)), ((), ())), preferred_element_type=F32)
        for s, g in ((summed_0, grad_0), (summed_1, grad_1))
    )
    grad_bias = jnp.sum(grad_0.astype(F32), axis=0) + jnp.sum(grad_1.astype(F32), axis=0)
    grad_weight, grad_bias = halve(grad_weight, grad_bias, "col", 1)
    grad_weight, grad_bias = halve(grad_weight, grad_bias, "row", 4)

    near, grad_weight, pieces[0] = lax.optimization_barrier((near, grad_weight, pieces[0]))
    other = [near, swap(near, "col", 2)]
    grad_weight, other[1] = lax.optimization_barrier((grad_weight, other[1]))
    grad_weight, grad_bias = add_all(grad_weight, grad_bias, from_z)
    grads = pieces + [swap(p, "col", 1) for p in pieces]
    grads += other + [swap(p, "col", 1) for p in other]
    grads[0], grad_weight = lax.optimization_barrier((grads[0], grad_weight))

    *backs, near_1, far_1 = product(
        tile_values, tile_count, row_idx, col_idx, grads, [2 * half] * 4 + [4 * half] * 2, True
    )
    got = send_along(backs, from_z)
    far_1 = swap(far_1, "row", 4)
    grad_weight, got[1] = lax.optimization_barrier((grad_weight, got[1]))
    grad_weight, grad_bias = add_all(grad_weight, grad_bias, from_y)
    grad_weight, grad_bias = add_pair(grad_weight, grad_bias, "col", 2)
    grad_weight, far_1 = lax.optimization_barrier((grad_weight, far_1))
    parts_1 = meet_across(near_1, far_1)
    got_1 = send_along(parts_1, from_z)
    grad_weight = join(grad_weight, "row", 4)
    grad_weight, got_1[1], got_1[3] = lax.optimization_barrier((grad_weight, got_1[1], got_1[3]))
    grad_weight = join(grad_weight, "col", 1)
    back_1 = end_along(parts_1[0], got_1)
    back_0 = end_across(backs[0], got, "row", 4)
    grad_features = [
        lax.dot_general(
            b.astype(BF), weight, (((1,), (1,)), ((), ())), preferred_element_type=F32
        ).astype(BF)
        for b in (back_0, back_1)
    ]
    return (
        jnp.concatenate([output_0, output_1], 0),
        jnp.concatenate(grad_features, 0),
        grad_weight.astype(F32),
        grad_bias,
    )


def solution(mesh):
    in_specs = (
        P(("row", "col"), None),
        P(),
        P(),
        P(("row", "col"), None),
        P(("row", "col"), None, None),
        P(("row", "col"), None),
        P(("row", "col"), None),
        P(("row", "col")),
    )
    out_specs = (P(("row", "col"), None), P(("row", "col"), None), P(), P())
    return jax.shard_map(body, mesh=mesh, in_specs=in_specs, out_specs=out_specs, check_vma=False)
```

time: 288 us -> 265 us (0.920); the launches traced: 283 us -> 265 us
  starting transfers between devices: 108 us -> 47.3 us
  waiting for transfers between devices: 116 us -> 149 us
  Pallas kernels: 27.7 us -> 44 us
  other arithmetic: 19.1 us -> 13 us
    ppermute x20 -> x21, waiting for transfers between devices: 16.1 us -> 61.1 us  [swap(): lax.ppermute(x, axis, [(i, i ^ bit) for i in range(lax.axis_size(axis))])]
    ppermute x18 -> x15, waiting for transfers between devices: 53.5 us -> 24.8 us  [from_y(): return lax.ppermute(x, 'col', [(i, i - 4 * s & 15) for i in range(16)])]
    ppermute x18 -> x15, starting transfers between devices: 37.6 us -> 13.8 us  [from_z(): return lax.ppermute(x, 'row', [(i, i & 4 | i - s & 3) for i in range(8)])]
    ppermute x20 -> x21, starting transfers between devices: 46.6 us -> 24.6 us  [swap(): lax.ppermute(x, axis, [(i, i ^ bit) for i in range(lax.axis_size(axis))])]
    ppermute x18 -> x15, waiting for transfers between devices: 46.1 us -> 63.1 us  [from_z(): return lax.ppermute(x, 'row', [(i, i & 4 | i - s & 3) for i in range(8)])]
    pallas_call x2, Pallas kernels: 27.7 us -> 44 us  [product(): pl.pallas_call(functools.partial(product_kernel, len(sources), len(out_ro...]
    ppermute x18 -> x15, starting transfers between devices: 23.7 us -> 8.91 us  [from_y(): return lax.ppermute(x, 'col', [(i, i - 4 * s & 15) for i in range(16)])]
    another operation x8 -> x4, other arithmetic: 5.12 us -> 0.98 us
  transfers between devices with their start and end apart: 56 -> 51, of which waited for: 24 -> 28; matrix products, arithmetic and copies ran while one was open for 9% -> 6% of each run, Pallas kernels for 0% -> 0%
where the time goes in v3:
time: 265 us
  waiting for transfers between devices  149 us (56%)
  starting transfers between devices  47.3 us (18%)
  Pallas kernels  44 us (17%)
  other arithmetic  13 us (5%)
  local copies, waits for them, and re-layouts  7.31 us (3%)
    ppermute x15, waiting for transfers between devices, from_z(): return lax.ppermute(x, 'row', [(i, i & 4 | i - s & 3) for i in range(8)])  63.1 us
    ppermute x21, waiting for transfers between devices, swap(): lax.ppermute(x, axis, [(i, i ^ bit) for i in range(lax.axis_size(axis))])  61.1 us
    pallas_call x2, Pallas kernels, product(): pl.pallas_call(functools.partial(product_kernel, len(sources), len(out_ro...  44 us
    ppermute x15, waiting for transfers between devices, from_y(): return lax.ppermute(x, 'col', [(i, i - 4 * s & 15) for i in range(16)])  24.8 us
    ppermute x21, starting transfers between devices, swap(): lax.ppermute(x, axis, [(i, i ^ bit) for i in range(lax.axis_size(axis))])  24.6 us
    ppermute x15, starting transfers between devices, from_z(): return lax.ppermute(x, 'row', [(i, i & 4 | i - s & 3) for i in range(8)])  13.8 us
    ppermute x15, starting transfers between devices, from_y(): return lax.ppermute(x, 'col', [(i, i - 4 * s & 15) for i in range(16)])  8.91 us
  transfers between devices with their start and end apart: 51, of which 28 were waited for; matrix products, arithmetic and copies ran while one was open for 6% of the time, Pallas kernels for 0%

profile of v3, /device:TPU:1, one launch (start us, length us, event | category | flops | bytes accessed | tf_op | source)
XLA Modules:
  0.0 264.8 jit_solution(14382359182083489521)
XLA Ops:
  1.8 3.7 %collective-permute-start.3 = (bf16[256,512]{1,0:T(8,128)(2,1)S(1)}, bf16[256,512]{1,0:T(8,128)(2,1)S(1)}, u32[]{:S(2)}, u32[]{:S(2)}) collective-permute-start(bf16[256,512]{1,0:T(8,128)(2,1)S(1)} %get-tuple-element.99), channel_id=1, source_target_pairs={{0,64},{16,80},{32,96},{48,112},{64,0},{80,16},{96,32},{112,48},{1... | collective-permute-start | bytes 786440 | tf_op jit(solution)/shard_map/ppermute | solution.py:107
  5.4 3.8 %collective-permute-start = (bf16[256,512]{1,0:T(8,128)(2,1)S(1)}, bf16[256,512]{1,0:T(8,128)(2,1)S(1)}, u32[]{:S(2)}, u32[]{:S(2)}) collective-permute-start(bf16[256,512]{1,0:T(8,128)(2,1)S(1)} %get-tuple-element.100), channel_id=1, source_target_pairs={{0,48},{16,0},{32,16},{48,32},{64,112},{80,64},{96,80},{112,96},{1... | collective-permute-start | bytes 786440 | tf_op jit(solution)/shard_map/ppermute | solution.py:99
  11.0 8.3 %collective-permute-done = bf16[256,512]{1,0:T(8,128)(2,1)S(1)} collective-permute-done((bf16[256,512]{1,0:T(8,128)(2,1)S(1)}, bf16[256,512]{1,0:T(8,128)(2,1)S(1)}, u32[]{:S(2)}, u32[]{:S(2)}) %collective-permute-start) | collective-permute-done | bytes 262176 | tf_op jit(solution)/shard_map/ppermute | solution.py:99
  19.3 4.6 %collective-permute-done.2 = bf16[256,512]{1,0:T(8,128)(2,1)S(1)} collective-permute-done((bf16[256,512]{1,0:T(8,128)(2,1)S(1)}, bf16[256,512]{1,0:T(8,128)(2,1)S(1)}, u32[]{:S(2)}, u32[]{:S(2)}) %collective-permute-start.2) | collective-permute-done | bytes 262176 | tf_op jit(solution)/shard_map/ppermute | solution.py:99
  27.3 10.1 %collective-permute-done.4.refs_1_ = bf16[512,512]{1,0:T(8,128)(2,1)S(1)} collective-permute-done((bf16[512,512]{1,0:T(8,128)(2,1)S(1)}, bf16[512,512]{1,0:T(8,128)(2,1)S(1)}, u32[]{:S(2)}, u32[]{:S(2)}) %collective-permute-start.4) | collective-permute-done | bytes 524320 | tf_op jit(solution)/shard_map/ppermute | solution.py:99
  38.2 13.5 %collective-permute-done.6.refs_3_ = bf16[512,512]{1,0:T(8,128)(2,1)S(1)} collective-permute-done((bf16[512,512]{1,0:T(8,128)(2,1)S(1)}, bf16[512,512]{1,0:T(8,128)(2,1)S(1)}, u32[]{:S(2)}, u32[]{:S(2)}) %collective-permute-start.6) | collective-permute-done | bytes 524320 | tf_op jit(solution)/shard_map/ppermute | solution.py:99
  52.9 21.8 %shard_map.111 = (bf16[2048,512]{1,0:T(8,128)(2,1)}, bf16[2048,512]{1,0:T(8,128)(2,1)}, bf16[2048,512]{1,0:T(8,128)(2,1)}, bf16[2048,512]{1,0:T(8,128)(2,1)}) custom-call(s32[1]{0:T(128)} %copy.12.count_ref, s32[384]{0:T(512)} %get-tuple-element.103.src_idx, s32[384]{0:T(512)} %get-tuple-element.73.dst_idx, bf16[384,128,128]{2,1,0:T(8,128)(2,1)} %values.3, ...), custom_call_target="tpu_custom_call" | custom-call | flops 6442450944 | bytes 25165824 | tf_op jit(solution)/shard_map/pallas_call | solution.py:75
  75.3 3.9 %collective-permute-done.12 = bf16[2048,512]{1,0:T(8,128)(2,1)S(1)} collective-permute-done((bf16[2048,512]{1,0:T(8,128)(2,1)}, bf16[2048,512]{1,0:T(8,128)(2,1)S(1)}, u32[]{:S(2)}, u32[]{:S(2)}) %collective-permute-start.12) | collective-permute-done | bytes 2097184 | tf_op jit(solution)/shard_map/ppermute | solution.py:107
  79.2 1.5 add_convert_fusion
  80.8 1.4 collective-permute-done.8
  82.2 2.9 %convert_add_fusion = (f32[2048,512]{1,0:T(8,128)}, bf16[2048,512]{1,0:T(8,128)(2,1)S(1)}) fusion(bf16[2048,512]{1,0:T(8,128)(2,1)S(1)} %collective-permute-done.8, bf16[2048,512]{1,0:T(8,128)(2,1)S(1)} %copy-done.1), kind=kLoop, calls=%fused_computation | loop fusion | flops 4194304 | bytes 10485760 | tf_op jit(solution)/shard_map/add | solution.py:203
  85.1 1.2 fusion.20
  86.2 1.5 collective-permute-start.9
  87.7 17.8 %collective-permute-done.13 = bf16[1024,512]{1,0:T(8,128)(2,1)S(1)} collective-permute-done((bf16[1024,512]{1,0:T(8,128)(2,1)S(1)}, bf16[1024,512]{1,0:T(8,128)(2,1)S(1)}, u32[]{:S(2)}, u32[]{:S(2)}) %collective-permute-start.13) | collective-permute-done | bytes 1048608 | tf_op jit(solution)/shard_map/ppermute | solution.py:107
  107.0 2.7 %collective-permute-start.16 = (bf16[256,512]{1,0:T(8,128)(2,1)}, bf16[256,512]{1,0:T(8,128)(2,1)S(1)}, u32[]{:S(2)}, u32[]{:S(2)}) collective-permute-start(bf16[256,512]{1,0:T(8,128)(2,1)} %get-tuple-element.92), channel_id=1, source_target_pairs={{0,12},{1,13},{2,14},{3,15},{4,0},{5,1},{6,2},{7,3},{8,4},{9,5},{1... | collective-permute-start | bytes 786440 | tf_op jit(solution)/shard_map/ppermute | solution.py:103
  109.7 9.4 %collective-permute-done.14 = bf16[256,512]{1,0:T(8,128)(2,1)S(1)} collective-permute-done((bf16[256,512]{1,0:T(8,128)(2,1)}, bf16[256,512]{1,0:T(8,128)(2,1)S(1)}, u32[]{:S(2)}, u32[]{:S(2)}) %collective-permute-start.14) | collective-permute-done | bytes 262176 | tf_op jit(solution)/shard_map/ppermute | solution.py:103
  119.1 1.8 slice_add_fusion
  121.6 2.3 collective-permute-done.17
  124.0 4.5 %collective-permute-done.15 = bf16[256,512]{1,0:T(8,128)(2,1)S(1)} collective-permute-done((bf16[256,512]{1,0:T(8,128)(2,1)S(1)}, bf16[256,512]{1,0:T(8,128)(2,1)S(1)}, u32[]{:S(2)}, u32[]{:S(2)}) %collective-permute-start.15) | collective-permute-done | bytes 262176 | tf_op jit(solution)/shard_map/ppermute | solution.py:107
  130.4 1.5 collective-permute-start.21
  132.3 1.5 collective-permute-start.20
  134.2 5.6 %collective-permute-done.23 = bf16[256,512]{1,0:T(8,128)(2,1)S(1)} collective-permute-done((bf16[256,512]{1,0:T(8,128)(2,1)S(1)}, bf16[256,512]{1,0:T(8,128)(2,1)S(1)}, u32[]{:S(2)}, u32[]{:S(2)}) %collective-permute-start.23) | collective-permute-done | bytes 262176 | tf_op jit(solution)/shard_map/ppermute | solution.py:107
  139.8 1.6 collective-permute-done.19
  141.4 6.3 %collective-permute-done.20 = bf16[256,512]{1,0:T(8,128)(2,1)S(1)} collective-permute-done((bf16[256,512]{1,0:T(8,128)(2,1)S(1)}, bf16[256,512]{1,0:T(8,128)(2,1)S(1)}, u32[]{:S(2)}, u32[]{:S(2)}) %collective-permute-start.20) | collective-permute-done | bytes 262176 | tf_op jit(solution)/shard_map/ppermute | solution.py:103
  147.8 1.2 collective-permute-start.24
  149.2 1.3 collective-permute-start.30
  150.5 1.3 collective-permute-start.31
  151.8 20.3 %collective-permute-done.24.refs_9_ = bf16[1024,512]{1,0:T(8,128)(2,1)S(1)} collective-permute-done((bf16[1024,512]{1,0:T(8,128)(2,1)S(1)}, bf16[1024,512]{1,0:T(8,128)(2,1)S(1)}, u32[]{:S(2)}, u32[]{:S(2)}) %collective-permute-start.24) | collective-permute-done | bytes 1048608 | tf_op jit(solution)/shard_map/ppermute | solution.py:107
  172.2 1.3 collective-permute-start.35
  173.8 2.0 collective-permute-done.30.refs_3_
  175.8 1.5 collective-permute-start.27
  177.3 3.0 %collective-permute-done.25 = bf16[144,512]{1,0:T(8,128)(2,1)S(1)} collective-permute-done((bf16[144,512]{1,0:T(8,128)(2,1)S(1)}, bf16[144,512]{1,0:T(8,128)(2,1)S(1)}, u32[]{:S(2)}, u32[]{:S(2)}) %collective-permute-start.25) | collective-permute-done | bytes 147488 | tf_op jit(solution)/shard_map/ppermute | solution.py:99
  180.3 2.1 collective-permute-start.32
  182.4 1.7 collective-permute-done.27
  184.8 1.4 collective-permute-done.34.refs_7_
  188.2 22.2 %shard_map.112 = (bf16[512,512]{1,0:T(8,128)(2,1)}, bf16[512,512]{1,0:T(8,128)(2,1)}, bf16[512,512]{1,0:T(8,128)(2,1)}, bf16[512,512]{1,0:T(8,128)(2,1)}, bf16[1...) custom-call(s32[1]{0:T(128)} %copy.12.count_ref, s32[384]{0:T(512)} %get-tuple-element.72.src_idx, ...), custom_call_target="tpu_custom_call" | custom-call | flops 6442450944 | bytes 25165824 | tf_op jit(solution)/shard_map/pallas_call | solution.py:75
  210.5 2.7 %collective-permute-start.38 = (bf16[512,512]{1,0:T(8,128)(2,1)}, bf16[512,512]{1,0:T(8,128)(2,1)S(1)}, u32[]{:S(2)}, u32[]{:S(2)}) collective-permute-start(bf16[512,512]{1,0:T(8,128)(2,1)} %get-tuple-element.54), channel_id=1, source_target_pairs={{0,48},{16,0},{32,16},{48,32},{64,112},{80,64},{96,80},{112,96},{1... | collective-permute-start | bytes 1572872 | tf_op jit(solution)/shard_map/ppermute | solution.py:99
  214.1 17.4 %collective-permute-done.37 = bf16[512,512]{1,0:T(8,128)(2,1)S(1)} collective-permute-done((bf16[512,512]{1,0:T(8,128)(2,1)}, bf16[512,512]{1,0:T(8,128)(2,1)S(1)}, u32[]{:S(2)}, u32[]{:S(2)}) %collective-permute-start.37) | collective-permute-done | bytes 524320 | tf_op jit(solution)/shard_map/ppermute | solution.py:99
  231.9 1.4 collective-permute-start.43
  233.3 1.3 add_add_fusion
  234.7 1.3 collective-permute-start.40
  236.0 1.9 collective-permute-done.41
  237.9 1.4 collective-permute-done.43
  240.0 4.2 %collective-permute-done.40 = bf16[256,512]{1,0:T(8,128)(2,1)S(1)} collective-permute-done((bf16[256,512]{1,0:T(8,128)(2,1)S(1)}, bf16[256,512]{1,0:T(8,128)(2,1)S(1)}, u32[]{:S(2)}, u32[]{:S(2)}) %collective-permute-start.40) | collective-permute-done | bytes 262176 | tf_op jit(solution)/shard_map/ppermute | solution.py:107
  245.7 1.4 collective-permute-start.46
  247.7 2.7 %collective-permute-start.48 = (bf16[256,512]{1,0:T(8,128)(2,1)S(1)}, bf16[256,512]{1,0:T(8,128)(2,1)S(1)}, u32[]{:S(2)}, u32[]{:S(2)}) collective-permute-start(bf16[256,512]{1,0:T(8,128)(2,1)S(1)} %get-tuple-element.87), channel_id=1, source_target_pairs={{0,48},{16,0},{32,16},{48,32},{64,112},{80,64},{96,80},{112,96},{1... | collective-permute-start | bytes 786440 | tf_op jit(solution)/shard_map/ppermute | solution.py:99
  251.6 3.2 %collective-permute-done.47 = bf16[256,512]{1,0:T(8,128)(2,1)S(1)} collective-permute-done((bf16[256,512]{1,0:T(8,128)(2,1)S(1)}, bf16[256,512]{1,0:T(8,128)(2,1)S(1)}, u32[]{:S(2)}, u32[]{:S(2)}) %collective-permute-start.47) | collective-permute-done | bytes 262176 | tf_op jit(solution)/shard_map/ppermute | solution.py:99
  255.3 7.2 %collective-permute-start.50 = (bf16[256,512]{1,0:T(8,128)(2,1)S(1)}, bf16[256,512]{1,0:T(8,128)(2,1)S(1)}, u32[]{:S(2)}, u32[]{:S(2)}) collective-permute-start(bf16[256,512]{1,0:T(8,128)(2,1)S(1)} %pad_maximum_fusion.7), channel_id=1, source_target_pairs={{0,1},{1,0},{2,3},{3,2},{4,5},{5,4},{6,7},{7,6},{8,9},{9,8},{10,11... | collective-permute-start | bytes 786440 | tf_op jit(solution)/shard_map/ppermute | solution.py:107
  (172 shorter events, 24.8 us)
Async XLA Ops:
  1.8 9.2 %collective-permute-start.3 = (bf16[256,512]{1,0:T(8,128)(2,1)S(1)}, bf16[256,512]{1,0:T(8,128)(2,1)S(1)}, u32[]{:S(2)}, u32[]{:S(2)}) collective-permute-start(bf16[256,512]{1,0:T(8,128)(2,1)S(1)} %get-tuple-element.99), channel_id=1, source_target_pairs={{0,64},{16,80},{32,96},{48,112},{64,0},{80,16},{96,32},{112,48},{1... | collective-permute-start | bytes 786440 | tf_op jit(solution)/shard_map/ppermute | solution.py:107
  5.4 13.9 %collective-permute-start = (bf16[256,512]{1,0:T(8,128)(2,1)S(1)}, bf16[256,512]{1,0:T(8,128)(2,1)S(1)}, u32[]{:S(2)}, u32[]{:S(2)}) collective-permute-start(bf16[256,512]{1,0:T(8,128)(2,1)S(1)} %get-tuple-element.100), channel_id=1, source_target_pairs={{0,48},{16,0},{32,16},{48,32},{64,112},{80,64},{96,80},{112,96},{1... | collective-permute-start | bytes 786440 | tf_op jit(solution)/shard_map/ppermute | solution.py:99
  9.2 10.1 %collective-permute-start.1 = (bf16[256,512]{1,0:T(8,128)(2,1)S(1)}, bf16[256,512]{1,0:T(8,128)(2,1)S(1)}, u32[]{:S(2)}, u32[]{:S(2)}) collective-permute-start(bf16[256,512]{1,0:T(8,128)(2,1)S(1)} %get-tuple-element.100), channel_id=1, source_target_pairs={{0,32},{16,48},{32,0},{48,16},{64,96},{80,112},{96,64},{112,80},{1... | collective-permute-start | bytes 786440 | tf_op jit(solution)/shard_map/ppermute | solution.py:99
  9.2 14.7 %collective-permute-start.2 = (bf16[256,512]{1,0:T(8,128)(2,1)S(1)}, bf16[256,512]{1,0:T(8,128)(2,1)S(1)}, u32[]{:S(2)}, u32[]{:S(2)}) collective-permute-start(bf16[256,512]{1,0:T(8,128)(2,1)S(1)} %get-tuple-element.100), channel_id=1, source_target_pairs={{0,16},{16,32},{32,48},{48,0},{64,80},{80,96},{96,112},{112,64},{1... | collective-permute-start | bytes 786440 | tf_op jit(solution)/shard_map/ppermute | solution.py:99
  24.0 27.8 %collective-permute-start.7 = (bf16[1024,512]{1,0:T(8,128)(2,1)S(1)}, bf16[1024,512]{1,0:T(8,128)(2,1)S(1)}, u32[]{:S(2)}, u32[]{:S(2)}) collective-permute-start(bf16[1024,512]{1,0:T(8,128)(2,1)S(1)} %pad_maximum_fusion.refs_4_), channel_id=1, source_target_pairs={{0,64},{16,80},{32,96},{48,112},{64,0},{80,16},{96,32},{112,48},{1... | collective-permute-start | bytes 3145736 | tf_op jit(solution)/shard_map/ppermute | solution.py:107
  25.0 12.4 %collective-permute-start.4 = (bf16[512,512]{1,0:T(8,128)(2,1)S(1)}, bf16[512,512]{1,0:T(8,128)(2,1)S(1)}, u32[]{:S(2)}, u32[]{:S(2)}) collective-permute-start(bf16[512,512]{1,0:T(8,128)(2,1)S(1)} %pad_maximum_fusion.2.refs_0_), channel_id=1, source_target_pairs={{0,48},{16,0},{32,16},{48,32},{64,112},{80,64},{96,80},{112,96},{1... | collective-permute-start | bytes 1572872 | tf_op jit(solution)/shard_map/ppermute | solution.py:99
  25.1 13.2 %collective-permute-start.5 = (bf16[512,512]{1,0:T(8,128)(2,1)S(1)}, bf16[512,512]{1,0:T(8,128)(2,1)S(1)}, u32[]{:S(2)}, u32[]{:S(2)}) collective-permute-start(bf16[512,512]{1,0:T(8,128)(2,1)S(1)} %pad_maximum_fusion.2.refs_0_), channel_id=1, source_target_pairs={{0,32},{16,48},{32,0},{48,16},{64,96},{80,112},{96,64},{112,80},{1... | collective-permute-start | bytes 1572872 | tf_op jit(solution)/shard_map/ppermute | solution.py:99
  25.8 25.9 %collective-permute-start.6 = (bf16[512,512]{1,0:T(8,128)(2,1)S(1)}, bf16[512,512]{1,0:T(8,128)(2,1)S(1)}, u32[]{:S(2)}, u32[]{:S(2)}) collective-permute-start(bf16[512,512]{1,0:T(8,128)(2,1)S(1)} %pad_maximum_fusion.2.refs_0_), channel_id=1, source_target_pairs={{0,16},{16,32},{32,48},{48,0},{64,80},{80,96},{96,112},{112,64},{1... | collective-permute-start | bytes 1572872 | tf_op jit(solution)/shard_map/ppermute | solution.py:99
  74.7 4.5 %collective-permute-start.12 = (bf16[2048,512]{1,0:T(8,128)(2,1)}, bf16[2048,512]{1,0:T(8,128)(2,1)S(1)}, u32[]{:S(2)}, u32[]{:S(2)}) collective-permute-start(bf16[2048,512]{1,0:T(8,128)(2,1)} %get-tuple-element.39), channel_id=1, source_target_pairs={{0,1},{1,0},{2,3},{3,2},{4,5},{5,4},{6,7},{7,6},{8,9},{9,8},{10,11... | collective-permute-start | bytes 6291464 | tf_op jit(solution)/shard_map/ppermute | solution.py:107
  74.8 7.4 %collective-permute-start.8 = (bf16[2048,512]{1,0:T(8,128)(2,1)}, bf16[2048,512]{1,0:T(8,128)(2,1)S(1)}, u32[]{:S(2)}, u32[]{:S(2)}) collective-permute-start(bf16[2048,512]{1,0:T(8,128)(2,1)} %get-tuple-element.37), channel_id=1, source_target_pairs={{0,1},{1,0},{2,3},{3,2},{4,5},{5,4},{6,7},{7,6},{8,9},{9,8},{10,11... | collective-permute-start | bytes 6291464 | tf_op jit(solution)/shard_map/ppermute | solution.py:107
  80.7 24.8 %collective-permute-start.13 = (bf16[1024,512]{1,0:T(8,128)(2,1)S(1)}, bf16[1024,512]{1,0:T(8,128)(2,1)S(1)}, u32[]{:S(2)}, u32[]{:S(2)}) collective-permute-start(bf16[1024,512]{1,0:T(8,128)(2,1)S(1)} %add_convert_fusion), channel_id=1, source_target_pairs={{0,2},{1,3},{2,0},{3,1},{4,6},{5,7},{6,4},{7,5},{8,10},{9,11},{10,... | collective-permute-start | bytes 3145736 | tf_op jit(solution)/shard_map/ppermute | solution.py:107
  86.2 23.5 %collective-permute-start.11 = (bf16[512,512]{1,0:T(8,128)(2,1)}, bf16[512,512]{1,0:T(8,128)(2,1)S(1)}, u32[]{:S(2)}, u32[]{:S(2)}) collective-permute-start(bf16[512,512]{1,0:T(8,128)(2,1)} %get-tuple-element.85), channel_id=1, source_target_pairs={{0,8},{1,9},{2,10},{3,11},{4,12},{5,13},{6,14},{7,15},{8,0},{9,1},... | collective-permute-start | bytes 1572872 | tf_op jit(solution)/shard_map/ppermute | solution.py:103
  86.2 32.8 %collective-permute-start.10 = (bf16[512,512]{1,0:T(8,128)(2,1)}, bf16[512,512]{1,0:T(8,128)(2,1)}, u32[]{:S(2)}, u32[]{:S(2)}) collective-permute-start(bf16[512,512]{1,0:T(8,128)(2,1)} %get-tuple-element.86), channel_id=1, source_target_pairs={{0,12},{1,13},{2,14},{3,15},{4,0},{5,1},{6,2},{7,3},{8,4},{9,5},{1... | collective-permute-start | bytes 1572872 | tf_op jit(solution)/shard_map/ppermute | solution.py:103
  86.2 32.8 %collective-permute-start.9 = (bf16[512,512]{1,0:T(8,128)(2,1)}, bf16[512,512]{1,0:T(8,128)(2,1)}, u32[]{:S(2)}, u32[]{:S(2)}) collective-permute-start(bf16[512,512]{1,0:T(8,128)(2,1)} %get-tuple-element.84), channel_id=1, source_target_pairs={{0,4},{1,5},{2,6},{3,7},{4,8},{5,9},{6,10},{7,11},{8,12},{9,13},{1... | collective-permute-start | bytes 1572872 | tf_op jit(solution)/shard_map/ppermute | solution.py:103
  107.0 12.1 %collective-permute-start.14 = (bf16[256,512]{1,0:T(8,128)(2,1)}, bf16[256,512]{1,0:T(8,128)(2,1)S(1)}, u32[]{:S(2)}, u32[]{:S(2)}) collective-permute-start(bf16[256,512]{1,0:T(8,128)(2,1)} %get-tuple-element.90), channel_id=1, source_target_pairs={{0,4},{1,5},{2,6},{3,7},{4,8},{5,9},{6,10},{7,11},{8,12},{9,13},{1... | collective-permute-start | bytes 786440 | tf_op jit(solution)/shard_map/ppermute | solution.py:103
  107.0 14.6 %collective-permute-start.16 = (bf16[256,512]{1,0:T(8,128)(2,1)}, bf16[256,512]{1,0:T(8,128)(2,1)S(1)}, u32[]{:S(2)}, u32[]{:S(2)}) collective-permute-start(bf16[256,512]{1,0:T(8,128)(2,1)} %get-tuple-element.92), channel_id=1, source_target_pairs={{0,12},{1,13},{2,14},{3,15},{4,0},{5,1},{6,2},{7,3},{8,4},{9,5},{1... | collective-permute-start | bytes 786440 | tf_op jit(solution)/shard_map/ppermute | solution.py:103
  109.7 14.2 %collective-permute-start.17 = (bf16[256,512]{1,0:T(8,128)(2,1)}, bf16[256,512]{1,0:T(8,128)(2,1)S(1)}, u32[]{:S(2)}, u32[]{:S(2)}) collective-permute-start(bf16[256,512]{1,0:T(8,128)(2,1)} %get-tuple-element.91), channel_id=1, source_target_pairs={{0,8},{1,9},{2,10},{3,11},{4,12},{5,13},{6,14},{7,15},{8,0},{9,1},... | collective-permute-start | bytes 786440 | tf_op jit(solution)/shard_map/ppermute | solution.py:103
  120.9 7.6 %collective-permute-start.15 = (bf16[256,512]{1,0:T(8,128)(2,1)S(1)}, bf16[256,512]{1,0:T(8,128)(2,1)S(1)}, u32[]{:S(2)}, u32[]{:S(2)}) collective-permute-start(bf16[256,512]{1,0:T(8,128)(2,1)S(1)} %slice.223), channel_id=1, source_target_pairs={{0,2},{1,3},{2,0},{3,1},{4,6},{5,7},{6,4},{7,5},{8,10},{9,11},{10,... | collective-permute-start | bytes 786440 | tf_op jit(solution)/shard_map/ppermute | solution.py:107
  131.9 7.9 %collective-permute-start.23 = (bf16[256,512]{1,0:T(8,128)(2,1)S(1)}, bf16[256,512]{1,0:T(8,128)(2,1)S(1)}, u32[]{:S(2)}, u32[]{:S(2)}) collective-permute-start(bf16[256,512]{1,0:T(8,128)(2,1)S(1)} %get-tuple-element.42), channel_id=1, source_target_pairs={{0,2},{1,3},{2,0},{3,1},{4,6},{5,7},{6,4},{7,5},{8,10},{9,11},{10,... | collective-permute-start | bytes 786440 | tf_op jit(solution)/shard_map/ppermute | solution.py:107
  132.3 7.5 %collective-permute-start.18 = (bf16[256,512]{1,0:T(8,128)(2,1)S(1)}, bf16[256,512]{1,0:T(8,128)(2,1)S(1)}, u32[]{:S(2)}, u32[]{:S(2)}) collective-permute-start(bf16[256,512]{1,0:T(8,128)(2,1)S(1)} %get-tuple-element.43), channel_id=1, source_target_pairs={{0,12},{1,13},{2,14},{3,15},{4,0},{5,1},{6,2},{7,3},{8,4},{9,5},{1... | collective-permute-start | bytes 786440 | tf_op jit(solution)/shard_map/ppermute | solution.py:103
  132.3 9.1 %collective-permute-start.19 = (bf16[256,512]{1,0:T(8,128)(2,1)S(1)}, bf16[256,512]{1,0:T(8,128)(2,1)S(1)}, u32[]{:S(2)}, u32[]{:S(2)}) collective-permute-start(bf16[256,512]{1,0:T(8,128)(2,1)S(1)} %get-tuple-element.43), channel_id=1, source_target_pairs={{0,8},{1,9},{2,10},{3,11},{4,12},{5,13},{6,14},{7,15},{8,0},{9,1},... | collective-permute-start | bytes 786440 | tf_op jit(solution)/shard_map/ppermute | solution.py:103
  132.3 15.3 %collective-permute-start.20 = (bf16[256,512]{1,0:T(8,128)(2,1)S(1)}, bf16[256,512]{1,0:T(8,128)(2,1)S(1)}, u32[]{:S(2)}, u32[]{:S(2)}) collective-permute-start(bf16[256,512]{1,0:T(8,128)(2,1)S(1)} %get-tuple-element.43), channel_id=1, source_target_pairs={{0,4},{1,5},{2,6},{3,7},{4,8},{5,9},{6,10},{7,11},{8,12},{9,13},{1... | collective-permute-start | bytes 786440 | tf_op jit(solution)/shard_map/ppermute | solution.py:103
  134.0 13.7 %collective-permute-start.22 = (bf16[144,512]{1,0:T(8,128)(2,1)S(1)}, bf16[144,512]{1,0:T(8,128)(2,1)S(1)}, u32[]{:S(2)}, u32[]{:S(2)}) collective-permute-start(bf16[144,512]{1,0:T(8,128)(2,1)S(1)} %pad_maximum_fusion.8), channel_id=1, source_target_pairs={{0,64},{16,80},{32,96},{48,112},{64,0},{80,16},{96,32},{112,48},{1... | collective-permute-start | bytes 442376 | tf_op jit(solution)/shard_map/ppermute | solution.py:107
  147.8 24.3 %collective-permute-start.24 = (bf16[1024,512]{1,0:T(8,128)(2,1)S(1)}, bf16[1024,512]{1,0:T(8,128)(2,1)S(1)}, u32[]{:S(2)}, u32[]{:S(2)}) collective-permute-start(bf16[1024,512]{1,0:T(8,128)(2,1)S(1)} %pad_maximum_fusion.1.refs_8_), channel_id=1, source_target_pairs={{0,2},{1,3},{2,0},{3,1},{4,6},{5,7},{6,4},{7,5},{8,10},{9,11},{10,... | collective-permute-start | bytes 3145736 | tf_op jit(solution)/shard_map/ppermute | solution.py:107
  149.0 24.5 %collective-permute-start.28 = (bf16[512,512]{1,0:T(8,128)(2,1)S(1)}, bf16[512,512]{1,0:T(8,128)(2,1)S(1)}, u32[]{:S(2)}, u32[]{:S(2)}) collective-permute-start(bf16[512,512]{1,0:T(8,128)(2,1)S(1)} %pad_maximum_fusion.4.refs_0_), channel_id=1, source_target_pairs={{0,12},{1,13},{2,14},{3,15},{4,0},{5,1},{6,2},{7,3},{8,4},{9,5},{1... | collective-permute-start | bytes 1572872 | tf_op jit(solution)/shard_map/ppermute | solution.py:103
  149.2 24.4 %collective-permute-start.29 = (bf16[512,512]{1,0:T(8,128)(2,1)S(1)}, bf16[512,512]{1,0:T(8,128)(2,1)S(1)}, u32[]{:S(2)}, u32[]{:S(2)}) collective-permute-start(bf16[512,512]{1,0:T(8,128)(2,1)S(1)} %pad_maximum_fusion.4.refs_0_), channel_id=1, source_target_pairs={{0,8},{1,9},{2,10},{3,11},{4,12},{5,13},{6,14},{7,15},{8,0},{9,1},... | collective-permute-start | bytes 1572872 | tf_op jit(solution)/shard_map/ppermute | solution.py:103
  149.2 26.6 %collective-permute-start.30 = (bf16[512,512]{1,0:T(8,128)(2,1)S(1)}, bf16[512,512]{1,0:T(8,128)(2,1)S(1)}, u32[]{:S(2)}, u32[]{:S(2)}) collective-permute-start(bf16[512,512]{1,0:T(8,128)(2,1)S(1)} %pad_maximum_fusion.4.refs_0_), channel_id=1, source_target_pairs={{0,4},{1,5},{2,6},{3,7},{4,8},{5,9},{6,10},{7,11},{8,12},{9,13},{1... | collective-permute-start | bytes 1572872 | tf_op jit(solution)/shard_map/ppermute | solution.py:103
  150.5 25.3 %collective-permute-start.31 = (bf16[512,512]{1,0:T(8,128)(2,1)S(1)}, bf16[512,512]{1,0:T(8,128)(2,1)S(1)}, u32[]{:S(2)}, u32[]{:S(2)}) collective-permute-start(bf16[512,512]{1,0:T(8,128)(2,1)S(1)} %pad_maximum_fusion.4.refs_0_), channel_id=1, source_target_pairs={{0,1},{1,0},{2,3},{3,2},{4,5},{5,4},{6,7},{7,6},{8,9},{9,8},{10,11... | collective-permute-start | bytes 1572872 | tf_op jit(solution)/shard_map/ppermute | solution.py:107
  172.2 14.1 %collective-permute-start.35 = (bf16[1024,512]{1,0:T(8,128)(2,1)S(1)}, bf16[1024,512]{1,0:T(8,128)(2,1)S(1)}, u32[]{:S(2)}, u32[]{:S(2)}) collective-permute-start(bf16[1024,512]{1,0:T(8,128)(2,1)S(1)} %pad_maximum_fusion.1.refs_8_), channel_id=1, source_target_pairs={{0,1},{1,0},{2,3},{3,2},{4,5},{5,4},{6,7},{7,6},{8,9},{9,8},{10,11... | collective-permute-start | bytes 3145736 | tf_op jit(solution)/shard_map/ppermute | solution.py:107
  173.5 12.7 %collective-permute-start.36 = (bf16[1024,512]{1,0:T(8,128)(2,1)S(1)}, bf16[1024,512]{1,0:T(8,128)(2,1)S(1)}, u32[]{:S(2)}, u32[]{:S(2)}) collective-permute-start(bf16[1024,512]{1,0:T(8,128)(2,1)S(1)} %collective-permute-done.24.refs_9_), channel_id=1, source_target_pairs={{0,1},{1,0},{2,3},{3,2},{4,5},{5,4},{6,7},{7,6},{8,9},{9,8},{10,11... | collective-permute-start | bytes 3145736 | tf_op jit(solution)/shard_map/ppermute | solution.py:107
  173.7 6.6 %collective-permute-start.25 = (bf16[144,512]{1,0:T(8,128)(2,1)S(1)}, bf16[144,512]{1,0:T(8,128)(2,1)S(1)}, u32[]{:S(2)}, u32[]{:S(2)}) collective-permute-start(bf16[144,512]{1,0:T(8,128)(2,1)S(1)} %pad_maximum_fusion.9), channel_id=1, source_target_pairs={{0,32},{16,48},{32,0},{48,16},{64,96},{80,112},{96,64},{112,80},{1... | collective-permute-start | bytes 442376 | tf_op jit(solution)/shard_map/ppermute | solution.py:99
  175.8 6.6 %collective-permute-start.26 = (bf16[144,512]{1,0:T(8,128)(2,1)S(1)}, bf16[144,512]{1,0:T(8,128)(2,1)S(1)}, u32[]{:S(2)}, u32[]{:S(2)}) collective-permute-start(bf16[144,512]{1,0:T(8,128)(2,1)S(1)} %pad_maximum_fusion.9), channel_id=1, source_target_pairs={{0,48},{16,0},{32,16},{48,32},{64,112},{80,64},{96,80},{112,96},{1... | collective-permute-start | bytes 442376 | tf_op jit(solution)/shard_map/ppermute | solution.py:99
  175.8 8.2 %collective-permute-start.27 = (bf16[144,512]{1,0:T(8,128)(2,1)S(1)}, bf16[144,512]{1,0:T(8,128)(2,1)S(1)}, u32[]{:S(2)}, u32[]{:S(2)}) collective-permute-start(bf16[144,512]{1,0:T(8,128)(2,1)S(1)} %pad_maximum_fusion.9), channel_id=1, source_target_pairs={{0,16},{16,32},{32,48},{48,0},{64,80},{80,96},{96,112},{112,64},{1... | collective-permute-start | bytes 442376 | tf_op jit(solution)/shard_map/ppermute | solution.py:99
  180.3 4.5 %collective-permute-start.32 = (bf16[512,512]{1,0:T(8,128)(2,1)S(1)}, bf16[512,512]{1,0:T(8,128)(2,1)S(1)}, u32[]{:S(2)}, u32[]{:S(2)}) collective-permute-start(bf16[512,512]{1,0:T(8,128)(2,1)S(1)} %collective-permute-done.28.refs_1_), channel_id=1, source_target_pairs={{0,1},{1,0},{2,3},{3,2},{4,5},{5,4},{6,7},{7,6},{8,9},{9,8},{10,11... | collective-permute-start | bytes 1572872 | tf_op jit(solution)/shard_map/ppermute | solution.py:107
  210.4 21.1 %collective-permute-start.37 = (bf16[512,512]{1,0:T(8,128)(2,1)}, bf16[512,512]{1,0:T(8,128)(2,1)S(1)}, u32[]{:S(2)}, u32[]{:S(2)}) collective-permute-start(bf16[512,512]{1,0:T(8,128)(2,1)} %get-tuple-element.52), channel_id=1, source_target_pairs={{0,16},{16,32},{32,48},{48,0},{64,80},{80,96},{96,112},{112,64},{1... | collective-permute-start | bytes 1572872 | tf_op jit(solution)/shard_map/ppermute | solution.py:99
  210.5 21.4 %collective-permute-start.38 = (bf16[512,512]{1,0:T(8,128)(2,1)}, bf16[512,512]{1,0:T(8,128)(2,1)S(1)}, u32[]{:S(2)}, u32[]{:S(2)}) collective-permute-start(bf16[512,512]{1,0:T(8,128)(2,1)} %get-tuple-element.54), channel_id=1, source_target_pairs={{0,48},{16,0},{32,16},{48,32},{64,112},{80,64},{96,80},{112,96},{1... | collective-permute-start | bytes 1572872 | tf_op jit(solution)/shard_map/ppermute | solution.py:99
  213.2 20.2 %collective-permute-start.39 = (bf16[512,512]{1,0:T(8,128)(2,1)}, bf16[512,512]{1,0:T(8,128)(2,1)S(1)}, u32[]{:S(2)}, u32[]{:S(2)}) collective-permute-start(bf16[512,512]{1,0:T(8,128)(2,1)} %get-tuple-element.55), channel_id=1, source_target_pairs={{0,32},{16,48},{32,0},{48,16},{64,96},{80,112},{96,64},{112,80},{1... | collective-permute-start | bytes 1572872 | tf_op jit(solution)/shard_map/ppermute | solution.py:99
  214.0 31.7 %collective-permute-start.45 = (bf16[1024,512]{1,0:T(8,128)(2,1)}, bf16[1024,512]{1,0:T(8,128)(2,1)S(1)}, u32[]{:S(2)}, u32[]{:S(2)}) collective-permute-start(bf16[1024,512]{1,0:T(8,128)(2,1)} %get-tuple-element.58), channel_id=1, source_target_pairs={{0,64},{16,80},{32,96},{48,112},{64,0},{80,16},{96,32},{112,48},{1... | collective-permute-start | bytes 3145736 | tf_op jit(solution)/shard_map/ppermute | solution.py:107
  231.5 6.4 %collective-permute-start.41 = (bf16[144,512]{1,0:T(8,128)(2,1)S(1)}, bf16[144,512]{1,0:T(8,128)(2,1)S(1)}, u32[]{:S(2)}, u32[]{:S(2)}) collective-permute-start(bf16[144,512]{1,0:T(8,128)(2,1)S(1)} %pad_maximum_fusion.10), channel_id=1, source_target_pairs={{0,8},{1,9},{2,10},{3,11},{4,12},{5,13},{6,14},{7,15},{8,0},{9,1},... | collective-permute-start | bytes 442376 | tf_op jit(solution)/shard_map/ppermute | solution.py:103
  231.8 6.1 %collective-permute-start.42 = (bf16[144,512]{1,0:T(8,128)(2,1)S(1)}, bf16[144,512]{1,0:T(8,128)(2,1)S(1)}, u32[]{:S(2)}, u32[]{:S(2)}) collective-permute-start(bf16[144,512]{1,0:T(8,128)(2,1)S(1)} %pad_maximum_fusion.10), channel_id=1, source_target_pairs={{0,12},{1,13},{2,14},{3,15},{4,0},{5,1},{6,2},{7,3},{8,4},{9,5},{1... | collective-permute-start | bytes 442376 | tf_op jit(solution)/shard_map/ppermute | solution.py:103
  231.9 7.4 %collective-permute-start.43 = (bf16[144,512]{1,0:T(8,128)(2,1)S(1)}, bf16[144,512]{1,0:T(8,128)(2,1)S(1)}, u32[]{:S(2)}, u32[]{:S(2)}) collective-permute-start(bf16[144,512]{1,0:T(8,128)(2,1)S(1)} %pad_maximum_fusion.10), channel_id=1, source_target_pairs={{0,4},{1,5},{2,6},{3,7},{4,8},{5,9},{6,10},{7,11},{8,12},{9,13},{1... | collective-permute-start | bytes 442376 | tf_op jit(solution)/shard_map/ppermute | solution.py:103
  234.7 9.5 %collective-permute-start.40 = (bf16[256,512]{1,0:T(8,128)(2,1)S(1)}, bf16[256,512]{1,0:T(8,128)(2,1)S(1)}, u32[]{:S(2)}, u32[]{:S(2)}) collective-permute-start(bf16[256,512]{1,0:T(8,128)(2,1)S(1)} %slice.222), channel_id=1, source_target_pairs={{0,64},{16,80},{32,96},{48,112},{64,0},{80,16},{96,32},{112,48},{1... | collective-permute-start | bytes 786440 | tf_op jit(solution)/shard_map/ppermute | solution.py:107
  239.4 5.6 %collective-permute-start.44 = (bf16[144,512]{1,0:T(8,128)(2,1)S(1)}, bf16[144,512]{1,0:T(8,128)(2,1)S(1)}, u32[]{:S(2)}, u32[]{:S(2)}) collective-permute-start(bf16[144,512]{1,0:T(8,128)(2,1)S(1)} %pad_maximum_fusion.11), channel_id=1, source_target_pairs={{0,2},{1,3},{2,0},{3,1},{4,6},{5,7},{6,4},{7,5},{8,10},{9,11},{10,... | collective-permute-start | bytes 442376 | tf_op jit(solution)/shard_map/ppermute | solution.py:107
  245.7 5.8 %collective-permute-start.46 = (bf16[128,512]{1,0:T(8,128)(2,1)S(1)}, bf16[128,512]{1,0:T(8,128)(2,1)S(1)}, u32[]{:S(2)}, u32[]{:S(2)}) collective-permute-start(bf16[128,512]{1,0:T(8,128)(2,1)S(1)} %slice.170), channel_id=1, source_target_pairs={{0,64},{16,80},{32,96},{48,112},{64,0},{80,16},{96,32},{112,48},{1... | collective-permute-start | bytes 393224 | tf_op jit(solution)/shard_map/ppermute | solution.py:107
  247.6 7.2 %collective-permute-start.47 = (bf16[256,512]{1,0:T(8,128)(2,1)S(1)}, bf16[256,512]{1,0:T(8,128)(2,1)S(1)}, u32[]{:S(2)}, u32[]{:S(2)}) collective-permute-start(bf16[256,512]{1,0:T(8,128)(2,1)S(1)} %get-tuple-element.89), channel_id=1, source_target_pairs={{0,16},{16,32},{32,48},{48,0},{64,80},{80,96},{96,112},{112,64},{1... | collective-permute-start | bytes 786440 | tf_op jit(solution)/shard_map/ppermute | solution.py:99
  247.7 7.6 %collective-permute-start.48 = (bf16[256,512]{1,0:T(8,128)(2,1)S(1)}, bf16[256,512]{1,0:T(8,128)(2,1)S(1)}, u32[]{:S(2)}, u32[]{:S(2)}) collective-permute-start(bf16[256,512]{1,0:T(8,128)(2,1)S(1)} %get-tuple-element.87), channel_id=1, source_target_pairs={{0,48},{16,0},{32,16},{48,32},{64,112},{80,64},{96,80},{112,96},{1... | collective-permute-start | bytes 786440 | tf_op jit(solution)/shard_map/ppermute | solution.py:99
  250.4 12.1 %collective-permute-start.49 = (bf16[256,512]{1,0:T(8,128)(2,1)S(1)}, bf16[256,512]{1,0:T(8,128)(2,1)S(1)}, u32[]{:S(2)}, u32[]{:S(2)}) collective-permute-start(bf16[256,512]{1,0:T(8,128)(2,1)S(1)} %get-tuple-element.88), channel_id=1, source_target_pairs={{0,32},{16,48},{32,0},{48,16},{64,96},{80,112},{96,64},{112,80},{1... | collective-permute-start | bytes 786440 | tf_op jit(solution)/shard_map/ppermute | solution.py:99
  255.3 8.4 %collective-permute-start.50 = (bf16[256,512]{1,0:T(8,128)(2,1)S(1)}, bf16[256,512]{1,0:T(8,128)(2,1)S(1)}, u32[]{:S(2)}, u32[]{:S(2)}) collective-permute-start(bf16[256,512]{1,0:T(8,128)(2,1)S(1)} %pad_maximum_fusion.7), channel_id=1, source_target_pairs={{0,1},{1,0},{2,3},{3,2},{4,5},{5,4},{6,7},{7,6},{8,9},{9,8},{10,11... | collective-permute-start | bytes 786440 | tf_op jit(solution)/shard_map/ppermute | solution.py:107
  (29 other events, 501.2 us)

commit v4 on v3

--- a/solution.py
+++ b/solution.py
@@ -244,10 +244,11 @@
     )
     got = send_along(backs, from_z)
     far_1 = swap(far_1, "row", 4)
-    grad_weight, got[1] = lax.optimization_barrier((grad_weight, got[1]))
+    grad_weight, got[1], got[3] = lax.optimization_barrier((grad_weight, got[1], got[3]))
     grad_weight, grad_bias = add_all(grad_weight, grad_bias, from_y)
     grad_weight, grad_bias = add_pair(grad_weight, grad_bias, "col", 2)
     grad_weight, far_1 = lax.optimization_barrier((grad_weight, far_1))
+    got[2], far_1 = lax.optimization_barrier((got[2], far_1))
     parts_1 = meet_across(near_1, far_1)
     got_1 = send_along(parts_1, from_z)
     grad_weight = join(grad_weight, "row", 4)

time: 265 us -> 263 us (level)
  waiting for transfers between devices: 149 us -> 128 us
  starting transfers between devices: 47.3 us -> 65.5 us
  Pallas kernels: 44 us -> 38.9 us
    ppermute x15, starting transfers between devices: 8.91 us -> 19.7 us  [from_y(): return lax.ppermute(x, 'col', [(i, i - 4 * s & 15) for i in range(16)])]
    ppermute x15, waiting for transfers between devices: 63.1 us -> 52.4 us  [from_z(): return lax.ppermute(x, 'row', [(i, i & 4 | i - s & 3) for i in range(8)])]
    ppermute x21, waiting for transfers between devices: 61.1 us -> 51.9 us  [swap(): lax.ppermute(x, axis, [(i, i ^ bit) for i in range(lax.axis_size(axis))])]
    ppermute x21, starting transfers between devices: 24.6 us -> 30 us  [swap(): lax.ppermute(x, axis, [(i, i ^ bit) for i in range(lax.axis_size(axis))])]
    pallas_call x2, Pallas kernels: 44 us -> 38.9 us  [product(): pl.pallas_call(functools.partial(product_kernel, len(sources), len(out_ro...]
  transfers between devices with their start and end apart: 51 -> 51, of which waited for: 28 -> 27; matrix products, arithmetic and copies ran while one was open for 6% -> 7% of each run, Pallas kernels for 0% -> 0%
where the time goes in v4:
time: 263 us; the launch traced here: 260 us
  waiting for transfers between devices  128 us (49%)
  starting transfers between devices  65.5 us (25%)
  Pallas kernels  38.9 us (15%)
  other arithmetic  15.5 us (6%)
  local copies, waits for them, and re-layouts  7.32 us (3%)
  matrix products  3.05 us (1%)
    ppermute x15, waiting for transfers between devices, from_z(): return lax.ppermute(x, 'row', [(i, i & 4 | i - s & 3) for i in range(8)])  52.4 us
    ppermute x21, waiting for transfers between devices, swap(): lax.ppermute(x, axis, [(i, i ^ bit) for i in range(lax.axis_size(axis))])  51.9 us
    pallas_call x2, Pallas kernels, product(): pl.pallas_call(functools.partial(product_kernel, len(sources), len(out_ro...  38.9 us
    ppermute x21, starting transfers between devices, swap(): lax.ppermute(x, axis, [(i, i ^ bit) for i in range(lax.axis_size(axis))])  30 us
    ppermute x15, waiting for transfers between devices, from_y(): return lax.ppermute(x, 'col', [(i, i - 4 * s & 15) for i in range(16)])  23.9 us
    ppermute x15, starting transfers between devices, from_y(): return lax.ppermute(x, 'col', [(i, i - 4 * s & 15) for i in range(16)])  19.7 us
    ppermute x15, starting transfers between devices, from_z(): return lax.ppermute(x, 'row', [(i, i & 4 | i - s & 3) for i in range(8)])  15.7 us
  transfers between devices with their start and end apart: 51, of which 27 were waited for; matrix products, arithmetic and copies ran while one was open for 7% of the time, Pallas kernels for 0%

profile of v4, /device:TPU:1, one launch (start us, length us, event | category | flops | bytes accessed | tf_op | source)
XLA Modules:
  0.0 260.3 jit_solution(4199922381852353780)
XLA Ops:
  1.8 3.7 %collective-permute-start.3 = (bf16[256,512]{1,0:T(8,128)(2,1)S(1)}, bf16[256,512]{1,0:T(8,128)(2,1)S(1)}, u32[]{:S(2)}, u32[]{:S(2)}) collective-permute-start(bf16[256,512]{1,0:T(8,128)(2,1)S(1)} %get-tuple-element.105), channel_id=1, source_target_pairs={{0,64},{16,80},{32,96},{48,112},{64,0},{80,16},{96,32},{112,48},{1... | collective-permute-start | bytes 786440 | tf_op jit(solution)/shard_map/ppermute | solution.py:107
  5.4 1.6 collective-permute-start.2
  7.1 3.3 %collective-permute-start.1 = (bf16[256,512]{1,0:T(8,128)(2,1)S(1)}, bf16[256,512]{1,0:T(8,128)(2,1)S(1)}, u32[]{:S(2)}, u32[]{:S(2)}) collective-permute-start(bf16[256,512]{1,0:T(8,128)(2,1)S(1)} %get-tuple-element.106), channel_id=1, source_target_pairs={{0,32},{16,48},{32,0},{48,16},{64,96},{80,112},{96,64},{112,80},{1... | collective-permute-start | bytes 786440 | tf_op jit(solution)/shard_map/ppermute | solution.py:99
  11.2 3.7 %collective-permute-done.2 = bf16[256,512]{1,0:T(8,128)(2,1)S(1)} collective-permute-done((bf16[256,512]{1,0:T(8,128)(2,1)S(1)}, bf16[256,512]{1,0:T(8,128)(2,1)S(1)}, u32[]{:S(2)}, u32[]{:S(2)}) %collective-permute-start.2) | collective-permute-done | bytes 262176 | tf_op jit(solution)/shard_map/ppermute | solution.py:99
  14.9 6.5 %collective-permute-done.1 = bf16[256,512]{1,0:T(8,128)(2,1)S(1)} collective-permute-done((bf16[256,512]{1,0:T(8,128)(2,1)S(1)}, bf16[256,512]{1,0:T(8,128)(2,1)S(1)}, u32[]{:S(2)}, u32[]{:S(2)}) %collective-permute-start.1) | collective-permute-done | bytes 262176 | tf_op jit(solution)/shard_map/ppermute | solution.py:99
  22.5 3.2 %collective-permute-start.4 = (bf16[512,512]{1,0:T(8,128)(2,1)S(1)}, bf16[512,512]{1,0:T(8,128)(2,1)S(1)}, u32[]{:S(2)}, u32[]{:S(2)}) collective-permute-start(bf16[512,512]{1,0:T(8,128)(2,1)S(1)} %pad_maximum_fusion.2.refs_0_), channel_id=1, source_target_pairs={{0,48},{16,0},{32,16},{48,32},{64,112},{80,64},{96,80},{112,96},{1... | collective-permute-start | bytes 1572872 | tf_op jit(solution)/shard_map/ppermute | solution.py:99
  27.1 20.2 %collective-permute-done.4.refs_1_ = bf16[512,512]{1,0:T(8,128)(2,1)S(1)} collective-permute-done((bf16[512,512]{1,0:T(8,128)(2,1)S(1)}, bf16[512,512]{1,0:T(8,128)(2,1)S(1)}, u32[]{:S(2)}, u32[]{:S(2)}) %collective-permute-start.4) | collective-permute-done | bytes 524320 | tf_op jit(solution)/shard_map/ppermute | solution.py:99
  47.3 5.0 %collective-permute-done.6.refs_3_ = bf16[512,512]{1,0:T(8,128)(2,1)S(1)} collective-permute-done((bf16[512,512]{1,0:T(8,128)(2,1)S(1)}, bf16[512,512]{1,0:T(8,128)(2,1)S(1)}, u32[]{:S(2)}, u32[]{:S(2)}) %collective-permute-start.6) | collective-permute-done | bytes 524320 | tf_op jit(solution)/shard_map/ppermute | solution.py:99
  53.5 19.3 %shard_map.111 = (bf16[2048,512]{1,0:T(8,128)(2,1)}, bf16[2048,512]{1,0:T(8,128)(2,1)}, bf16[2048,512]{1,0:T(8,128)(2,1)}, bf16[2048,512]{1,0:T(8,128)(2,1)}) custom-call(s32[1]{0:T(128)} %copy.12.count_ref, s32[384]{0:T(512)} %get-tuple-element.109.src_idx, s32[384]{0:T(512)} %get-tuple-element.81.dst_idx, bf16[384,128,128]{2,1,0:T(8,128)(2,1)} %values.3, ...), custom_call_target="tpu_custom_call" | custom-call | flops 6442450944 | bytes 25165824 | tf_op jit(solution)/shard_map/pallas_call | solution.py:75
  72.8 1.8 collective-permute-start.12
  74.8 3.9 %collective-permute-done.12 = bf16[2048,512]{1,0:T(8,128)(2,1)S(1)} collective-permute-done((bf16[2048,512]{1,0:T(8,128)(2,1)}, bf16[2048,512]{1,0:T(8,128)(2,1)S(1)}, u32[]{:S(2)}, u32[]{:S(2)}) %collective-permute-start.12) | collective-permute-done | bytes 2097184 | tf_op jit(solution)/shard_map/ppermute | solution.py:107
  78.7 1.5 add_convert_fusion
  81.7 2.8 %convert_add_fusion = (f32[2048,512]{1,0:T(8,128)}, bf16[2048,512]{1,0:T(8,128)(2,1)S(1)}) fusion(bf16[2048,512]{1,0:T(8,128)(2,1)S(1)} %collective-permute-done.8, bf16[2048,512]{1,0:T(8,128)(2,1)S(1)} %copy-done.1), kind=kLoop, calls=%fused_computation | loop fusion | flops 4194304 | bytes 10485760 | tf_op jit(solution)/shard_map/add | solution.py:203
  85.7 1.5 collective-permute-start.11
  87.1 2.3 collective-permute-start.10
  90.0 14.7 %collective-permute-done.13 = bf16[1024,512]{1,0:T(8,128)(2,1)S(1)} collective-permute-done((bf16[1024,512]{1,0:T(8,128)(2,1)S(1)}, bf16[1024,512]{1,0:T(8,128)(2,1)S(1)}, u32[]{:S(2)}, u32[]{:S(2)}) %collective-permute-start.13) | collective-permute-done | bytes 1048608 | tf_op jit(solution)/shard_map/ppermute | solution.py:107
  106.2 5.2 %collective-permute-start.17 = (bf16[256,512]{1,0:T(8,128)(2,1)}, bf16[256,512]{1,0:T(8,128)(2,1)S(1)}, u32[]{:S(2)}, u32[]{:S(2)}) collective-permute-start(bf16[256,512]{1,0:T(8,128)(2,1)} %get-tuple-element.97), channel_id=1, source_target_pairs={{0,8},{1,9},{2,10},{3,11},{4,12},{5,13},{6,14},{7,15},{8,0},{9,1},... | collective-permute-start | bytes 786440 | tf_op jit(solution)/shard_map/ppermute | solution.py:103
  111.4 7.6 %collective-permute-done.14 = bf16[256,512]{1,0:T(8,128)(2,1)S(1)} collective-permute-done((bf16[256,512]{1,0:T(8,128)(2,1)}, bf16[256,512]{1,0:T(8,128)(2,1)S(1)}, u32[]{:S(2)}, u32[]{:S(2)}) %collective-permute-start.14) | collective-permute-done | bytes 262176 | tf_op jit(solution)/shard_map/ppermute | solution.py:103
  119.0 1.8 slice_add_fusion
  121.1 1.7 collective-permute-done.17
  124.7 3.7 %collective-permute-done.15 = bf16[256,512]{1,0:T(8,128)(2,1)S(1)} collective-permute-done((bf16[256,512]{1,0:T(8,128)(2,1)S(1)}, bf16[256,512]{1,0:T(8,128)(2,1)S(1)}, u32[]{:S(2)}, u32[]{:S(2)}) %collective-permute-start.15) | collective-permute-done | bytes 262176 | tf_op jit(solution)/shard_map/ppermute | solution.py:107
  130.7 1.5 collective-permute-start.21
  132.2 1.6 collective-permute-start.19
  133.8 2.1 collective-permute-start.18
  137.2 1.5 collective-permute-start.22
  138.6 4.1 %collective-permute-done.23 = bf16[256,512]{1,0:T(8,128)(2,1)S(1)} collective-permute-done((bf16[256,512]{1,0:T(8,128)(2,1)S(1)}, bf16[256,512]{1,0:T(8,128)(2,1)S(1)}, u32[]{:S(2)}, u32[]{:S(2)}) %collective-permute-start.23) | collective-permute-done | bytes 262176 | tf_op jit(solution)/shard_map/ppermute | solution.py:107
  142.8 4.1 %collective-permute-done.20 = bf16[256,512]{1,0:T(8,128)(2,1)S(1)} collective-permute-done((bf16[256,512]{1,0:T(8,128)(2,1)S(1)}, bf16[256,512]{1,0:T(8,128)(2,1)S(1)}, u32[]{:S(2)}, u32[]{:S(2)}) %collective-permute-start.20) | collective-permute-done | bytes 262176 | tf_op jit(solution)/shard_map/ppermute | solution.py:103
  147.5 3.1 %collective-permute-start.28 = (bf16[512,512]{1,0:T(8,128)(2,1)S(1)}, bf16[512,512]{1,0:T(8,128)(2,1)S(1)}, u32[]{:S(2)}, u32[]{:S(2)}) collective-permute-start(bf16[512,512]{1,0:T(8,128)(2,1)S(1)} %pad_maximum_fusion.4.refs_0_), channel_id=1, source_target_pairs={{0,12},{1,13},{2,14},{3,15},{4,0},{5,1},{6,2},{7,3},{8,4},{9,5},{1... | collective-permute-start | bytes 1572872 | tf_op jit(solution)/shard_map/ppermute | solution.py:103
  151.2 2.0 collective-permute-start.31
  153.3 17.4 %collective-permute-done.24.refs_9_ = bf16[1024,512]{1,0:T(8,128)(2,1)S(1)} collective-permute-done((bf16[1024,512]{1,0:T(8,128)(2,1)S(1)}, bf16[1024,512]{1,0:T(8,128)(2,1)S(1)}, u32[]{:S(2)}, u32[]{:S(2)}) %collective-permute-start.24) | collective-permute-done | bytes 1048608 | tf_op jit(solution)/shard_map/ppermute | solution.py:107
  170.7 2.4 collective-permute-start.35
  174.1 3.1 %collective-permute-done.30.refs_3_ = bf16[512,512]{1,0:T(8,128)(2,1)S(1)} collective-permute-done((bf16[512,512]{1,0:T(8,128)(2,1)S(1)}, bf16[512,512]{1,0:T(8,128)(2,1)S(1)}, u32[]{:S(2)}, u32[]{:S(2)}) %collective-permute-start.30) | collective-permute-done | bytes 524320 | tf_op jit(solution)/shard_map/ppermute | solution.py:103
  177.8 3.0 %collective-permute-done.27 = bf16[144,512]{1,0:T(8,128)(2,1)S(1)} collective-permute-done((bf16[144,512]{1,0:T(8,128)(2,1)S(1)}, bf16[144,512]{1,0:T(8,128)(2,1)S(1)}, u32[]{:S(2)}, u32[]{:S(2)}) %collective-permute-start.27) | collective-permute-done | bytes 147488 | tf_op jit(solution)/shard_map/ppermute | solution.py:99
  182.1 2.3 collective-permute-start.33
  188.7 19.5 %shard_map.112 = (bf16[512,512]{1,0:T(8,128)(2,1)}, bf16[512,512]{1,0:T(8,128)(2,1)}, bf16[512,512]{1,0:T(8,128)(2,1)}, bf16[512,512]{1,0:T(8,128)(2,1)}, bf16[1...) custom-call(s32[1]{0:T(128)} %copy.12.count_ref, s32[384]{0:T(512)} %get-tuple-element.80.src_idx, ...), custom_call_target="tpu_custom_call" | custom-call | flops 6442450944 | bytes 25165824 | tf_op jit(solution)/shard_map/pallas_call | solution.py:75
  208.2 1.4 collective-permute-start.37
  211.0 4.0 %collective-permute-start.44 = (bf16[1024,512]{1,0:T(8,128)(2,1)}, bf16[1024,512]{1,0:T(8,128)(2,1)S(1)}, u32[]{:S(2)}, u32[]{:S(2)}) collective-permute-start(bf16[1024,512]{1,0:T(8,128)(2,1)} %get-tuple-element.61), channel_id=1, source_target_pairs={{0,64},{16,80},{32,96},{48,112},{64,0},{80,16},{96,32},{112,48},{1... | collective-permute-start | bytes 3145736 | tf_op jit(solution)/shard_map/ppermute | solution.py:107
  215.0 6.5 %collective-permute-done.37 = bf16[512,512]{1,0:T(8,128)(2,1)S(1)} collective-permute-done((bf16[512,512]{1,0:T(8,128)(2,1)}, bf16[512,512]{1,0:T(8,128)(2,1)S(1)}, u32[]{:S(2)}, u32[]{:S(2)}) %collective-permute-start.37) | collective-permute-done | bytes 524320 | tf_op jit(solution)/shard_map/ppermute | solution.py:99
  221.5 1.5 collective-permute-done.38
  223.1 2.7 %collective-permute-start.41 = (bf16[144,512]{1,0:T(8,128)(2,1)S(1)}, bf16[144,512]{1,0:T(8,128)(2,1)S(1)}, u32[]{:S(2)}, u32[]{:S(2)}) collective-permute-start(bf16[144,512]{1,0:T(8,128)(2,1)S(1)} %pad_maximum_fusion.10), channel_id=1, source_target_pairs={{0,12},{1,13},{2,14},{3,15},{4,0},{5,1},{6,2},{7,3},{8,4},{9,5},{1... | collective-permute-start | bytes 442376 | tf_op jit(solution)/shard_map/ppermute | solution.py:103
  225.8 2.8 %collective-permute-done.42 = bf16[144,512]{1,0:T(8,128)(2,1)S(1)} collective-permute-done((bf16[144,512]{1,0:T(8,128)(2,1)S(1)}, bf16[144,512]{1,0:T(8,128)(2,1)S(1)}, u32[]{:S(2)}, u32[]{:S(2)}) %collective-permute-start.42) | collective-permute-done | bytes 147488 | tf_op jit(solution)/shard_map/ppermute | solution.py:103
  229.5 2.1 collective-permute-done.40
  232.4 1.8 pad_maximum_fusion.3
  234.2 5.2 %collective-permute-done.43 = bf16[144,512]{1,0:T(8,128)(2,1)} collective-permute-done((bf16[144,512]{1,0:T(8,128)(2,1)}, bf16[144,512]{1,0:T(8,128)(2,1)}, u32[]{:S(2)}, u32[]{:S(2)}) %collective-permute-start.43) | collective-permute-done | bytes 147488 | tf_op jit(solution)/shard_map/ppermute | solution.py:107
  241.5 4.9 %collective-permute-start.46 = (bf16[128,512]{1,0:T(8,128)(2,1)S(1)}, bf16[128,512]{1,0:T(8,128)(2,1)S(1)}, u32[]{:S(2)}, u32[]{:S(2)}) collective-permute-start(bf16[128,512]{1,0:T(8,128)(2,1)S(1)} %slice.168), channel_id=1, source_target_pairs={{0,64},{16,80},{32,96},{48,112},{64,0},{80,16},{96,32},{112,48},{1... | collective-permute-start | bytes 393224 | tf_op jit(solution)/shard_map/ppermute | solution.py:107
  247.5 1.6 collective-permute-start.48
  250.6 5.4 %collective-permute-done.47 = bf16[256,512]{1,0:T(8,128)(2,1)S(1)} collective-permute-done((bf16[256,512]{1,0:T(8,128)(2,1)S(1)}, bf16[256,512]{1,0:T(8,128)(2,1)S(1)}, u32[]{:S(2)}, u32[]{:S(2)}) %collective-permute-start.47) | collective-permute-done | bytes 262176 | tf_op jit(solution)/shard_map/ppermute | solution.py:99
  256.0 1.6 collective-permute-start.50
  (178 shorter events, 34.3 us)
Async XLA Ops:
  1.8 9.3 %collective-permute-start.3 = (bf16[256,512]{1,0:T(8,128)(2,1)S(1)}, bf16[256,512]{1,0:T(8,128)(2,1)S(1)}, u32[]{:S(2)}, u32[]{:S(2)}) collective-permute-start(bf16[256,512]{1,0:T(8,128)(2,1)S(1)} %get-tuple-element.105), channel_id=1, source_target_pairs={{0,64},{16,80},{32,96},{48,112},{64,0},{80,16},{96,32},{112,48},{1... | collective-permute-start | bytes 786440 | tf_op jit(solution)/shard_map/ppermute | solution.py:107
  5.4 9.5 %collective-permute-start.2 = (bf16[256,512]{1,0:T(8,128)(2,1)S(1)}, bf16[256,512]{1,0:T(8,128)(2,1)S(1)}, u32[]{:S(2)}, u32[]{:S(2)}) collective-permute-start(bf16[256,512]{1,0:T(8,128)(2,1)S(1)} %get-tuple-element.106), channel_id=1, source_target_pairs={{0,16},{16,32},{32,48},{48,0},{64,80},{80,96},{96,112},{112,64},{1... | collective-permute-start | bytes 786440 | tf_op jit(solution)/shard_map/ppermute | solution.py:99
  7.1 14.3 %collective-permute-start.1 = (bf16[256,512]{1,0:T(8,128)(2,1)S(1)}, bf16[256,512]{1,0:T(8,128)(2,1)S(1)}, u32[]{:S(2)}, u32[]{:S(2)}) collective-permute-start(bf16[256,512]{1,0:T(8,128)(2,1)S(1)} %get-tuple-element.106), channel_id=1, source_target_pairs={{0,32},{16,48},{32,0},{48,16},{64,96},{80,112},{96,64},{112,80},{1... | collective-permute-start | bytes 786440 | tf_op jit(solution)/shard_map/ppermute | solution.py:99
  10.4 11.0 %collective-permute-start = (bf16[256,512]{1,0:T(8,128)(2,1)S(1)}, bf16[256,512]{1,0:T(8,128)(2,1)S(1)}, u32[]{:S(2)}, u32[]{:S(2)}) collective-permute-start(bf16[256,512]{1,0:T(8,128)(2,1)S(1)} %get-tuple-element.106), channel_id=1, source_target_pairs={{0,48},{16,0},{32,16},{48,32},{64,112},{80,64},{96,80},{112,96},{1... | collective-permute-start | bytes 786440 | tf_op jit(solution)/shard_map/ppermute | solution.py:99
  21.5 30.8 %collective-permute-start.7 = (bf16[1024,512]{1,0:T(8,128)(2,1)S(1)}, bf16[1024,512]{1,0:T(8,128)(2,1)S(1)}, u32[]{:S(2)}, u32[]{:S(2)}) collective-permute-start(bf16[1024,512]{1,0:T(8,128)(2,1)S(1)} %pad_maximum_fusion.refs_4_), channel_id=1, source_target_pairs={{0,64},{16,80},{32,96},{48,112},{64,0},{80,16},{96,32},{112,48},{1... | collective-permute-start | bytes 3145736 | tf_op jit(solution)/shard_map/ppermute | solution.py:107
  22.5 24.8 %collective-permute-start.4 = (bf16[512,512]{1,0:T(8,128)(2,1)S(1)}, bf16[512,512]{1,0:T(8,128)(2,1)S(1)}, u32[]{:S(2)}, u32[]{:S(2)}) collective-permute-start(bf16[512,512]{1,0:T(8,128)(2,1)S(1)} %pad_maximum_fusion.2.refs_0_), channel_id=1, source_target_pairs={{0,48},{16,0},{32,16},{48,32},{64,112},{80,64},{96,80},{112,96},{1... | collective-permute-start | bytes 1572872 | tf_op jit(solution)/shard_map/ppermute | solution.py:99
  25.7 21.6 %collective-permute-start.5 = (bf16[512,512]{1,0:T(8,128)(2,1)S(1)}, bf16[512,512]{1,0:T(8,128)(2,1)S(1)}, u32[]{:S(2)}, u32[]{:S(2)}) collective-permute-start(bf16[512,512]{1,0:T(8,128)(2,1)S(1)} %pad_maximum_fusion.2.refs_0_), channel_id=1, source_target_pairs={{0,32},{16,48},{32,0},{48,16},{64,96},{80,112},{96,64},{112,80},{1... | collective-permute-start | bytes 1572872 | tf_op jit(solution)/shard_map/ppermute | solution.py:99
  26.1 26.2 %collective-permute-start.6 = (bf16[512,512]{1,0:T(8,128)(2,1)S(1)}, bf16[512,512]{1,0:T(8,128)(2,1)S(1)}, u32[]{:S(2)}, u32[]{:S(2)}) collective-permute-start(bf16[512,512]{1,0:T(8,128)(2,1)S(1)} %pad_maximum_fusion.2.refs_0_), channel_id=1, source_target_pairs={{0,16},{16,32},{32,48},{48,0},{64,80},{80,96},{96,112},{112,64},{1... | collective-permute-start | bytes 1572872 | tf_op jit(solution)/shard_map/ppermute | solution.py:99
  72.8 5.8 %collective-permute-start.12 = (bf16[2048,512]{1,0:T(8,128)(2,1)}, bf16[2048,512]{1,0:T(8,128)(2,1)S(1)}, u32[]{:S(2)}, u32[]{:S(2)}) collective-permute-start(bf16[2048,512]{1,0:T(8,128)(2,1)} %get-tuple-element.42), channel_id=1, source_target_pairs={{0,1},{1,0},{2,3},{3,2},{4,5},{5,4},{6,7},{7,6},{8,9},{9,8},{10,11... | collective-permute-start | bytes 6291464 | tf_op jit(solution)/shard_map/ppermute | solution.py:107
  74.7 7.0 %collective-permute-start.8 = (bf16[2048,512]{1,0:T(8,128)(2,1)}, bf16[2048,512]{1,0:T(8,128)(2,1)S(1)}, u32[]{:S(2)}, u32[]{:S(2)}) collective-permute-start(bf16[2048,512]{1,0:T(8,128)(2,1)} %get-tuple-element.40), channel_id=1, source_target_pairs={{0,1},{1,0},{2,3},{3,2},{4,5},{5,4},{6,7},{7,6},{8,9},{9,8},{10,11... | collective-permute-start | bytes 6291464 | tf_op jit(solution)/shard_map/ppermute | solution.py:107
  80.2 24.6 %collective-permute-start.13 = (bf16[1024,512]{1,0:T(8,128)(2,1)S(1)}, bf16[1024,512]{1,0:T(8,128)(2,1)S(1)}, u32[]{:S(2)}, u32[]{:S(2)}) collective-permute-start(bf16[1024,512]{1,0:T(8,128)(2,1)S(1)} %add_convert_fusion), channel_id=1, source_target_pairs={{0,2},{1,3},{2,0},{3,1},{4,6},{5,7},{6,4},{7,5},{8,10},{9,11},{10,... | collective-permute-start | bytes 3145736 | tf_op jit(solution)/shard_map/ppermute | solution.py:107
  85.7 25.7 %collective-permute-start.11 = (bf16[512,512]{1,0:T(8,128)(2,1)}, bf16[512,512]{1,0:T(8,128)(2,1)S(1)}, u32[]{:S(2)}, u32[]{:S(2)}) collective-permute-start(bf16[512,512]{1,0:T(8,128)(2,1)} %get-tuple-element.91), channel_id=1, source_target_pairs={{0,8},{1,9},{2,10},{3,11},{4,12},{5,13},{6,14},{7,15},{8,0},{9,1},... | collective-permute-start | bytes 1572872 | tf_op jit(solution)/shard_map/ppermute | solution.py:103
  87.1 31.8 %collective-permute-start.10 = (bf16[512,512]{1,0:T(8,128)(2,1)}, bf16[512,512]{1,0:T(8,128)(2,1)}, u32[]{:S(2)}, u32[]{:S(2)}) collective-permute-start(bf16[512,512]{1,0:T(8,128)(2,1)} %get-tuple-element.92), channel_id=1, source_target_pairs={{0,12},{1,13},{2,14},{3,15},{4,0},{5,1},{6,2},{7,3},{8,4},{9,5},{1... | collective-permute-start | bytes 1572872 | tf_op jit(solution)/shard_map/ppermute | solution.py:103
  89.5 29.5 %collective-permute-start.9 = (bf16[512,512]{1,0:T(8,128)(2,1)}, bf16[512,512]{1,0:T(8,128)(2,1)}, u32[]{:S(2)}, u32[]{:S(2)}) collective-permute-start(bf16[512,512]{1,0:T(8,128)(2,1)} %get-tuple-element.90), channel_id=1, source_target_pairs={{0,4},{1,5},{2,6},{3,7},{4,8},{5,9},{6,10},{7,11},{8,12},{9,13},{1... | collective-permute-start | bytes 1572872 | tf_op jit(solution)/shard_map/ppermute | solution.py:103
  106.2 12.8 %collective-permute-start.14 = (bf16[256,512]{1,0:T(8,128)(2,1)}, bf16[256,512]{1,0:T(8,128)(2,1)S(1)}, u32[]{:S(2)}, u32[]{:S(2)}) collective-permute-start(bf16[256,512]{1,0:T(8,128)(2,1)} %get-tuple-element.96), channel_id=1, source_target_pairs={{0,4},{1,5},{2,6},{3,7},{4,8},{5,9},{6,10},{7,11},{8,12},{9,13},{1... | collective-permute-start | bytes 786440 | tf_op jit(solution)/shard_map/ppermute | solution.py:103
  106.2 16.6 %collective-permute-start.17 = (bf16[256,512]{1,0:T(8,128)(2,1)}, bf16[256,512]{1,0:T(8,128)(2,1)S(1)}, u32[]{:S(2)}, u32[]{:S(2)}) collective-permute-start(bf16[256,512]{1,0:T(8,128)(2,1)} %get-tuple-element.97), channel_id=1, source_target_pairs={{0,8},{1,9},{2,10},{3,11},{4,12},{5,13},{6,14},{7,15},{8,0},{9,1},... | collective-permute-start | bytes 786440 | tf_op jit(solution)/shard_map/ppermute | solution.py:103
  111.4 12.8 %collective-permute-start.16 = (bf16[256,512]{1,0:T(8,128)(2,1)}, bf16[256,512]{1,0:T(8,128)(2,1)S(1)}, u32[]{:S(2)}, u32[]{:S(2)}) collective-permute-start(bf16[256,512]{1,0:T(8,128)(2,1)} %get-tuple-element.98), channel_id=1, source_target_pairs={{0,12},{1,13},{2,14},{3,15},{4,0},{5,1},{6,2},{7,3},{8,4},{9,5},{1... | collective-permute-start | bytes 786440 | tf_op jit(solution)/shard_map/ppermute | solution.py:103
  120.8 7.5 %collective-permute-start.15 = (bf16[256,512]{1,0:T(8,128)(2,1)S(1)}, bf16[256,512]{1,0:T(8,128)(2,1)S(1)}, u32[]{:S(2)}, u32[]{:S(2)}) collective-permute-start(bf16[256,512]{1,0:T(8,128)(2,1)S(1)} %slice.223), channel_id=1, source_target_pairs={{0,2},{1,3},{2,0},{3,1},{4,6},{5,7},{6,4},{7,5},{8,10},{9,11},{10,... | collective-permute-start | bytes 786440 | tf_op jit(solution)/shard_map/ppermute | solution.py:107
  130.7 6.3 %collective-permute-start.21 = (bf16[272,512]{1,0:T(8,128)(2,1)S(1)}, bf16[272,512]{1,0:T(8,128)(2,1)S(1)}, u32[]{:S(2)}, u32[]{:S(2)}) collective-permute-start(bf16[272,512]{1,0:T(8,128)(2,1)S(1)} %pad_maximum_fusion.6), channel_id=1, source_target_pairs={{0,1},{1,0},{2,3},{3,2},{4,5},{5,4},{6,7},{7,6},{8,9},{9,8},{10,11... | collective-permute-start | bytes 835592 | tf_op jit(solution)/shard_map/ppermute | solution.py:107
  132.2 14.7 %collective-permute-start.20 = (bf16[256,512]{1,0:T(8,128)(2,1)S(1)}, bf16[256,512]{1,0:T(8,128)(2,1)S(1)}, u32[]{:S(2)}, u32[]{:S(2)}) collective-permute-start(bf16[256,512]{1,0:T(8,128)(2,1)S(1)} %get-tuple-element.46), channel_id=1, source_target_pairs={{0,4},{1,5},{2,6},{3,7},{4,8},{5,9},{6,10},{7,11},{8,12},{9,13},{1... | collective-permute-start | bytes 786440 | tf_op jit(solution)/shard_map/ppermute | solution.py:103
  132.2 14.7 %collective-permute-start.19 = (bf16[256,512]{1,0:T(8,128)(2,1)S(1)}, bf16[256,512]{1,0:T(8,128)(2,1)S(1)}, u32[]{:S(2)}, u32[]{:S(2)}) collective-permute-start(bf16[256,512]{1,0:T(8,128)(2,1)S(1)} %get-tuple-element.46), channel_id=1, source_target_pairs={{0,8},{1,9},{2,10},{3,11},{4,12},{5,13},{6,14},{7,15},{8,0},{9,1},... | collective-permute-start | bytes 786440 | tf_op jit(solution)/shard_map/ppermute | solution.py:103
  133.8 13.4 %collective-permute-start.18 = (bf16[256,512]{1,0:T(8,128)(2,1)S(1)}, bf16[256,512]{1,0:T(8,128)(2,1)S(1)}, u32[]{:S(2)}, u32[]{:S(2)}) collective-permute-start(bf16[256,512]{1,0:T(8,128)(2,1)S(1)} %get-tuple-element.46), channel_id=1, source_target_pairs={{0,12},{1,13},{2,14},{3,15},{4,0},{5,1},{6,2},{7,3},{8,4},{9,5},{1... | collective-permute-start | bytes 786440 | tf_op jit(solution)/shard_map/ppermute | solution.py:103
  135.8 6.9 %collective-permute-start.23 = (bf16[256,512]{1,0:T(8,128)(2,1)S(1)}, bf16[256,512]{1,0:T(8,128)(2,1)S(1)}, u32[]{:S(2)}, u32[]{:S(2)}) collective-permute-start(bf16[256,512]{1,0:T(8,128)(2,1)S(1)} %get-tuple-element.45), channel_id=1, source_target_pairs={{0,2},{1,3},{2,0},{3,1},{4,6},{5,7},{6,4},{7,5},{8,10},{9,11},{10,... | collective-permute-start | bytes 786440 | tf_op jit(solution)/shard_map/ppermute | solution.py:107
  137.2 10.1 %collective-permute-start.22 = (bf16[144,512]{1,0:T(8,128)(2,1)S(1)}, bf16[144,512]{1,0:T(8,128)(2,1)S(1)}, u32[]{:S(2)}, u32[]{:S(2)}) collective-permute-start(bf16[144,512]{1,0:T(8,128)(2,1)S(1)} %pad_maximum_fusion.8), channel_id=1, source_target_pairs={{0,64},{16,80},{32,96},{48,112},{64,0},{80,16},{96,32},{112,48},{1... | collective-permute-start | bytes 442376 | tf_op jit(solution)/shard_map/ppermute | solution.py:107
  147.4 23.3 %collective-permute-start.24 = (bf16[1024,512]{1,0:T(8,128)(2,1)S(1)}, bf16[1024,512]{1,0:T(8,128)(2,1)S(1)}, u32[]{:S(2)}, u32[]{:S(2)}) collective-permute-start(bf16[1024,512]{1,0:T(8,128)(2,1)S(1)} %pad_maximum_fusion.1.refs_8_), channel_id=1, source_target_pairs={{0,2},{1,3},{2,0},{3,1},{4,6},{5,7},{6,4},{7,5},{8,10},{9,11},{10,... | collective-permute-start | bytes 3145736 | tf_op jit(solution)/shard_map/ppermute | solution.py:107
  147.5 25.6 %collective-permute-start.28 = (bf16[512,512]{1,0:T(8,128)(2,1)S(1)}, bf16[512,512]{1,0:T(8,128)(2,1)S(1)}, u32[]{:S(2)}, u32[]{:S(2)}) collective-permute-start(bf16[512,512]{1,0:T(8,128)(2,1)S(1)} %pad_maximum_fusion.4.refs_0_), channel_id=1, source_target_pairs={{0,12},{1,13},{2,14},{3,15},{4,0},{5,1},{6,2},{7,3},{8,4},{9,5},{1... | collective-permute-start | bytes 1572872 | tf_op jit(solution)/shard_map/ppermute | solution.py:103
  150.6 23.4 %collective-permute-start.29 = (bf16[512,512]{1,0:T(8,128)(2,1)S(1)}, bf16[512,512]{1,0:T(8,128)(2,1)S(1)}, u32[]{:S(2)}, u32[]{:S(2)}) collective-permute-start(bf16[512,512]{1,0:T(8,128)(2,1)S(1)} %pad_maximum_fusion.4.refs_0_), channel_id=1, source_target_pairs={{0,8},{1,9},{2,10},{3,11},{4,12},{5,13},{6,14},{7,15},{8,0},{9,1},... | collective-permute-start | bytes 1572872 | tf_op jit(solution)/shard_map/ppermute | solution.py:103
  150.9 26.2 %collective-permute-start.30 = (bf16[512,512]{1,0:T(8,128)(2,1)S(1)}, bf16[512,512]{1,0:T(8,128)(2,1)S(1)}, u32[]{:S(2)}, u32[]{:S(2)}) collective-permute-start(bf16[512,512]{1,0:T(8,128)(2,1)S(1)} %pad_maximum_fusion.4.refs_0_), channel_id=1, source_target_pairs={{0,4},{1,5},{2,6},{3,7},{4,8},{5,9},{6,10},{7,11},{8,12},{9,13},{1... | collective-permute-start | bytes 1572872 | tf_op jit(solution)/shard_map/ppermute | solution.py:103
  151.2 25.9 %collective-permute-start.31 = (bf16[512,512]{1,0:T(8,128)(2,1)S(1)}, bf16[512,512]{1,0:T(8,128)(2,1)S(1)}, u32[]{:S(2)}, u32[]{:S(2)}) collective-permute-start(bf16[512,512]{1,0:T(8,128)(2,1)S(1)} %pad_maximum_fusion.4.refs_0_), channel_id=1, source_target_pairs={{0,1},{1,0},{2,3},{3,2},{4,5},{5,4},{6,7},{7,6},{8,9},{9,8},{10,11... | collective-permute-start | bytes 1572872 | tf_op jit(solution)/shard_map/ppermute | solution.py:107
  170.7 16.0 %collective-permute-start.35 = (bf16[1024,512]{1,0:T(8,128)(2,1)S(1)}, bf16[1024,512]{1,0:T(8,128)(2,1)S(1)}, u32[]{:S(2)}, u32[]{:S(2)}) collective-permute-start(bf16[1024,512]{1,0:T(8,128)(2,1)S(1)} %pad_maximum_fusion.1.refs_8_), channel_id=1, source_target_pairs={{0,1},{1,0},{2,3},{3,2},{4,5},{5,4},{6,7},{7,6},{8,9},{9,8},{10,11... | collective-permute-start | bytes 3145736 | tf_op jit(solution)/shard_map/ppermute | solution.py:107
  173.0 13.6 %collective-permute-start.36 = (bf16[1024,512]{1,0:T(8,128)(2,1)S(1)}, bf16[1024,512]{1,0:T(8,128)(2,1)S(1)}, u32[]{:S(2)}, u32[]{:S(2)}) collective-permute-start(bf16[1024,512]{1,0:T(8,128)(2,1)S(1)} %collective-permute-done.24.refs_9_), channel_id=1, source_target_pairs={{0,1},{1,0},{2,3},{3,2},{4,5},{5,4},{6,7},{7,6},{8,9},{9,8},{10,11... | collective-permute-start | bytes 3145736 | tf_op jit(solution)/shard_map/ppermute | solution.py:107
  174.0 6.8 %collective-permute-start.27 = (bf16[144,512]{1,0:T(8,128)(2,1)S(1)}, bf16[144,512]{1,0:T(8,128)(2,1)S(1)}, u32[]{:S(2)}, u32[]{:S(2)}) collective-permute-start(bf16[144,512]{1,0:T(8,128)(2,1)S(1)} %pad_maximum_fusion.9), channel_id=1, source_target_pairs={{0,16},{16,32},{32,48},{48,0},{64,80},{80,96},{96,112},{112,64},{1... | collective-permute-start | bytes 442376 | tf_op jit(solution)/shard_map/ppermute | solution.py:99
  177.2 4.9 %collective-permute-start.26 = (bf16[144,512]{1,0:T(8,128)(2,1)S(1)}, bf16[144,512]{1,0:T(8,128)(2,1)S(1)}, u32[]{:S(2)}, u32[]{:S(2)}) collective-permute-start(bf16[144,512]{1,0:T(8,128)(2,1)S(1)} %pad_maximum_fusion.9), channel_id=1, source_target_pairs={{0,48},{16,0},{32,16},{48,32},{64,112},{80,64},{96,80},{112,96},{1... | collective-permute-start | bytes 442376 | tf_op jit(solution)/shard_map/ppermute | solution.py:99
  177.2 7.2 %collective-permute-start.25 = (bf16[144,512]{1,0:T(8,128)(2,1)S(1)}, bf16[144,512]{1,0:T(8,128)(2,1)S(1)}, u32[]{:S(2)}, u32[]{:S(2)}) collective-permute-start(bf16[144,512]{1,0:T(8,128)(2,1)S(1)} %pad_maximum_fusion.9), channel_id=1, source_target_pairs={{0,32},{16,48},{32,0},{48,16},{64,96},{80,112},{96,64},{112,80},{1... | collective-permute-start | bytes 442376 | tf_op jit(solution)/shard_map/ppermute | solution.py:99
  180.8 4.4 %collective-permute-start.32 = (bf16[512,512]{1,0:T(8,128)(2,1)S(1)}, bf16[512,512]{1,0:T(8,128)(2,1)S(1)}, u32[]{:S(2)}, u32[]{:S(2)}) collective-permute-start(bf16[512,512]{1,0:T(8,128)(2,1)S(1)} %collective-permute-done.28.refs_1_), channel_id=1, source_target_pairs={{0,1},{1,0},{2,3},{3,2},{4,5},{5,4},{6,7},{7,6},{8,9},{9,8},{10,11... | collective-permute-start | bytes 1572872 | tf_op jit(solution)/shard_map/ppermute | solution.py:107
  208.2 13.3 %collective-permute-start.37 = (bf16[512,512]{1,0:T(8,128)(2,1)}, bf16[512,512]{1,0:T(8,128)(2,1)S(1)}, u32[]{:S(2)}, u32[]{:S(2)}) collective-permute-start(bf16[512,512]{1,0:T(8,128)(2,1)} %get-tuple-element.55), channel_id=1, source_target_pairs={{0,16},{16,32},{32,48},{48,0},{64,80},{80,96},{96,112},{112,64},{1... | collective-permute-start | bytes 1572872 | tf_op jit(solution)/shard_map/ppermute | solution.py:99
  209.6 13.3 %collective-permute-start.38 = (bf16[512,512]{1,0:T(8,128)(2,1)}, bf16[512,512]{1,0:T(8,128)(2,1)S(1)}, u32[]{:S(2)}, u32[]{:S(2)}) collective-permute-start(bf16[512,512]{1,0:T(8,128)(2,1)} %get-tuple-element.56), channel_id=1, source_target_pairs={{0,48},{16,0},{32,16},{48,32},{64,112},{80,64},{96,80},{112,96},{1... | collective-permute-start | bytes 1572872 | tf_op jit(solution)/shard_map/ppermute | solution.py:99
  211.0 29.9 %collective-permute-start.44 = (bf16[1024,512]{1,0:T(8,128)(2,1)}, bf16[1024,512]{1,0:T(8,128)(2,1)S(1)}, u32[]{:S(2)}, u32[]{:S(2)}) collective-permute-start(bf16[1024,512]{1,0:T(8,128)(2,1)} %get-tuple-element.61), channel_id=1, source_target_pairs={{0,64},{16,80},{32,96},{48,112},{64,0},{80,16},{96,32},{112,48},{1... | collective-permute-start | bytes 3145736 | tf_op jit(solution)/shard_map/ppermute | solution.py:107
  223.0 5.6 %collective-permute-start.42 = (bf16[144,512]{1,0:T(8,128)(2,1)S(1)}, bf16[144,512]{1,0:T(8,128)(2,1)S(1)}, u32[]{:S(2)}, u32[]{:S(2)}) collective-permute-start(bf16[144,512]{1,0:T(8,128)(2,1)S(1)} %pad_maximum_fusion.10), channel_id=1, source_target_pairs={{0,4},{1,5},{2,6},{3,7},{4,8},{5,9},{6,10},{7,11},{8,12},{9,13},{1... | collective-permute-start | bytes 442376 | tf_op jit(solution)/shard_map/ppermute | solution.py:103
  223.1 6.4 %collective-permute-start.41 = (bf16[144,512]{1,0:T(8,128)(2,1)S(1)}, bf16[144,512]{1,0:T(8,128)(2,1)S(1)}, u32[]{:S(2)}, u32[]{:S(2)}) collective-permute-start(bf16[144,512]{1,0:T(8,128)(2,1)S(1)} %pad_maximum_fusion.10), channel_id=1, source_target_pairs={{0,12},{1,13},{2,14},{3,15},{4,0},{5,1},{6,2},{7,3},{8,4},{9,5},{1... | collective-permute-start | bytes 442376 | tf_op jit(solution)/shard_map/ppermute | solution.py:103
  225.7 5.8 %collective-permute-start.40 = (bf16[144,512]{1,0:T(8,128)(2,1)S(1)}, bf16[144,512]{1,0:T(8,128)(2,1)S(1)}, u32[]{:S(2)}, u32[]{:S(2)}) collective-permute-start(bf16[144,512]{1,0:T(8,128)(2,1)S(1)} %pad_maximum_fusion.10), channel_id=1, source_target_pairs={{0,8},{1,9},{2,10},{3,11},{4,12},{5,13},{6,14},{7,15},{8,0},{9,1},... | collective-permute-start | bytes 442376 | tf_op jit(solution)/shard_map/ppermute | solution.py:103
  225.7 15.1 %collective-permute-start.39 = (bf16[512,512]{1,0:T(8,128)(2,1)}, bf16[512,512]{1,0:T(8,128)(2,1)}, u32[]{:S(2)}, u32[]{:S(2)}) collective-permute-start(bf16[512,512]{1,0:T(8,128)(2,1)} %get-tuple-element.59), channel_id=1, source_target_pairs={{0,32},{16,48},{32,0},{48,16},{64,96},{80,112},{96,64},{112,80},{1... | collective-permute-start | bytes 1572872 | tf_op jit(solution)/shard_map/ppermute | solution.py:99
  232.4 6.9 %collective-permute-start.43 = (bf16[144,512]{1,0:T(8,128)(2,1)}, bf16[144,512]{1,0:T(8,128)(2,1)}, u32[]{:S(2)}, u32[]{:S(2)}) collective-permute-start(bf16[144,512]{1,0:T(8,128)(2,1)} %pad_maximum_fusion.11), channel_id=1, source_target_pairs={{0,2},{1,3},{2,0},{3,1},{4,6},{5,7},{6,4},{7,5},{8,10},{9,11},{10,... | collective-permute-start | bytes 442376 | tf_op jit(solution)/shard_map/ppermute | solution.py:107
  241.4 16.2 %collective-permute-start.49 = (bf16[256,512]{1,0:T(8,128)(2,1)S(1)}, bf16[256,512]{1,0:T(8,128)(2,1)S(1)}, u32[]{:S(2)}, u32[]{:S(2)}) collective-permute-start(bf16[256,512]{1,0:T(8,128)(2,1)S(1)} %get-tuple-element.94), channel_id=1, source_target_pairs={{0,32},{16,48},{32,0},{48,16},{64,96},{80,112},{96,64},{112,80},{1... | collective-permute-start | bytes 786440 | tf_op jit(solution)/shard_map/ppermute | solution.py:99
  241.5 9.0 %collective-permute-start.46 = (bf16[128,512]{1,0:T(8,128)(2,1)S(1)}, bf16[128,512]{1,0:T(8,128)(2,1)S(1)}, u32[]{:S(2)}, u32[]{:S(2)}) collective-permute-start(bf16[128,512]{1,0:T(8,128)(2,1)S(1)} %slice.168), channel_id=1, source_target_pairs={{0,64},{16,80},{32,96},{48,112},{64,0},{80,16},{96,32},{112,48},{1... | collective-permute-start | bytes 393224 | tf_op jit(solution)/shard_map/ppermute | solution.py:107
  246.4 9.6 %collective-permute-start.47 = (bf16[256,512]{1,0:T(8,128)(2,1)S(1)}, bf16[256,512]{1,0:T(8,128)(2,1)S(1)}, u32[]{:S(2)}, u32[]{:S(2)}) collective-permute-start(bf16[256,512]{1,0:T(8,128)(2,1)S(1)} %get-tuple-element.95), channel_id=1, source_target_pairs={{0,16},{16,32},{32,48},{48,0},{64,80},{80,96},{96,112},{112,64},{1... | collective-permute-start | bytes 786440 | tf_op jit(solution)/shard_map/ppermute | solution.py:99
  247.5 8.5 %collective-permute-start.48 = (bf16[256,512]{1,0:T(8,128)(2,1)S(1)}, bf16[256,512]{1,0:T(8,128)(2,1)S(1)}, u32[]{:S(2)}, u32[]{:S(2)}) collective-permute-start(bf16[256,512]{1,0:T(8,128)(2,1)S(1)} %get-tuple-element.93), channel_id=1, source_target_pairs={{0,48},{16,0},{32,16},{48,32},{64,112},{80,64},{96,80},{112,96},{1... | collective-permute-start | bytes 786440 | tf_op jit(solution)/shard_map/ppermute | solution.py:99
  250.4 7.6 %collective-permute-start.45 = (bf16[256,512]{1,0:T(8,128)(2,1)S(1)}, bf16[256,512]{1,0:T(8,128)(2,1)S(1)}, u32[]{:S(2)}, u32[]{:S(2)}) collective-permute-start(bf16[256,512]{1,0:T(8,128)(2,1)S(1)} %slice.222), channel_id=1, source_target_pairs={{0,64},{16,80},{32,96},{48,112},{64,0},{80,16},{96,32},{112,48},{1... | collective-permute-start | bytes 786440 | tf_op jit(solution)/shard_map/ppermute | solution.py:107
  (32 other events, 519.7 us)
